TPU v7x, 512 devices: a whole 4x8x8 slice. The times are simulated.
512 devices in a mesh: lat: 16 (over z, core), lon: 32 (over y, x).
Axes of the slice: x: 4, y: 8, z: 8, core: 2. Of those that a mesh axis runs over, the one named last changes fastest.
Arguments:
- mlp_input: bfloat16 [512, 384, 640], P('lat', 'lon'), may hold values from -6 to 6
- out_cot: bfloat16 [512, 384, 640], P('lat', 'lon'), may hold values from -6 to 6
- w_in: bfloat16 [640, 1280], replicated, may hold values from -0.25 to 0.25
- w_out: bfloat16 [1280, 640], replicated, may hold values from -0.15625 to 0.15625
- chan_weights: float32 [9, 640], replicated, may hold values from -2 to 2
- row_weights: float32 [9, 512, 9], replicated, may hold values from -2 to 2
- basis_spectra: float32 [9, 384], replicated, may hold values from -6 to 6
- band_cols: int32 [512, 9], replicated, may hold values from 0 to 511, as said below
- band_widths: int32 [512], replicated, may hold values from 1 to 9, as said below
Outputs:
- grid_grad: bfloat16 [512, 384, 640], P('lat', 'lon')
- grad_in: float32 [640, 1280], P('lat', 'lon')
- grad_out: float32 [1280, 640], P('lon', 'lat')
Inputs may be any that keep to these rules, and one draw needn't show every extreme that they name: `band_cols`: slot 0 of each row is the row itself; every slot lies within 4 rows of its own row. `band_widths`: the 4 rows nearest each pole use all 9 slots; slots at or beyond a row's width are padding.
All inputs are finite; a program needn't handle non-finite values.
Results may differ from a plain program's by a relative error of at most 0.02.
Values may be sent and summed in bfloat16 or wider, within the bound.
No kernel may reach another device: no remote copies, remote signals or barrier semaphores. Data moves between devices by JAX's collectives and lax.ppermute only.
A program may use at most 64 MiB of HBM per device.

v0:
```python
import math

import jax
import jax.numpy as jnp
from jax import lax
from jax.sharding import PartitionSpec as P


def padded(cells, sides, width):
    for axis, dim in sides:
        count = lax.axis_size(axis)
        ends = count - 1
        head = lax.slice_in_dim(cells, 0, width, axis=dim)
        tail = lax.slice_in_dim(cells, cells.shape[dim] - width, cells.shape[dim], axis=dim)
        cells = jnp.concatenate(
            [
                lax.ppermute(tail, axis, [(i, (i + 1) % count) for i in range(ends)]),
                cells,
                lax.ppermute(head, axis, [((i + 1) % count, i) for i in range(ends)]),
            ],
            axis=dim,
        )
    return cells


def gelu_parts(pre_act):
    inner_arg = 0.7978845608 * (pre_act + 0.044715 * pre_act * pre_act * pre_act)
    tangent = jnp.tanh(inner_arg)
    gelu_value = 0.5 * pre_act * (1.0 + tangent)
    gelu_slope = 0.5 * (1.0 + tangent) + 0.5 * pre_act * (
        1.0 - tangent * tangent
    ) * 0.7978845608 * (1.0 + 0.134145 * pre_act * pre_act)
    return (gelu_value, gelu_slope)


def tables(lon_total):
    half_len = lon_total // 2
    lon_index = jnp.arange(lon_total, dtype=jnp.int32)
    frequency = jnp.arange(2 * half_len, dtype=jnp.int32) % half_len
    phases = lon_index[:, None] * frequency[None, :] % lon_total
    angles = phases.astype(jnp.float32) * jnp.float32(2.0 * math.pi / lon_total)
    is_sine = jnp.arange(2 * half_len, dtype=jnp.int32) >= half_len
    forward = jnp.where(is_sine[None, :], jnp.sin(angles), jnp.cos(angles))
    scaling = jnp.where(frequency == 0, jnp.float32(1.0), jnp.float32(2.0)) / jnp.float32(lon_total)
    inverse = forward.T * scaling[:, None]
    return (forward, inverse)


def weighted(spectra, basis_spectra, chan_w):
    half_len = spectra.shape[-1] // 2
    real_part = spectra[..., :half_len]
    imag_part = spectra[..., half_len:]
    cosine = basis_spectra[:, None, None, :half_len]
    sine = basis_spectra[:, None, None, half_len:]
    first = cosine * real_part[None] + sine * imag_part[None]
    second = cosine * imag_part[None] - sine * real_part[None]
    return jnp.concatenate([first, second], -1) * chan_w[:, None, :, None]


def contract_tokens(left, right):
    return lax.dot_general(
        left, right, (((0,), (0,)), ((), ())), preferred_element_type=jnp.float32
    )


def body(
    mlp_input,
    out_cot,
    w_in,
    w_out,
    chan_weights,
    row_weights,
    basis_spectra,
    band_cols,
    band_widths,
):
    lat_rows, lon_cols, channels = mlp_input.shape
    lon_shards = lax.axis_size("lon")
    local_chans = channels // lon_shards
    lon_total = lon_cols * lon_shards
    band_slots = row_weights.shape[2]
    band_reach = (band_slots - 1) // 2
    row_start = lax.axis_index("lat") * lat_rows
    chan_start = lax.axis_index("lon") * local_chans
    tokens = mlp_input.reshape(lat_rows * lon_cols, channels)
    cotangent = out_cot.reshape(lat_rows * lon_cols, channels)
    pre_act = jnp.dot(tokens, w_in, preferred_element_type=jnp.float32)
    gelu_value, gelu_slope = gelu_parts(pre_act)
    hidden = gelu_value.astype(jnp.bfloat16)
    back_proj = lax.dot_general(
        cotangent, w_out, (((1,), (1,)), ((), ())), preferred_element_type=jnp.float32
    )
    pre_grad = (back_proj * gelu_slope).astype(jnp.bfloat16)
    input_back = lax.dot_general(
        pre_grad, w_in, (((1,), (1,)), ((), ())), preferred_element_type=jnp.float32
    )
    grid_cot = (
        (cotangent.astype(jnp.float32) + input_back)
        .astype(jnp.bfloat16)
        .reshape(lat_rows, lon_cols, channels)
    )
    part_in = lax.optimization_barrier(
        contract_tokens(tokens, pre_grad).astype(jnp.bfloat16)
    ).astype(jnp.float32)
    part_out = lax.optimization_barrier(
        contract_tokens(hidden, cotangent).astype(jnp.bfloat16)
    ).astype(jnp.float32)
    half_in, half_out = (
        lax.psum_scatter(
            part_in.astype(jnp.bfloat16), "lon", scatter_dimension=1, tiled=True
        ).astype(jnp.float32),
        lax.psum_scatter(
            part_out.astype(jnp.bfloat16), "lon", scatter_dimension=0, tiled=True
        ).astype(jnp.float32),
    )
    grad_in, grad_out = (
        lax.psum_scatter(half_in, "lat", scatter_dimension=0, tiled=True),
        lax.psum_scatter(half_out, "lat", scatter_dimension=1, tiled=True),
    )
    chan_w = lax.dynamic_slice_in_dim(chan_weights, chan_start, local_chans, 1)
    forward, inverse = tables(lon_total)
    slot_index = jnp.arange(band_slots, dtype=jnp.int32)
    src_cols = lax.dynamic_slice_in_dim(band_cols, row_start, lat_rows, 0)
    src_widths = lax.dynamic_slice_in_dim(band_widths, row_start, lat_rows, 0)
    src_coeffs = lax.dynamic_slice_in_dim(row_weights, row_start, lat_rows, 1)
    target = src_cols - (row_start - band_reach)
    target_count = lat_rows + 2 * band_reach
    moved = lax.all_to_all(
        grid_cot.reshape(lat_rows, lon_cols, lon_shards, local_chans),
        "lon",
        split_axis=2,
        concat_axis=1,
        tiled=True,
    )
    spectra = jnp.einsum(
        "rlc,lg->rcg",
        moved[:, :, 0, :].astype(jnp.float32),
        forward,
        precision=lax.Precision.HIGHEST,
    )
    mixed = weighted(spectra, basis_spectra, chan_w)
    live_slot = slot_index[None, :] < src_widths[:, None]
    onehot = (
        (target[:, :, None] == jnp.arange(target_count, dtype=jnp.int32)[None, None, :])
        & live_slot[:, :, None]
    ).astype(jnp.float32)
    band_mat = jnp.einsum("koj,ojt->kto", src_coeffs, onehot, precision=lax.Precision.HIGHEST)
    summed = jnp.einsum("kto,kocg->tcg", band_mat, mixed, precision=lax.Precision.HIGHEST)
    rim_rows = jnp.concatenate([summed[:band_reach], summed[lat_rows + band_reach :]], 0)
    received = padded(rim_rows, (("lat", 0),), band_reach)
    own_rows = summed[band_reach : band_reach + lat_rows]
    own_rows = own_rows.at[:band_reach].add(received[:band_reach])
    own_rows = own_rows.at[lat_rows - band_reach :].add(received[3 * band_reach :])
    backed = jnp.einsum("tcg,gl->tlc", own_rows, inverse, precision=lax.Precision.HIGHEST).astype(
        jnp.bfloat16
    )
    returned = lax.all_to_all(
        backed.reshape(lat_rows, lon_total, 1, local_chans),
        "lon",
        split_axis=1,
        concat_axis=2,
        tiled=True,
    )
    returned = returned.reshape(lat_rows, lon_cols, channels)
    grid_grad = (out_cot.astype(jnp.float32) + returned.astype(jnp.float32)).astype(jnp.bfloat16)
    return (grid_grad, grad_in, grad_out)


def solution(mesh):
    return jax.shard_map(
        body,
        mesh=mesh,
        in_specs=(P("lat", "lon", None), P("lat", "lon", None), P(), P(), P(), P(), P(), P(), P()),
        out_specs=(P("lat", "lon", None), P("lat", "lon"), P("lon", "lat")),
        check_vma=False,
    )
```

profile of v0, /device:TPU:16, one launch (start us, length us, event | category | flops | bytes accessed | tf_op | source)
XLA Modules:
  0.0 492.9 jit_solution(15375943509068664420)
XLA Ops:
  7.2 1.3 copy.30
  8.6 0.9 reshape.135
  9.5 0.2 copy.29
  9.7 0.9 reshape.134
  10.5 2.0 fusion.79
  12.6 1.3 copy-done.5
  13.9 2.5 convolution_convert_fusion
  16.4 3.6 fusion.5
  20.0 0.9 copy-done.6
  21.0 1.0 fusion.14
  21.9 8.5 %reshape_reshape.3 = bf16[32,12,32,20]{3,2,1,0:T(8,128)(2,1)} reshape(bf16[384,640]{1,0:T(8,128)(2,1)S(1)} %fusion.14) | data formatting | bytes 983040 | tf_op jit(solution)/shard_map/reshape;reshape | solution.py:129
  30.5 6.3 %copy.31 = bf16[32,12,32,20]{0,3,1,2:T(8,128)(2,1)} copy(bf16[32,12,32,20]{3,2,1,0:T(8,128)(2,1)} %reshape_reshape.3) | data formatting | bytes 983040 | tf_op jit(solution)/shard_map/reshape;reshape | solution.py:129
  36.8 4.5 reshape.151
  41.3 10.1 %all-to-all-start = ((bf16[32,2,3840]{2,1,0:T(2,128)(2,1)}), bf16[32,2,3840]{2,1,0:T(2,128)(2,1)S(1)}, u32[]{:S(2)}, u32[]{:S(2)}) async-start(bf16[32,2,3840]{2,1,0:T(2,128)(2,1)} %reshape.151), calls=%async_computation | async-start | bytes 983040 | tf_op jit(solution)/shard_map/all_to_all | solution.py:128
  51.3 0.3 reduce-scatter.9.cloned.1.call-start
  51.7 3.6 fusion.4
  55.3 0.8 constant_dynamic-slice_fusion
  56.1 1.0 constant_dynamic-slice_fusion.1
  57.1 0.8 dynamic-slice_subtract_fusion
  57.8 0.8 dynamic_slice.13
  58.6 0.1 copy.33
  58.8 0.2 copy.43
  59.1 0.4 convolution_bitcast_fusion
  59.6 8.6 %all-to-all-done = bf16[32,2,3840]{2,1,0:T(2,128)(2,1)S(1)} async-done(((bf16[32,2,3840]{2,1,0:T(2,128)(2,1)}), bf16[32,2,3840]{2,1,0:T(2,128)(2,1)S(1)}, u32[]{:S(2)}, u32[]{:S(2)}) %all-to-all-start) | async-done | bytes 491552 | tf_op jit(solution)/shard_map/all_to_all | solution.py:128
  68.2 2.9 reshape.152
  71.1 5.7 %fusion.11 = f32[32,20,384]{2,0,1:T(8,128)S(1)} fusion(bf16[32,384,20]{0,2,1:T(8,128)(2,1)} %bitcast.57, s32[384]{0:T(512)S(1)} %add_select_fusion.2, pred[384]{0:T(512)(128)(4,1)S(1)} %iota_compare_fusion.2), kind=kOutput, calls=%fused_computation.19 | convolution fusion | flops 1133936640 | bytes 1476480 | tf_op jit(solution)/shard_map/rlc,lg->rcg/dot_general | solution.py:135
  76.8 0.2 fusion.77
  77.1 2.0 multiply_add_fusion
  79.1 6.7 %fusion.13 = f32[40,20,384]{2,0,1:T(8,128)S(1)} fusion(f32[9,32,20,192]{3,1,0,2:T(8,128)S(1)} %get-tuple-element.39, f32[9,32,20,192]{3,1,0,2:T(8,128)S(1)} %get-tuple-element.38, f32[9,20]{0,1:T(8,128)S(1)} %copy.33, f32[9,40,32]{1,0,2:T(8,128)S(1)} %convolution_bitcast_fusion), kind=kOutput, calls=%fused_computation.22 | convolution fusion | flops 1066106880 | bytes 10122960 | tf_op jit(solution)/shard_map/kto,kocg->tcg/dot_general | solution.py:148
  85.8 1.3 collective-permute-start
  87.2 0.1 slice.81
  87.3 10.2 %collective-permute-start.1 = (f32[4,20,384]{2,0,1:T(4,128)S(1)}, f32[4,20,384]{2,0,1:T(4,128)S(1)}, u32[]{:S(2)}, u32[]{:S(2)}) collective-permute-start(f32[4,20,384]{2,0,1:T(4,128)S(1)} %get-tuple-element.40), channel_id=1, source_target_pairs={{32,0},{64,32},{96,64},{128,96},{160,128},{192,160},{224,192},{256... | collective-permute-start | bytes 368648 | tf_op jit(solution)/shard_map/ppermute | solution.py:19
  97.7 4.5 fusion.15
  102.1 2.6 copy.35
  104.7 4.4 reshape.153
  109.1 5.4 %all-to-all-start.1 = ((bf16[32,2,3840]{2,1,0:T(2,128)(2,1)}), bf16[32,2,3840]{2,1,0:T(2,128)(2,1)S(1)}, u32[]{:S(2)}, u32[]{:S(2)}) async-start(bf16[32,2,3840]{2,1,0:T(2,128)(2,1)} %reshape.153), calls=%async_computation.1 | async-start | bytes 983040 | tf_op jit(solution)/shard_map/all_to_all | solution.py:157
  114.5 1.3 dynamic-slice.18
  116.4 13.0 %all-to-all-done.1 = bf16[32,2,3840]{2,1,0:T(2,128)(2,1)S(1)} async-done(((bf16[32,2,3840]{2,1,0:T(2,128)(2,1)}), bf16[32,2,3840]{2,1,0:T(2,128)(2,1)S(1)}, u32[]{:S(2)}, u32[]{:S(2)}) %all-to-all-start.1) | async-done | bytes 491552 | tf_op jit(solution)/shard_map/all_to_all | solution.py:157
  129.4 2.9 reshape.154
  132.3 6.6 %reshape.138 = f32[32,32,12,1,20]{0,3,4,2,1:T(1,128)} reshape(bf16[32,384,1,20]{0,3,2,1:T(8,128)(2,1)} %bitcast.54) | data formatting | bytes 1474560 | tf_op jit(solution)/shard_map/convert_element_type | solution.py:165
  138.9 11.2 %copy.36 = f32[32,12,32,1,20]{4,2,0,1,3:T(8,128)} copy(f32[32,12,32,1,20]{0,3,4,1,2:T(1,128)} %bitcast.53) | data formatting | bytes 1966080 | tf_op jit(solution)/shard_map/convert_element_type | solution.py:165
  150.1 6.1 %reshape.137 = f32[32,12,640]{2,0,1:T(8,128)S(1)} reshape(f32[32,12,32,1,20]{4,2,0,1,3:T(8,128)} %copy.36) | data formatting | bytes 1966080 | tf_op jit(solution)/shard_map/convert_element_type | solution.py:165
  156.2 0.9 add_convert_fusion
  157.1 71.8 %reduce-scatter.11.cloned.1.call-done = bf16[40,640]{1,0:T(8,128)(2,1)} async-done(((bf16[1280,640]{1,0:T(8,128)(2,1)}), bf16[40,640]{1,0:T(8,128)(2,1)}) %reduce-scatter.11.cloned.1.call-update) | async-done | bytes 51216
  228.9 205.9 %reduce-scatter.9.cloned.1.call-done = bf16[640,40]{0,1:T(8,128)(2,1)} async-done(((bf16[640,1280]{0,1:T(8,128)(2,1)}), bf16[640,40]{0,1:T(8,128)(2,1)}) %reduce-scatter.9.cloned.1.call-update) | async-done | bytes 51216
  434.8 49.6 %all-reduce.6 = (f32[640,40]{0,1:T(8,128)S(1)}, f32[40,640]{1,0:T(8,128)S(1)}) all-reduce(bf16[640,40]{0,1:T(8,128)(2,1)} %reduce-scatter.9.cloned.1.call-done, bf16[40,640]{1,0:T(8,128)(2,1)} %reduce-scatter.11.cloned.1.call-done), channel_id=3, replica_groups=mesh['lat'=16,'lon'=32] {'lat'}, use_global_device_ids=true, to_apply=%region_1.0.clone | all-reduce | flops 51200 | bytes 307200
  484.5 0.7 constant_dynamic-slice_fusion.3
  485.2 0.7 copy.37
  (27 shorter events, 0.6 us)
Async XLA Ops:
  7.2 3.4 copy-start
  7.2 2.3 copy-start.1
  7.2 221.7 %reduce-scatter.11.cloned.1.call-start = ((), (), s32[]{:S(2)}) async-start(), calls=%async_computation.5 | async-start | bytes 1689600
  10.5 3.3 copy-start.3
  12.6 1.3 copy-start.5
  20.0 1.0 copy-start.6
  36.8 14.8 %copy-start.2 = (bf16[384,640]{1,0:T(8,128)(2,1)S(1)}, bf16[384,640]{1,0:T(8,128)(2,1)}, u32[]{:S(2)}) copy-start(bf16[384,640]{1,0:T(8,128)(2,1)} %reshape.135) | copy-start | bytes 1474564
  41.3 26.9 %all-to-all-start = ((bf16[32,2,3840]{2,1,0:T(2,128)(2,1)}), bf16[32,2,3840]{2,1,0:T(2,128)(2,1)S(1)}, u32[]{:S(2)}, u32[]{:S(2)}) async-start(bf16[32,2,3840]{2,1,0:T(2,128)(2,1)} %reshape.151), calls=%async_computation | async-start | bytes 983040 | tf_op jit(solution)/shard_map/all_to_all | solution.py:128
  51.3 7.7 %copy-start.4 = (f32[9,384]{1,0:T(8,128)S(1)}, f32[9,384]{1,0:T(8,128)}, u32[]{:S(2)}) copy-start(f32[9,384]{1,0:T(8,128)} %param.19) | copy-start | bytes 41476
  51.3 383.4 %reduce-scatter.9.cloned.1.call-start = ((), (), s32[]{:S(2)}) async-start(), calls=%async_computation.4 | async-start | bytes 1689600
  85.8 11.7 %collective-permute-start = (f32[4,20,384]{2,0,1:T(4,128)S(1)}, f32[4,20,384]{2,0,1:T(4,128)S(1)}, u32[]{:S(2)}, u32[]{:S(2)}) collective-permute-start(f32[4,20,384]{2,0,1:T(4,128)S(1)} %get-tuple-element.41), channel_id=1, source_target_pairs={{0,32},{32,64},{64,96},{96,128},{128,160},{160,192},{192,224},{224... | collective-permute-start | bytes 368648 | tf_op jit(solution)/shard_map/ppermute | solution.py:17
  87.3 10.3 %collective-permute-start.1 = (f32[4,20,384]{2,0,1:T(4,128)S(1)}, f32[4,20,384]{2,0,1:T(4,128)S(1)}, u32[]{:S(2)}, u32[]{:S(2)}) collective-permute-start(f32[4,20,384]{2,0,1:T(4,128)S(1)} %get-tuple-element.40), channel_id=1, source_target_pairs={{32,0},{64,32},{96,64},{128,96},{160,128},{192,160},{224,192},{256... | collective-permute-start | bytes 368648 | tf_op jit(solution)/shard_map/ppermute | solution.py:19
  109.1 20.3 %all-to-all-start.1 = ((bf16[32,2,3840]{2,1,0:T(2,128)(2,1)}), bf16[32,2,3840]{2,1,0:T(2,128)(2,1)S(1)}, u32[]{:S(2)}, u32[]{:S(2)}) async-start(bf16[32,2,3840]{2,1,0:T(2,128)(2,1)} %reshape.153), calls=%async_computation.1 | async-start | bytes 983040 | tf_op jit(solution)/shard_map/all_to_all | solution.py:157
Sparse Core Ops, SparseCore 0:
  16.5 212.3 reduce-scatter.10
  233.3 201.4 reduce-scatter.8
where the time goes:
time: 501 us; the launch traced here: 493 us
  waiting for transfers between devices  299 us (60%)
  local copies, waits for them, and re-layouts  67.7 us (14%)
  blocking collectives  49.6 us (10%)
  matrix products  30 us (6%)
  starting transfers between devices  27.3 us (5%)
  between operations  15.1 us (3%)
    unnamed x4, waiting for transfers between devices  278 us
    unnamed x1, blocking collectives  49.6 us
    convert_element_type x3, local copies, waits for them, and re-layouts, body(): returned.astype(jnp.float32)  23.9 us
    unnamed x25, local copies, waits for them, and re-layouts  21.4 us
    another operation x2, local copies, waits for them, and re-layouts, body(): grid_cot.reshape(lat_rows, lon_cols, lon_shards, local_chans)  14.9 us
    all_to_all x1, waiting for transfers between devices, body(): lax.all_to_all(backed.reshape(lat_rows, lon_total, 1, local_chans), 'lon'...  13 us
    ppermute x1, starting transfers between devices, padded(): lax.ppermute(head, axis, [((i + 1) % count, i) for i in range(ends)])  10.2 us
    all_to_all x1, starting transfers between devices, body(): lax.all_to_all(grid_cot.reshape(lat_rows, lon_cols, lon_shards, local_cha...  10.1 us
  transfers between devices with their start and end apart: 6, of which 4 were waited for; matrix products, arithmetic and copies ran while one was open for 18% of the time, Pallas kernels for 0%

commit v1 on v0

v1 whole, which is shorter than its diff:
```python
import functools
import math

import jax
import jax.numpy as jnp
import numpy as np
from jax import lax
from jax.experimental import pallas as pl
from jax.experimental.pallas import tpu as pltpu
from jax.sharding import Mesh, PartitionSpec as P

f32 = jnp.float32
bf16 = jnp.bfloat16
LAT = ("z", "core")
LON = ("y", "x")
ROWS = 32
LONS = 12
PEERS = 32
LOCAL = 20
NLON = 384
NF = 192
NB = 9
REACH = 4
GROUPS = 5
SLAB = LONS * GROUPS
PAD = 64
TALL = PEERS * SLAB + 8


def nt(a, b, precision=None):
    return lax.dot_general(a, b, (((1,), (1,)), ((), ())), preferred_element_type=f32, precision=precision)


def tn(a, b):
    return lax.dot_general(a, b, (((0,), (0,)), ((), ())), preferred_element_type=f32)


def nn(a, b, precision=None):
    return lax.dot_general(a, b, (((1,), (0,)), ((), ())), preferred_element_type=f32, precision=precision)


def swap_quarters(tiles):
    quarter = lax.broadcasted_iota(jnp.int32, tiles[0].shape, 1) // 32
    out = []
    for b in range(4):
        made = None
        for q in range(4):
            shift = (32 * (q - b)) % 128
            moved = pltpu.roll(tiles[q], shift, 1) if shift else tiles[q]
            made = moved if made is None else jnp.where(quarter == q, moved, made)
        out.append(made)
    return out


def gelu_parts(v):
    square = v * v
    tangent = jnp.tanh(0.7978845608 * (v + 0.044715 * v * square))
    half = 0.5 * (1.0 + tangent)
    slope = half + 0.5 * v * (1.0 - tangent * tangent) * 0.7978845608 * (1.0 + 0.134145 * square)
    return v * half, slope


def to_slabs(tall, out):
    for d in range(PEERS):
        out[d] = tall[SLAB * d : SLAB * d + PAD, :].astype(bf16)


def from_slabs(slabs, tall):
    for d in range(PEERS):
        tall[SLAB * d : SLAB * d + PAD, :] = slabs[d].astype(f32)


def mlp_kernel(tok, cot, w_in, w_out, send, hidden, pre_grad, acc, tall):
    step = pl.program_id(0)
    last = pl.num_programs(0) - 1
    gelu_value, slope = gelu_parts(nn(tok[...], w_in[...]))
    hidden[...] = gelu_value.astype(bf16)
    grad = (nt(cot[...], w_out[...]) * slope).astype(bf16)
    pre_grad[...] = grad

    @pl.when(step == 0)
    def _():
        acc[...] = cot[...].astype(f32).T

    acc[...] += nt(w_in[...], grad)

    @pl.when(step == last)
    def _():
        tall[TALL - 8 :, :] = jnp.zeros((8, 128), f32)
        for j in range(GROUPS):
            for a in range(LONS // 4):
                tiles = [acc[(4 * j + q) * 32 : (4 * j + q + 1) * 32, a * 128 : (a + 1) * 128] for q in range(4)]
                for b, tile in enumerate(swap_quarters(tiles)):
                    tall[pl.ds((4 * a + b) * GROUPS + j, PEERS, stride=SLAB), :] = tile
        to_slabs(tall, send)


def grads_kernel(core, tok, cot, hidden, pre_grad, mine, theirs, tok_t, cot_t, scr):
    @pl.when(pl.program_id(0) == 0)
    def _():
        tok_t[...] = tok[...].astype(f32).T.astype(bf16)
        cot_t[...] = cot[...].astype(f32).T.astype(bf16)

    c = core[0]
    depth, _, size = mine.shape[0], mine.shape[1], mine.shape[2]
    for which, (left, right) in enumerate(((tok_t, pre_grad), (cot_t, hidden))):
        scr[...] = nn(left[...], right[...])
        for z in range(depth):
            own = pl.multiple_of((2 * z + c) * size, 8)
            other = pl.multiple_of((2 * z + 1 - c) * size, 8)
            mine[z, which] = scr[pl.ds(own, size), :].astype(bf16)
            theirs[z, which] = scr[pl.ds(other, size), :].astype(bf16)


def prep_kernel(place, row_w, cols, widths, chan, basis, own_mix, rim_mix, spread, coefs):
    row_start, lon = place[0], place[1]
    high = lax.Precision.HIGHEST
    count = cols.shape[1]
    at = lax.broadcasted_iota(jnp.int32, (64, count), 0)
    rim = at % 4
    source = jnp.where(at < 32, at, jnp.where(at < 48, rim - REACH, rim + ROWS)) + row_start
    pick = (source == lax.broadcasted_iota(jnp.int32, (64, count), 1)).astype(f32)
    col = nt(pick, cols[...].astype(f32), high) - row_start.astype(f32)
    width = nt(pick, widths[...].astype(f32), high)
    lane = lax.broadcasted_iota(jnp.int32, (64, 128), 1)
    target = (lane % 32).astype(f32)
    hits = [
        jnp.where((col[:, s : s + 1] == target) & (width > s), 1.0, 0.0) for s in range(NB)
    ]
    chan_row = lax.broadcasted_iota(jnp.int32, (640, 640), 0)
    chan_lane = lax.broadcasted_iota(jnp.int32, (640, 640), 1)
    chan_pick = (chan_row == (chan_lane // 32) * 32 + lon).astype(f32)
    chan_w = nn(chan[...], chan_pick, high)
    rim_mix[...] = jnp.zeros(rim_mix.shape, bf16)
    quarter = lane[:32] // 32
    rim_at = lax.broadcasted_iota(jnp.int32, (16, 128), 0) // 4
    rim_quarter = lane[:16] // 32
    for k in range(NB):
        coef = nt(pick, row_w[k], high)
        weight = None
        for s in range(NB):
            term = coef[:, s : s + 1] * hits[s]
            weight = term if weight is None else weight + term
        for j in range(GROUPS):
            scaled = weight * chan_w[k : k + 1, 128 * j : 128 * (j + 1)]
            for q in range(4):
                own_mix[j, k * 128 + q * 32 : k * 128 + (q + 1) * 32, :] = jnp.where(
                    quarter == q, scaled[:32], 0.0
                ).astype(bf16)
            for side in range(2):
                part = scaled[32 + 16 * side : 48 + 16 * side]
                start = (k * 2 + side) * 128 + 16 * j
                rim_mix[start : start + 16, 128 * j : 128 * (j + 1)] = jnp.where(
                    rim_quarter == rim_at, part, 0.0
                ).astype(bf16)
        spread[k] = jnp.broadcast_to(basis[k : k + 1, :], (128, NLON)).T


def open_kernel(slabs, pick, moved, rims, tall):
    from_slabs(slabs, tall)
    for j in range(GROUPS):
        moved[:, 128 * j : 128 * (j + 1)] = tall[pl.ds(j, NLON, stride=GROUPS), :].astype(bf16)
    edges = nn(moved[...], pick[...]).astype(bf16)
    rims[0] = edges[:, :128]
    rims[1] = edges[:, 128:]


def own_kernel(moved, forward, spread, own_mix, filtered, mixed):
    spectra = nn(forward[...], moved[...])
    first, second = spectra[:NF], spectra[NF:]
    for k in range(NB):
        cosine, sine = spread[k, :NF], spread[k, NF:]
        mixed[:NF, k * 128 : (k + 1) * 128] = (cosine * first + sine * second).astype(bf16)
        mixed[NF:, k * 128 : (k + 1) * 128] = (cosine * second - sine * first).astype(bf16)
    filtered[...] = nn(mixed[...], own_mix[0])


def close_kernel(filtered, before, after, forward, inverse, spread, rim_mix, send, mixed, tall):
    for side, rim in enumerate((before, after)):
        spectra = nn(forward[...], rim[...])
        first, second = spectra[:NF], spectra[NF:]
        for k in range(NB):
            cosine, sine = spread[k, :NF], spread[k, NF:]
            at = (k * 2 + side) * 128
            mixed[:NF, at : at + 128] = (cosine * first + sine * second).astype(bf16)
            mixed[NF:, at : at + 128] = (cosine * second - sine * first).astype(bf16)
    whole = (filtered[...] + nn(mixed[...], rim_mix[...])).astype(bf16)
    tall[TALL - 8 :, :] = jnp.zeros((8, 128), f32)
    for j in range(GROUPS):
        tall[pl.ds(j, NLON, stride=GROUPS), :] = nn(inverse[...], whole[:, 128 * j : 128 * (j + 1)])
    to_slabs(tall, send)


def final_kernel(slabs, cot, out, tall):
    from_slabs(slabs, tall)
    for j in range(GROUPS):
        for a in range(LONS // 4):
            tiles = [tall[pl.ds((4 * a + b) * GROUPS + j, PEERS, stride=SLAB), :] for b in range(4)]
            turned = jnp.concatenate(tiles, 0).T
            for b, tile in enumerate(swap_quarters([turned[32 * q : 32 * (q + 1)] for q in range(4)])):
                rows = slice((4 * a + b) * 32, (4 * a + b + 1) * 32)
                lanes = slice(128 * j, 128 * (j + 1))
                out[rows, lanes] = (cot[rows, lanes].astype(f32) + tile).astype(bf16)


def turn_kernel(block, out):
    rows = block[0].astype(f32), block[1].astype(f32)
    size = rows[0].shape[0]
    fill = jnp.zeros((-(2 * size) % 128, rows[0].shape[1]), f32)
    out[...] = jnp.concatenate([rows[0], rows[1], fill], 0).T.astype(bf16)


def sum_kernel(parts, grad_in, grad_out):
    total = parts[0].astype(f32)
    for d in range(1, parts.shape[0]):
        total = total + parts[d].astype(f32)
    size = grad_in.shape[0]
    lanes = total.shape[1]
    filled = jnp.concatenate([total, jnp.zeros((-total.shape[0] % 128, lanes), f32)], 0)
    grad_in[...] = filled.T[:size, : grad_in.shape[1]]
    grad_out[...] = total[:, size : 2 * size]


def tables():
    lon = np.arange(NLON)
    freq = np.arange(NLON) % NF
    phase = (lon[:, None] * freq[None, :] % NLON) * (2.0 * math.pi / NLON)
    forward = np.where(np.arange(NLON)[None, :] >= NF, np.sin(phase), np.cos(phase))
    inverse = forward.T * (np.where(freq == 0, 1.0, 2.0) / NLON)[:, None]
    return jnp.asarray(forward.T, bf16), jnp.asarray(inverse.T, bf16)


def rim_picks():
    pick = np.zeros((640, 256), np.float32)
    for c in range(LOCAL):
        for r in range(REACH):
            pick[c * 32 + ROWS - REACH + r, c * 4 + r] = 1.0
            pick[c * 32 + r, 128 + c * 4 + r] = 1.0
    return jnp.asarray(pick, bf16)


def shape(*dims, dtype=bf16):
    return jax.ShapeDtypeStruct(dims, dtype)


VMEM = pl.BlockSpec(memory_space=pltpu.VMEM)
SMEM = pl.BlockSpec(memory_space=pltpu.SMEM)


def call(kernel, out, ins, flops, moved, scratch=(), **grid):
    options = dict(grid)
    if "grid" not in options:
        options["in_specs"] = ins
        options["out_specs"] = jax.tree.map(lambda _: VMEM, out)
    return pl.pallas_call(
        kernel,
        out_shape=out,
        scratch_shapes=list(scratch),
        compiler_params=pltpu.CompilerParams(vmem_limit_bytes=40 << 20),
        cost_estimate=pl.CostEstimate(flops=int(flops), bytes_accessed=int(moved), transcendentals=0),
        **options,
    )


def body(mlp_input, out_cot, w_in, w_out, chan_weights, row_weights, basis_spectra, band_cols, band_widths):
    tokens_n = ROWS * LONS
    depth = lax.axis_size("z")
    n_lat = depth * lax.axis_size("core")
    part = 640 // n_lat
    lat, lon, core = lax.axis_index(LAT), lax.axis_index(LON), lax.axis_index("core")
    tokens = mlp_input.transpose(1, 0, 2).reshape(tokens_n, 640)
    cotangent = out_cot.transpose(1, 0, 2).reshape(tokens_n, 640)
    whole = lambda *dims: pl.BlockSpec(dims, lambda i: (0,) * len(dims))

    send, hidden, pre_grad = call(
        mlp_kernel,
        (shape(PEERS, PAD, 128), shape(tokens_n, 1280), shape(tokens_n, 1280)),
        None,
        2e9,
        6e6,
        [pltpu.VMEM((640, tokens_n), f32), pltpu.VMEM((TALL, 128), f32)],
        grid=(5,),
        in_specs=[
            whole(tokens_n, 640),
            whole(tokens_n, 640),
            pl.BlockSpec((640, 256), lambda i: (0, i)),
            pl.BlockSpec((256, 640), lambda i: (i, 0)),
        ],
        out_specs=[
            whole(PEERS, PAD, 128),
            pl.BlockSpec((tokens_n, 256), lambda i: (0, i)),
            pl.BlockSpec((tokens_n, 256), lambda i: (0, i)),
        ],
    )(tokens, cotangent, w_in, w_out)

    received = lax.all_to_all(send, LON, split_axis=0, concat_axis=0, tiled=True)

    half = shape(depth, 2, part, 1280)
    half_spec = pl.BlockSpec((depth, 2, part, 256), lambda i: (0, 0, 0, i))
    wide = pl.BlockSpec((tokens_n, 256), lambda i: (0, i))
    mine, theirs = call(
        grads_kernel,
        (half, half),
        None,
        1.3e9,
        8e6,
        [pltpu.VMEM((640, tokens_n), bf16), pltpu.VMEM((640, tokens_n), bf16), pltpu.VMEM((640, 256), f32)],
        grid=(5,),
        in_specs=[SMEM, whole(tokens_n, 640), whole(tokens_n, 640), wide, wide],
        out_specs=[half_spec, half_spec],
    )(core.reshape(1), tokens, cotangent, hidden, pre_grad)
    partner = lax.ppermute(theirs, "core", [(0, 1), (1, 0)])
    chip = (mine.astype(f32) + partner.astype(f32)).astype(bf16)
    column = lax.psum_scatter(chip, "z", scatter_dimension=0, tiled=True)

    own_mix, rim_mix, spread = call(
        prep_kernel,
        (shape(GROUPS, NB * 128, 128), shape(NB * 256, 640), shape(NB, NLON, 128, dtype=f32)),
        [SMEM] + [VMEM] * 5,
        1e9,
        6e6,
        [pltpu.VMEM((8, 128), f32)],
    )(
        jnp.stack([lat * ROWS, lon]).astype(jnp.int32),
        row_weights.transpose(0, 2, 1),
        band_cols.T,
        band_widths.reshape(1, -1),
        chan_weights,
        basis_spectra,
    )

    forward, inverse = tables()
    moved, rims = call(
        open_kernel,
        (shape(NLON, 640), shape(2, NLON, 128)),
        [VMEM] * 2,
        1e8,
        2e6,
        [pltpu.VMEM((TALL, 128), f32)],
    )(received, rim_picks())
    up = [(i, i + 1) for i in range(n_lat - 1)]
    before = lax.ppermute(rims[0], LAT, up)
    after = lax.ppermute(rims[1], LAT, [(b, a) for a, b in up])

    filtered = call(
        own_kernel,
        shape(NLON, 640, dtype=f32),
        None,
        8e8,
        5e6,
        [pltpu.VMEM((NLON, NB * 128), bf16)],
        grid=(GROUPS,),
        in_specs=[
            pl.BlockSpec((NLON, 128), lambda j: (0, j)),
            whole(NLON, NLON),
            whole(NB, NLON, 128),
            pl.BlockSpec((1, NB * 128, 128), lambda j: (j, 0, 0)),
        ],
        out_specs=pl.BlockSpec((NLON, 128), lambda j: (0, j)),
    )(moved, forward, spread, own_mix)

    answer = call(
        close_kernel,
        shape(PEERS, PAD, 128),
        [VMEM] * 7,
        1.5e9,
        7e6,
        [pltpu.VMEM((NLON, NB * 256), bf16), pltpu.VMEM((TALL, 128), f32)],
    )(filtered, before, after, forward, inverse, spread, rim_mix)
    returned = lax.all_to_all(answer, LON, split_axis=0, concat_axis=0, tiled=True)
    grid_grad = call(
        final_kernel, shape(tokens_n, 640), [VMEM] * 2, 1e8, 2e6, [pltpu.VMEM((TALL, 128), f32)]
    )(returned, cotangent)
    grid_grad = grid_grad.reshape(LONS, ROWS, 640).transpose(1, 0, 2)

    lanes = -(-2 * part // 128) * 128
    turned = call(turn_kernel, shape(1280, lanes), [VMEM], 1e6, 1e6)(column.reshape(2, part, 1280))
    pieces = lax.all_to_all(
        turned.reshape(PEERS, 1280 // PEERS, lanes), LON, split_axis=0, concat_axis=0, tiled=True
    )
    grad_in, grad_out = call(
        sum_kernel,
        (shape(part, 1280 // PEERS, dtype=f32), shape(1280 // PEERS, part, dtype=f32)),
        [VMEM],
        1e6,
        1e6,
    )(pieces)
    return grid_grad, grad_in, grad_out


def solution(mesh):
    chips = Mesh(mesh.devices.reshape(-1, 2, 8, 4), ("z", "core", "y", "x"))
    grid = P(LAT, LON, None)
    return jax.shard_map(
        body,
        mesh=chips,
        in_specs=(grid, grid, P(), P(), P(), P(), P(), P(), P()),
        out_specs=(grid, P(LAT, LON), P(LON, LAT)),
        check_vma=False,
    )
```

time: 501 us -> 125 us (0.25)
  the two profiles are of different devices: /device:TPU:16 before, /device:TPU:64 now
where the time goes in v1:
time: 125 us; the launch traced here: 124 us
  waiting for transfers between devices  50.9 us (41%)
  starting transfers between devices  26.3 us (21%)
  Pallas kernels  25 us (20%)
  between operations  14.3 us (11%)
  local copies, waits for them, and re-layouts  5.9 us (5%)
  other arithmetic  1.69 us (1%)
    all_to_all x1, waiting for transfers between devices, body(): lax.all_to_all(send, LON, split_axis=0, concat_axis=0, tiled=True)  18 us
    all_to_all x1, waiting for transfers between devices, body(): lax.all_to_all(answer, LON, split_axis=0, concat_axis=0, tiled=True)  16.1 us
    all_to_all x1, waiting for transfers between devices, body(): lax.all_to_all(turned.reshape(PEERS, 1280 // PEERS, lanes), LON, split_ax...  13.3 us
    all_to_all x1, starting transfers between devices, body(): lax.all_to_all(send, LON, split_axis=0, concat_axis=0, tiled=True)  10.1 us
    pallas_call x1, Pallas kernels, body(): call(mlp_kernel, (shape(PEERS, PAD, 128), shape(tokens_n, 1280), shape(to...  7.16 us
    unnamed x28, local copies, waits for them, and re-layouts  5.88 us
    all_to_all x1, starting transfers between devices, body(): lax.all_to_all(turned.reshape(PEERS, 1280 // PEERS, lanes), LON, split_ax...  5.25 us
    all_to_all x1, starting transfers between devices, body(): lax.all_to_all(answer, LON, split_axis=0, concat_axis=0, tiled=True)  4.72 us
  transfers between devices with their start and end apart: 7, of which 4 were waited for; matrix products, arithmetic and copies ran while one was open for 0% of the time, Pallas kernels for 11%

profile of v1, /device:TPU:64, one launch (start us, length us, event | category | flops | bytes accessed | tf_op | source)
XLA Modules:
  0.0 124.2 jit_solution(1910318188071579770)
XLA Ops:
  7.2 0.0 reduce-scatter.2.cloned.1.call-start
  7.2 0.0 copy-start.1
  7.2 1.0 copy-done.1
  8.2 0.0 copy-start.6
  8.3 1.4 %copy-done.6 = bf16[640,1280]{1,0:T(8,128)(2,1)S(1)} copy-done((bf16[640,1280]{1,0:T(8,128)(2,1)S(1)}, bf16[640,1280]{1,0:T(8,128)(2,1)}, u32[]{:S(2)}) %copy-start.6) | copy-done | bytes 1638424
  9.7 1.4 %copy-done.7 = bf16[1280,640]{1,0:T(8,128)(2,1)S(1)} copy-done((bf16[1280,640]{1,0:T(8,128)(2,1)S(1)}, bf16[1280,640]{1,0:T(8,128)(2,1)}, u32[]{:S(2)}) %copy-start.7) | copy-done | bytes 1638424
  11.1 0.0 copy-start.8
  11.1 1.0 copy-done.8
  12.1 7.2 %shard_map.139 = (bf16[32,64,128]{2,1,0:T(8,128)(2,1)}, bf16[384,1280]{1,0:T(8,128)(2,1)S(1)}, bf16[384,1280]{1,0:T(8,128)(2,1)S(1)}) custom-call(bf16[384,640]{1,0:T(8,128)(2,1)S(1)} %bitcast.25, bf16[384,640]{1,0:T(8,128)(2,1)S(1)} %bitcast.21, bf16[640,1280]{1,0:T(8,128)(2,1)S(1)} %copy-done.6, bf16[1280,640]{1,0:T(8,128)(2,1)S(1)} %copy-done.7), custom_call_target="tpu_custom_call" | custom-call | flops 2000000000 | bytes 6000000 | tf_op jit(solution)/shard_map/pallas_call | solution.py:275
  19.3 3.9 %shard_map.145 = (bf16[8,2,40,1280]{3,2,1,0:T(8,128)(2,1)S(1)}, bf16[8,2,40,1280]{3,2,1,0:T(8,128)(2,1)S(1)}) custom-call(s32[1]{0:T(128)} %bitcast.13.core, bf16[384,640]{1,0:T(8,128)(2,1)S(1)} %bitcast.26, bf16[384,640]{1,0:T(8,128)(2,1)S(1)} %bitcast.22, bf16[384,1280]{1,0:T(8,128)(2,1)S(1)} %get-tuple-element.21.hidden, ...), custom_call_target="tpu_custom_call" | custom-call | flops 1300000000 | bytes 8000000 | tf_op jit(solution)/shard_map/pallas_call | solution.py:301
  23.2 1.9 %collective-permute-start.2 = (bf16[8,2,40,1280]{3,2,1,0:T(8,128)(2,1)S(1)}, bf16[8,2,40,1280]{3,2,1,0:T(8,128)(2,1)S(1)}, u32[]{:S(2)}, u32[]{:S(2)}) collective-permute-start(bf16[8,2,40,1280]{3,2,1,0:T(8,128)(2,1)S(1)} %get-tuple-element.24), channel_id=1, source_target_pairs={{0,32},{32,0},{1,33},{33,1},{2,34},{34,2},{3,35},{35,3},{4,36},{36... | collective-permute-start | bytes 4915208 | tf_op jit(solution)/shard_map/ppermute | solution.py:312
  25.1 3.5 %collective-permute-done.2 = bf16[8,2,40,1280]{3,2,1,0:T(8,128)(2,1)S(1)} collective-permute-done((bf16[8,2,40,1280]{3,2,1,0:T(8,128)(2,1)S(1)}, bf16[8,2,40,1280]{3,2,1,0:T(8,128)(2,1)S(1)}, u32[]{:S(2)}, u32[]{:S(2)}) %collective-permute-start.2) | collective-permute-done | bytes 1638432 | tf_op jit(solution)/shard_map/ppermute | solution.py:312
  28.6 1.6 %add_convert_fusion = bf16[8,2,40,1280]{3,2,1,0:T(8,128)(2,1)} fusion(bf16[8,2,40,1280]{3,2,1,0:T(8,128)(2,1)S(1)} %collective-permute-done.2, bf16[8,2,40,1280]{3,2,1,0:T(8,128)(2,1)S(1)} %get-tuple-element.23), kind=kLoop, calls=%fused_computation | loop fusion | flops 3276800 | bytes 4915200 | tf_op jit(solution)/shard_map/convert_element_type | solution.py:313
  30.2 0.0 copy-start.12
  30.2 0.0 copy-start.13
  30.3 0.0 reduce-scatter.2.cloned.1.call-update
  30.3 10.1 %all-to-all-start = ((bf16[32,64,128]{2,1,0:T(8,128)(2,1)}), bf16[32,64,128]{2,1,0:T(8,128)(2,1)S(1)}, u32[]{:S(2)}, u32[]{:S(2)}) async-start(bf16[32,64,128]{2,1,0:T(8,128)(2,1)} %get-tuple-element.15), calls=%async_computation | async-start | bytes 1048576 | tf_op jit(solution)/shard_map/all_to_all | solution.py:296
  40.4 0.1 pad_add_fusion.place
  40.5 18.0 %all-to-all-done.slabs = bf16[32,64,128]{2,1,0:T(8,128)(2,1)S(1)} async-done(((bf16[32,64,128]{2,1,0:T(8,128)(2,1)}), bf16[32,64,128]{2,1,0:T(8,128)(2,1)S(1)}, u32[]{:S(2)}, u32[]{:S(2)}) %all-to-all-start) | async-done | bytes 524320 | tf_op jit(solution)/shard_map/all_to_all | solution.py:296
  58.5 0.0 copy-done.3
  58.5 0.4 shard_map.140
  58.9 1.9 %collective-permute-start.1 = (bf16[384,128]{1,0:T(8,128)(2,1)S(1)}, bf16[384,128]{1,0:T(8,128)(2,1)S(1)}, u32[]{:S(2)}, u32[]{:S(2)}) collective-permute-start(bf16[384,128]{1,0:T(8,128)(2,1)S(1)} %get-tuple-element.27), channel_id=1, source_target_pairs={{32,0},{64,32},{96,64},{128,96},{160,128},{192,160},{224,192},{256... | collective-permute-start | bytes 294920 | tf_op jit(solution)/shard_map/ppermute | solution.py:343
  60.8 2.4 %collective-permute-start = (bf16[384,128]{1,0:T(8,128)(2,1)S(1)}, bf16[384,128]{1,0:T(8,128)(2,1)S(1)}, u32[]{:S(2)}, u32[]{:S(2)}) collective-permute-start(bf16[384,128]{1,0:T(8,128)(2,1)S(1)} %get-tuple-element.28), channel_id=1, source_target_pairs={{0,32},{32,64},{64,96},{96,128},{128,160},{160,192},{192,224},{224... | collective-permute-start | bytes 294920 | tf_op jit(solution)/shard_map/ppermute | solution.py:342
  63.2 0.0 copy-done.9
  63.3 0.0 copy-done.10
  63.3 0.0 copy-done.11
  63.3 0.0 copy-done.12
  63.3 0.0 copy-done.13
  63.3 0.0 copy-start
  63.3 3.4 %shard_map.141 = (bf16[5,1152,128]{2,1,0:T(8,128)(2,1)S(1)}, bf16[2304,640]{1,0:T(8,128)(2,1)S(1)}, f32[9,384,128]{2,1,0:T(8,128)S(1)}) custom-call(s32[2]{0:T(128)S(1)} %pad_add_fusion.place, f32[9,9,512]{2,1,0:T(8,128)S(1)} %bitcast.27, s32[9,512]{1,0:T(8,128)S(1)} %bitcast.28, s32[1,512]{1,0:T(1,128)S(1)} %bitcast.29, f32[9,640]{1,0:T(8,128)S(1)} %copy-done.10, ...), custom_call_target="tpu_custom_call" | custom-call | flops 1000000000 | bytes 6000000 | tf_op jit(solution)/shard_map/pallas_call | solution.py:316
  66.7 0.0 copy-done
  66.7 0.0 copy-start.4
  66.7 3.9 %shard_map.142.filtered = f32[384,640]{1,0:T(8,128)S(1)} custom-call(bf16[384,640]{1,0:T(8,128)(2,1)S(1)} %get-tuple-element.16.moved, bf16[384,384]{1,0:T(8,128)(2,1)S(1)} %copy-done, f32[9,384,128]{2,1,0:T(8,128)S(1)} %get-tuple-element.17.spread, bf16[5,1152,128]{2,1,0:T(8,128)(2,1)S(1)} %get-tuple-element.18.own_mix), custom_call_target="tpu_custom_call" | custom-call | flops 800000000 | bytes 5000000 | tf_op jit(solution)/shard_map/pallas_call | solution.py:345
  70.6 0.0 collective-permute-done.1.after
  70.6 0.0 collective-permute-done.before
  70.6 0.0 copy-done.4
  70.6 3.3 %shard_map.143 = bf16[32,64,128]{2,1,0:T(8,128)(2,1)} custom-call(f32[384,640]{1,0:T(8,128)S(1)} %shard_map.142.filtered, bf16[384,128]{1,0:T(8,128)(2,1)S(1)} %collective-permute-done.before, bf16[384,128]{1,0:T(8,128)(2,1)S(1)} %collective-permute-done.1.after, bf16[384,384]{1,0:T(8,128)(2,1)S(1)} %copy-done, bf16[384,384]{1,0:T(8,128)(2,1)S(1)} %copy-done.4, ...), custom_call_target="tpu_custom_call" | custom-call | flops 1500000000 | bytes 7000000 | tf_op jit(solution)/shard_map/pallas_call | solution.py:362
  73.9 4.7 %all-to-all-start.1 = ((bf16[32,64,128]{2,1,0:T(8,128)(2,1)}), bf16[32,64,128]{2,1,0:T(8,128)(2,1)S(1)}, u32[]{:S(2)}, u32[]{:S(2)}) async-start(bf16[32,64,128]{2,1,0:T(8,128)(2,1)} %shard_map.143), calls=%async_computation.1 | async-start | bytes 1048576 | tf_op jit(solution)/shard_map/all_to_all | solution.py:370
  78.6 0.0 reduce-scatter.2.cloned.1.call-done
  78.6 0.0 copy-start.5
  78.6 0.9 copy-done.5
  79.6 0.9 shard_map.146
  80.5 16.1 %all-to-all-done.1.slabs = bf16[32,64,128]{2,1,0:T(8,128)(2,1)S(1)} async-done(((bf16[32,64,128]{2,1,0:T(8,128)(2,1)}), bf16[32,64,128]{2,1,0:T(8,128)(2,1)S(1)}, u32[]{:S(2)}, u32[]{:S(2)}) %all-to-all-start.1) | async-done | bytes 524320 | tf_op jit(solution)/shard_map/all_to_all | solution.py:370
  96.6 5.2 %all-to-all-start.2 = ((bf16[32,40,128]{2,1,0:T(8,128)(2,1)}), bf16[32,40,128]{2,1,0:T(8,128)(2,1)S(1)}, u32[]{:S(2)}, u32[]{:S(2)}) async-start(bf16[32,40,128]{2,1,0:T(8,128)(2,1)} %bitcast.17), calls=%async_computation.3 | async-start | bytes 655360 | tf_op jit(solution)/shard_map/all_to_all | solution.py:378
  101.8 0.0 copy-done.2
  101.8 1.5 %shard_map.144 = bf16[384,640]{1,0:T(8,128)(2,1)} custom-call(bf16[32,64,128]{2,1,0:T(8,128)(2,1)S(1)} %all-to-all-done.1.slabs, bf16[384,640]{1,0:T(8,128)(2,1)S(1)} %bitcast.23), custom_call_target="tpu_custom_call" | custom-call | flops 100000000 | bytes 2000000 | tf_op jit(solution)/shard_map/pallas_call | solution.py:371
  103.3 13.3 %all-to-all-done.2.parts = bf16[32,40,128]{2,1,0:T(8,128)(2,1)S(1)} async-done(((bf16[32,40,128]{2,1,0:T(8,128)(2,1)}), bf16[32,40,128]{2,1,0:T(8,128)(2,1)S(1)}, u32[]{:S(2)}, u32[]{:S(2)}) %all-to-all-start.2) | async-done | bytes 327712 | tf_op jit(solution)/shard_map/all_to_all | solution.py:378
  116.6 0.8 shard_map.147
  (7 shorter events, 0.0 us)
Async XLA Ops:
  7.2 71.5 %reduce-scatter.2.cloned.1.call-start = ((), (), s32[]{:S(2)}) async-start(), calls=%async_computation.4 | async-start | bytes 1843200 | tf_op jit(solution)/shard_map/reduce_scatter | solution.py:314
  7.2 1.0 copy-start.1
  8.2 1.4 %copy-start.6 = (bf16[640,1280]{1,0:T(8,128)(2,1)S(1)}, bf16[640,1280]{1,0:T(8,128)(2,1)}, u32[]{:S(2)}) copy-start(bf16[640,1280]{1,0:T(8,128)(2,1)} %w_in.1) | copy-start | bytes 4915204
  9.7 1.4 %copy-start.7 = (bf16[1280,640]{1,0:T(8,128)(2,1)S(1)}, bf16[1280,640]{1,0:T(8,128)(2,1)}, u32[]{:S(2)}) copy-start(bf16[1280,640]{1,0:T(8,128)(2,1)} %w_out.1) | copy-start | bytes 4915204
  11.1 1.0 copy-start.8
  23.2 5.4 %collective-permute-start.2 = (bf16[8,2,40,1280]{3,2,1,0:T(8,128)(2,1)S(1)}, bf16[8,2,40,1280]{3,2,1,0:T(8,128)(2,1)S(1)}, u32[]{:S(2)}, u32[]{:S(2)}) collective-permute-start(bf16[8,2,40,1280]{3,2,1,0:T(8,128)(2,1)S(1)} %get-tuple-element.24), channel_id=1, source_target_pairs={{0,32},{32,0},{1,33},{33,1},{2,34},{34,2},{3,35},{35,3},{4,36},{36... | collective-permute-start | bytes 4915208 | tf_op jit(solution)/shard_map/ppermute | solution.py:312
  30.2 28.3 %copy-start.3 = (bf16[640,256]{1,0:T(8,128)(2,1)S(1)}, bf16[640,256]{1,0:T(8,128)(2,1)}, u32[]{:S(2)}) copy-start(bf16[640,256]{1,0:T(8,128)(2,1)} %constant.33.clone.pick) | copy-start | bytes 983044
  30.2 33.0 %copy-start.9 = (f32[9,512,9]{1,2,0:T(8,128)S(1)}, f32[9,512,9]{1,2,0:T(8,128)}, u32[]{:S(2)}) copy-start(f32[9,512,9]{1,2,0:T(8,128)} %param.17) | copy-start | bytes 497668
  30.2 33.0 %copy-start.10 = (f32[9,640]{1,0:T(8,128)S(1)}, f32[9,640]{1,0:T(8,128)}, u32[]{:S(2)}) copy-start(f32[9,640]{1,0:T(8,128)} %chan.1) | copy-start | bytes 69124
  30.2 33.0 %copy-start.11 = (s32[512,9]{0,1:T(8,128)S(1)}, s32[512,9]{0,1:T(8,128)}, u32[]{:S(2)}) copy-start(s32[512,9]{0,1:T(8,128)} %param.19) | copy-start | bytes 55300
  30.2 33.0 %copy-start.12 = (f32[9,384]{1,0:T(8,128)S(1)}, f32[9,384]{1,0:T(8,128)}, u32[]{:S(2)}) copy-start(f32[9,384]{1,0:T(8,128)} %basis.1) | copy-start | bytes 41476
  30.2 33.0 %copy-start.13 = (s32[512]{0:T(512)S(1)}, s32[512]{0:T(512)}, u32[]{:S(2)}) copy-start(s32[512]{0:T(512)} %param.20) | copy-start | bytes 6148
  30.3 28.2 %all-to-all-start = ((bf16[32,64,128]{2,1,0:T(8,128)(2,1)}), bf16[32,64,128]{2,1,0:T(8,128)(2,1)S(1)}, u32[]{:S(2)}, u32[]{:S(2)}) async-start(bf16[32,64,128]{2,1,0:T(8,128)(2,1)} %get-tuple-element.15), calls=%async_computation | async-start | bytes 1048576 | tf_op jit(solution)/shard_map/all_to_all | solution.py:296
  58.9 11.7 %collective-permute-start.1 = (bf16[384,128]{1,0:T(8,128)(2,1)S(1)}, bf16[384,128]{1,0:T(8,128)(2,1)S(1)}, u32[]{:S(2)}, u32[]{:S(2)}) collective-permute-start(bf16[384,128]{1,0:T(8,128)(2,1)S(1)} %get-tuple-element.27), channel_id=1, source_target_pairs={{32,0},{64,32},{96,64},{128,96},{160,128},{192,160},{224,192},{256... | collective-permute-start | bytes 294920 | tf_op jit(solution)/shard_map/ppermute | solution.py:343
  60.8 9.8 %collective-permute-start = (bf16[384,128]{1,0:T(8,128)(2,1)S(1)}, bf16[384,128]{1,0:T(8,128)(2,1)S(1)}, u32[]{:S(2)}, u32[]{:S(2)}) collective-permute-start(bf16[384,128]{1,0:T(8,128)(2,1)S(1)} %get-tuple-element.28), channel_id=1, source_target_pairs={{0,32},{32,64},{64,96},{96,128},{128,160},{160,192},{192,224},{224... | collective-permute-start | bytes 294920 | tf_op jit(solution)/shard_map/ppermute | solution.py:342
  63.3 3.4 %copy-start = (bf16[384,384]{1,0:T(8,128)(2,1)S(1)}, bf16[384,384]{1,0:T(8,128)(2,1)}, u32[]{:S(2)}) copy-start(bf16[384,384]{1,0:T(8,128)(2,1)} %constant.31.clone.forward) | copy-start | bytes 884740
  66.7 3.9 %copy-start.4 = (bf16[384,384]{1,0:T(8,128)(2,1)S(1)}, bf16[384,384]{1,0:T(8,128)(2,1)}, u32[]{:S(2)}) copy-start(bf16[384,384]{1,0:T(8,128)(2,1)} %constant.32.clone.inverse) | copy-start | bytes 884740
  73.9 27.9 %copy-start.2 = (bf16[32,12,640]{2,0,1:T(8,128)(2,1)S(1)}, bf16[32,12,640]{2,0,1:T(8,128)(2,1)}, u32[]{:S(2)}) copy-start(bf16[32,12,640]{2,0,1:T(8,128)(2,1)} %param.13) | copy-start | bytes 1474564
  73.9 22.7 %all-to-all-start.1 = ((bf16[32,64,128]{2,1,0:T(8,128)(2,1)}), bf16[32,64,128]{2,1,0:T(8,128)(2,1)S(1)}, u32[]{:S(2)}, u32[]{:S(2)}) async-start(bf16[32,64,128]{2,1,0:T(8,128)(2,1)} %shard_map.143), calls=%async_computation.1 | async-start | bytes 1048576 | tf_op jit(solution)/shard_map/all_to_all | solution.py:370
  78.6 0.9 copy-start.5
  96.6 20.0 %all-to-all-start.2 = ((bf16[32,40,128]{2,1,0:T(8,128)(2,1)}), bf16[32,40,128]{2,1,0:T(8,128)(2,1)S(1)}, u32[]{:S(2)}, u32[]{:S(2)}) async-start(bf16[32,40,128]{2,1,0:T(8,128)(2,1)} %bitcast.17), calls=%async_computation.3 | async-start | bytes 655360 | tf_op jit(solution)/shard_map/all_to_all | solution.py:378
Sparse Core Ops, SparseCore 0:
  30.4 48.0 reduce-scatter.1

commit v2 on v1

v2 whole, which is shorter than its diff:
```python
import functools
import math

import jax
import jax.numpy as jnp
import numpy as np
from jax import lax
from jax.experimental import pallas as pl
from jax.experimental.pallas import tpu as pltpu
from jax.sharding import Mesh, PartitionSpec as P

f32 = jnp.float32
bf16 = jnp.bfloat16
LAT = ("z", "core")
LON = ("y", "x")
ROWS = 32
LONS = 12
PEERS = 32
LOCAL = 20
NLON = 384
NF = 192
NB = 9
REACH = 4
GROUPS = 5
SLAB = LONS * GROUPS
PAD = 64
TALL = PEERS * SLAB + 8


def nt(a, b, precision=None):
    return lax.dot_general(a, b, (((1,), (1,)), ((), ())), preferred_element_type=f32, precision=precision)


def tn(a, b):
    return lax.dot_general(a, b, (((0,), (0,)), ((), ())), preferred_element_type=f32)


def nn(a, b, precision=None):
    return lax.dot_general(a, b, (((1,), (0,)), ((), ())), preferred_element_type=f32, precision=precision)


def swap_quarters(tiles):
    quarter = lax.broadcasted_iota(jnp.int32, tiles[0].shape, 1) // 32
    out = []
    for b in range(4):
        made = None
        for q in range(4):
            shift = (32 * (q - b)) % 128
            moved = pltpu.roll(tiles[q], shift, 1) if shift else tiles[q]
            made = moved if made is None else jnp.where(quarter == q, moved, made)
        out.append(made)
    return out


def gelu_parts(v):
    square = v * v
    tangent = jnp.tanh(0.7978845608 * (v + 0.044715 * v * square))
    half = 0.5 * (1.0 + tangent)
    slope = half + 0.5 * v * (1.0 - tangent * tangent) * 0.7978845608 * (1.0 + 0.134145 * square)
    return v * half, slope


def to_slabs(tall, out):
    for d in range(PEERS):
        out[d] = tall[SLAB * d : SLAB * d + PAD, :].astype(bf16)


def from_slabs(slabs, tall):
    for d in range(PEERS):
        tall[SLAB * d : SLAB * d + PAD, :] = slabs[d].astype(f32)


def head_kernel(core, tok, cot, w_in, w_out, pre_grad, mine, theirs, tok_t, cot_t, scr):
    @pl.when(pl.program_id(0) == 0)
    def _():
        tok_t[...] = tok[...].astype(f32).T.astype(bf16)
        cot_t[...] = cot[...].astype(f32).T.astype(bf16)

    gelu_value, slope = gelu_parts(nn(tok[...], w_in[...]))
    grad = (nt(cot[...], w_out[...]) * slope).astype(bf16)
    pre_grad[...] = grad
    c = core[0]
    depth, _, size = mine.shape[0], mine.shape[1], mine.shape[2]
    for which, (left, right) in enumerate(((tok_t, grad), (cot_t, gelu_value.astype(bf16)))):
        scr[which] = nn(left[...], right)
        for z in range(depth):
            own = pl.multiple_of((2 * z + c) * size, 8)
            other = pl.multiple_of((2 * z + 1 - c) * size, 8)
            mine[z, which] = scr[which, pl.ds(own, size), :].astype(bf16)
            theirs[z, which] = scr[which, pl.ds(other, size), :].astype(bf16)


def lift_kernel(pre_grad, cot, w_in, send, tall):
    j = pl.program_id(0)
    whole = cot[...].astype(f32).T + nt(w_in[...], pre_grad[...])
    for a in range(LONS // 4):
        tiles = [whole[q * 32 : (q + 1) * 32, a * 128 : (a + 1) * 128] for q in range(4)]
        for b, tile in enumerate(swap_quarters(tiles)):
            tall[pl.ds((4 * a + b) * GROUPS + j, PEERS, stride=SLAB), :] = tile

    @pl.when(j == pl.num_programs(0) - 1)
    def _():
        tall[TALL - 8 :, :] = jnp.zeros((8, 128), f32)
        to_slabs(tall, send)


def add_kernel(one, two, out):
    for z in range(one.shape[0]):
        for w in range(one.shape[1]):
            out[z, w] = (one[z, w].astype(f32) + two[z, w].astype(f32)).astype(bf16)


def prep_kernel(place, row_w, cols, widths, chan, own_mix, rim_mix, token):
    token[...] = jnp.zeros(token.shape, f32)
    row_start, lon = place[0], place[1]
    high = lax.Precision.HIGHEST
    count = cols.shape[1]
    at = lax.broadcasted_iota(jnp.int32, (64, count), 0)
    rim = at % 4
    source = jnp.where(at < 32, at, jnp.where(at < 48, rim - REACH, rim + ROWS)) + row_start
    pick = (source == lax.broadcasted_iota(jnp.int32, (64, count), 1)).astype(f32)
    col = nt(pick, cols[...].astype(f32), high) - row_start.astype(f32)
    width = nt(pick, widths[...].astype(f32), high)
    lane = lax.broadcasted_iota(jnp.int32, (64, 128), 1)
    target = (lane % 32).astype(f32)
    hits = [
        jnp.where((col[:, s : s + 1] == target) & (width > s), 1.0, 0.0) for s in range(NB)
    ]
    chan_row = lax.broadcasted_iota(jnp.int32, (640, 640), 0)
    chan_lane = lax.broadcasted_iota(jnp.int32, (640, 640), 1)
    chan_pick = (chan_row == (chan_lane // 32) * 32 + lon).astype(f32)
    chan_w = nn(chan[...], chan_pick, high)
    rim_mix[...] = jnp.zeros(rim_mix.shape, bf16)
    quarter = lane[:32] // 32
    rim_at = lax.broadcasted_iota(jnp.int32, (16, 128), 0) // 4
    rim_quarter = lane[:16] // 32
    for k in range(NB):
        coef = nt(pick, row_w[k], high)
        weight = None
        for s in range(NB):
            term = coef[:, s : s + 1] * hits[s]
            weight = term if weight is None else weight + term
        for j in range(GROUPS):
            scaled = weight * chan_w[k : k + 1, 128 * j : 128 * (j + 1)]
            for q in range(4):
                own_mix[j, k * 128 + q * 32 : k * 128 + (q + 1) * 32, :] = jnp.where(
                    quarter == q, scaled[:32], 0.0
                ).astype(bf16)
            for side in range(2):
                part = scaled[32 + 16 * side : 48 + 16 * side]
                start = (k * 2 + side) * 128 + 16 * j
                rim_mix[start : start + 16, 128 * j : 128 * (j + 1)] = jnp.where(
                    rim_quarter == rim_at, part, 0.0
                ).astype(bf16)


def open_kernel(slabs, pick, _ready, moved, first, last, tall):
    from_slabs(slabs, tall)
    for j in range(GROUPS):
        moved[:, 128 * j : 128 * (j + 1)] = tall[pl.ds(j, NLON, stride=GROUPS), :].astype(bf16)
    edges = nn(moved[...], pick[...]).astype(bf16)
    last[...] = edges[:, :128]
    first[...] = edges[:, 128:]


def mix(spectra, basis_t, mixed, step, start):
    first, second = spectra[:NF], spectra[NF:]
    lanes = spectra.shape[1]
    for k in range(NB):
        cosine = jnp.broadcast_to(basis_t[:NF, k : k + 1], (NF, lanes))
        sine = jnp.broadcast_to(basis_t[NF:, k : k + 1], (NF, lanes))
        at = start + step * k
        mixed[:NF, at : at + lanes] = (cosine * first + sine * second).astype(bf16)
        mixed[NF:, at : at + lanes] = (cosine * second - sine * first).astype(bf16)


def turned_basis(basis):
    return jnp.concatenate([basis[...], jnp.zeros((128 - NB, NLON), f32)], 0).T


def own_kernel(moved, forward, basis, own_mix, filtered, mixed, held, sems):
    copies = [pltpu.make_async_copy(own_mix.at[j], held.at[j], sems.at[j]) for j in range(GROUPS)]
    for copy in copies:
        copy.start()
    basis_t = turned_basis(basis)
    for j in range(GROUPS):
        lanes = slice(128 * j, 128 * (j + 1))
        mix(nn(forward[...], moved[:, lanes]), basis_t, mixed.at[j % 2], 128, 0)
        copies[j].wait()
        filtered[:, lanes] = nn(mixed[j % 2], held[j])


def close_kernel(filtered, before, after, forward, inverse, basis, rim_mix, send, mixed, tall, held, sem):
    copy = pltpu.make_async_copy(rim_mix, held, sem)
    copy.start()
    basis_t = turned_basis(basis)
    for side, rim in enumerate((before, after)):
        mix(nn(forward[...], rim[...]), basis_t, mixed, 256, 128 * side)
    tall[TALL - 8 :, :] = jnp.zeros((8, 128), f32)
    copy.wait()
    for j in range(GROUPS):
        lanes = slice(128 * j, 128 * (j + 1))
        whole = (filtered[:, lanes] + nn(mixed[...], held[:, lanes])).astype(bf16)
        tall[pl.ds(j, NLON, stride=GROUPS), :] = nn(inverse[...], whole)
    to_slabs(tall, send)


def merge_kernel(answer, column, out):
    rows = column[0, 0].astype(f32), column[0, 1].astype(f32)
    fill = jnp.zeros((-(2 * rows[0].shape[0]) % 128, rows[0].shape[1]), f32)
    turned = jnp.concatenate([rows[0], rows[1], fill], 0).T
    for d in range(PEERS):
        out[d, :PAD] = answer[d]
        for i in range(turned.shape[1] // 128):
            out[d, PAD + 40 * i : PAD + 40 * (i + 1)] = turned[40 * d : 40 * (d + 1), 128 * i : 128 * (i + 1)].astype(bf16)


def final_kernel(slabs, cot, out, grad_in, grad_out, tall):
    for d in range(PEERS):
        tall[SLAB * d : SLAB * d + PAD, :] = slabs[d, :PAD].astype(f32)
    for j in range(GROUPS):
        for a in range(LONS // 4):
            tiles = [tall[pl.ds((4 * a + b) * GROUPS + j, PEERS, stride=SLAB), :] for b in range(4)]
            turned = jnp.concatenate(tiles, 0).T
            for b, tile in enumerate(swap_quarters([turned[32 * q : 32 * (q + 1)] for q in range(4)])):
                rows = slice((4 * a + b) * 32, (4 * a + b + 1) * 32)
                lanes = slice(128 * j, 128 * (j + 1))
                out[rows, lanes] = (cot[rows, lanes].astype(f32) + tile).astype(bf16)
    size = grad_in.shape[0]
    total = slabs[0, PAD:].astype(f32)
    for d in range(1, PEERS):
        total = total + slabs[d, PAD:].astype(f32)
    if total.shape[0] > 40:
        total = jnp.concatenate([total[i : i + 40] for i in range(0, total.shape[0], 40)], 1)
    lanes = total.shape[1]
    filled = jnp.concatenate([total, jnp.zeros((128 - 40, lanes), f32)], 0)
    grad_in[...] = filled.T[:size, :40]
    grad_out[...] = total[:, size : 2 * size]


def tables():
    lon = np.arange(NLON)
    freq = np.arange(NLON) % NF
    phase = (lon[:, None] * freq[None, :] % NLON) * (2.0 * math.pi / NLON)
    forward = np.where(np.arange(NLON)[None, :] >= NF, np.sin(phase), np.cos(phase))
    inverse = forward.T * (np.where(freq == 0, 1.0, 2.0) / NLON)[:, None]
    return jnp.asarray(forward.T, bf16), jnp.asarray(inverse.T, bf16)


def rim_picks():
    pick = np.zeros((640, 256), np.float32)
    for c in range(LOCAL):
        for r in range(REACH):
            pick[c * 32 + ROWS - REACH + r, c * 4 + r] = 1.0
            pick[c * 32 + r, 128 + c * 4 + r] = 1.0
    return jnp.asarray(pick, bf16)


def shape(*dims, dtype=bf16):
    return jax.ShapeDtypeStruct(dims, dtype)


VMEM = pl.BlockSpec(memory_space=pltpu.VMEM)
TOKEN = shape(8, 128, dtype=f32)
HBM = pl.BlockSpec(memory_space=pltpu.HBM)
SMEM = pl.BlockSpec(memory_space=pltpu.SMEM)


def call(kernel, out, ins, flops, moved, scratch=(), limit=24, **grid):
    options = dict(grid)
    if "grid" not in options:
        options["in_specs"] = ins
        options["out_specs"] = jax.tree.map(lambda _: VMEM, out)
    return pl.pallas_call(
        kernel,
        out_shape=out,
        scratch_shapes=list(scratch),
        compiler_params=pltpu.CompilerParams(vmem_limit_bytes=limit << 20),
        cost_estimate=pl.CostEstimate(flops=int(flops), bytes_accessed=int(moved), transcendentals=0),
        **options,
    )


def body(mlp_input, out_cot, w_in, w_out, chan_weights, row_weights, basis_spectra, band_cols, band_widths):
    tokens_n = ROWS * LONS
    depth = lax.axis_size("z")
    n_lat = depth * lax.axis_size("core")
    part = 640 // n_lat
    lat, lon, core = lax.axis_index(LAT), lax.axis_index(LON), lax.axis_index("core")
    tokens = mlp_input.transpose(1, 0, 2).reshape(tokens_n, 640)
    cotangent = out_cot.transpose(1, 0, 2).reshape(tokens_n, 640)
    whole = lambda *dims: pl.BlockSpec(dims, lambda i: (0,) * len(dims))

    half = shape(depth, 2, part, 1280)
    half_spec = pl.BlockSpec((depth, 2, part, 256), lambda i: (0, 0, 0, i))
    pre_grad, mine, theirs = call(
        head_kernel,
        (shape(tokens_n, 1280), half, half),
        None,
        3e9,
        8e6,
        [pltpu.VMEM((640, tokens_n), bf16), pltpu.VMEM((640, tokens_n), bf16), pltpu.VMEM((2, 640, 256), f32)],
        limit=62,
        grid=(5,),
        in_specs=[
            SMEM,
            whole(tokens_n, 640),
            whole(tokens_n, 640),
            pl.BlockSpec((640, 256), lambda i: (0, i)),
            pl.BlockSpec((256, 640), lambda i: (i, 0)),
        ],
        out_specs=[pl.BlockSpec((tokens_n, 256), lambda i: (0, i)), half_spec, half_spec],
    )(core.reshape(1), tokens, cotangent, w_in, w_out)
    partner = lax.ppermute(theirs, "core", [(0, 1), (1, 0)])

    send = call(
        lift_kernel,
        shape(PEERS, PAD, 128),
        None,
        2e9,
        4e6,
        [pltpu.VMEM((TALL, 128), f32)],
        limit=62,
        grid=(GROUPS,),
        in_specs=[
            whole(tokens_n, 1280),
            pl.BlockSpec((tokens_n, 128), lambda j: (0, j)),
            pl.BlockSpec((128, 1280), lambda j: (j, 0)),
        ],
        out_specs=whole(PEERS, PAD, 128),
    )(pre_grad, cotangent, w_in)
    received = lax.all_to_all(send, LON, split_axis=0, concat_axis=0, tiled=True)

    slab = pl.BlockSpec((1, 2, part, 1280), lambda i: (i, 0, 0, 0))
    chip = call(
        add_kernel, half, None, 1e6, 5e6, limit=62, grid=(depth,), in_specs=[slab] * 2, out_specs=slab
    )(mine, partner)
    column = lax.psum_scatter(chip, "z", scatter_dimension=0, tiled=True)

    own_mix, rim_mix, ready = call(
        prep_kernel,
        (shape(GROUPS, NB * 128, 128), shape(NB * 256, 640), TOKEN),
        [SMEM] + [VMEM] * 4,
        1e9,
        6e6,
        limit=62,
    )(
        jnp.stack([lat * ROWS, lon]).astype(jnp.int32),
        row_weights.transpose(0, 2, 1),
        band_cols.T,
        band_widths.reshape(1, -1),
        chan_weights,
    )

    forward, inverse = tables()
    moved, first, last = call(
        open_kernel,
        (shape(NLON, 640), shape(NLON, 128), shape(NLON, 128)),
        [VMEM] * 3,
        1e8,
        2e6,
        [pltpu.VMEM((TALL, 128), f32)],
    )(received, rim_picks(), ready)
    up = [(i, i + 1) for i in range(n_lat - 1)]
    before = lax.ppermute(last, LAT, up)
    after = lax.ppermute(first, LAT, [(b, a) for a, b in up])

    filtered = call(
        own_kernel,
        shape(NLON, 640, dtype=f32),
        [VMEM] * 3 + [HBM],
        8e8,
        5e6,
        [
            pltpu.VMEM((2, NLON, NB * 128), bf16),
            pltpu.VMEM((GROUPS, NB * 128, 128), bf16),
            pltpu.SemaphoreType.DMA((GROUPS,)),
        ],
        limit=62,
    )(moved, forward, basis_spectra, own_mix)

    answer = call(
        close_kernel,
        shape(PEERS, PAD, 128),
        [VMEM] * 6 + [HBM],
        1.5e9,
        7e6,
        [
            pltpu.VMEM((NLON, NB * 256), bf16),
            pltpu.VMEM((TALL, 128), f32),
            pltpu.VMEM((NB * 256, 640), bf16),
            pltpu.SemaphoreType.DMA,
        ],
        limit=62,
    )(filtered, before, after, forward, inverse, basis_spectra, rim_mix)
    tall = PAD + 40 * -(-2 * part // 128)
    merged = call(merge_kernel, shape(PEERS, tall, 128), [VMEM] * 2, 1e6, 2e6, limit=62)(answer, column)
    returned = lax.all_to_all(merged, LON, split_axis=0, concat_axis=0, tiled=True)
    grid_grad, grad_in, grad_out = call(
        final_kernel,
        (shape(tokens_n, 640), shape(part, 40, dtype=f32), shape(40, part, dtype=f32)),
        [VMEM] * 2,
        1e8,
        2e6,
        [pltpu.VMEM((TALL, 128), f32)],
    )(returned, cotangent)
    grid_grad = grid_grad.reshape(LONS, ROWS, 640).transpose(1, 0, 2)
    return grid_grad, grad_in, grad_out


def solution(mesh):
    chips = Mesh(mesh.devices.reshape(-1, 2, 8, 4), ("z", "core", "y", "x"))
    grid = P(LAT, LON, None)
    return jax.shard_map(
        body,
        mesh=chips,
        in_specs=(grid, grid, P(), P(), P(), P(), P(), P(), P()),
        out_specs=(grid, P(LAT, LON), P(LON, LAT)),
        check_vma=False,
    )
```

time: 125 us -> 127 us (1.016)
  the two profiles are of different devices: /device:TPU:64 before, /device:TPU:195 now
where the time goes in v2:
time: 127 us; the launch traced here: 126 us
  Pallas kernels  45.1 us (36%)
  blocking collectives  28.7 us (23%)
  starting transfers between devices  21.6 us (17%)
  between operations  14.2 us (11%)
  waiting for transfers between devices  12.9 us (10%)
  local copies, waits for them, and re-layouts  3.3 us (3%)
    all_to_all x1, blocking collectives, body(): lax.all_to_all(merged, LON, split_axis=0, concat_axis=0, tiled=True)  28.7 us
    all_to_all x1, starting transfers between devices, body(): lax.all_to_all(send, LON, split_axis=0, concat_axis=0, tiled=True)  9.68 us
    all_to_all x1, waiting for transfers between devices, body(): lax.all_to_all(send, LON, split_axis=0, concat_axis=0, tiled=True)  9.58 us
    pallas_call x1, Pallas kernels, body(): call(head_kernel, (shape(tokens_n, 1280), half, half), None, 3000000000.0...  8.79 us
    pallas_call x1, Pallas kernels, body(): call(close_kernel, shape(PEERS, PAD, 128), [VMEM] * 6 + [HBM], 1500000000...  7.79 us
    ppermute x1, starting transfers between devices, body(): before = lax.ppermute(last, LAT, up)  7.23 us
    pallas_call x1, Pallas kernels, body(): call(own_kernel, shape(NLON, 640, dtype=f32), [VMEM] * 3 + [HBM], 8000000...  6.46 us
    pallas_call x1, Pallas kernels, body(): call(lift_kernel, shape(PEERS, PAD, 128), None, 2000000000.0, 4000000.0,...  6.17 us
  transfers between devices with their start and end apart: 5, of which 2 were waited for; matrix products, arithmetic and copies ran while one was open for 0% of the time, Pallas kernels for 21%

profile of v2, /device:TPU:195, one launch (start us, length us, event | category | flops | bytes accessed | tf_op | source)
XLA Modules:
  0.0 126.4 jit_solution(7680061897227624164)
XLA Ops:
  7.2 0.0 reduce-scatter.2.cloned.1.call-start
  7.2 8.8 %shard_map.139 = (bf16[384,1280]{1,0:T(8,128)(2,1)}, bf16[8,2,40,1280]{3,2,1,0:T(8,128)(2,1)}, bf16[8,2,40,1280]{3,2,1,0:T(8,128)(2,1)}) custom-call(s32[1]{0:T(128)} %bitcast.core, bf16[384,640]{1,0:T(8,128)(2,1)} %bitcast.18, bf16[384,640]{1,0:T(8,128)(2,1)} %bitcast.15, bf16[640,1280]{1,0:T(8,128)(2,1)} %w_in.3, bf16[1280,640]{1,0:T(8,128)(2,1)} %w_out.1), custom_call_target="tpu_custom_call" | custom-call | flops 3000000000 | bytes 8000000 | tf_op jit(solution)/shard_map/pallas_call | solution.py:296
  16.0 2.6 %collective-permute-start.2 = (bf16[8,2,40,1280]{3,2,1,0:T(8,128)(2,1)}, bf16[8,2,40,1280]{3,2,1,0:T(8,128)(2,1)S(1)}, u32[]{:S(2)}, u32[]{:S(2)}) collective-permute-start(bf16[8,2,40,1280]{3,2,1,0:T(8,128)(2,1)} %get-tuple-element.23), channel_id=1, source_target_pairs={{0,32},{32,0},{1,33},{33,1},{2,34},{34,2},{3,35},{35,3},{4,36},{36... | collective-permute-start | bytes 4915208 | tf_op jit(solution)/shard_map/ppermute | solution.py:314
  18.6 3.3 %collective-permute-done.2.two = bf16[8,2,40,1280]{3,2,1,0:T(8,128)(2,1)S(1)} collective-permute-done((bf16[8,2,40,1280]{3,2,1,0:T(8,128)(2,1)}, bf16[8,2,40,1280]{3,2,1,0:T(8,128)(2,1)S(1)}, u32[]{:S(2)}, u32[]{:S(2)}) %collective-permute-start.2) | collective-permute-done | bytes 1638432 | tf_op jit(solution)/shard_map/ppermute | solution.py:314
  21.9 0.0 copy-start.4
  21.9 1.2 copy-done.4
  23.1 6.0 %shard_map.145 = bf16[8,2,40,1280]{3,2,1,0:T(8,128)(2,1)} custom-call(bf16[8,2,40,1280]{3,2,1,0:T(8,128)(2,1)} %get-tuple-element.22.one, bf16[8,2,40,1280]{3,2,1,0:T(8,128)(2,1)} %copy-done.4), custom_call_target="tpu_custom_call" | custom-call | flops 1000000 | bytes 5000000 | tf_op jit(solution)/shard_map/pallas_call | solution.py:335
  29.1 0.0 reduce-scatter.2.cloned.1.call-update
  29.1 6.2 %shard_map.140 = bf16[32,64,128]{2,1,0:T(8,128)(2,1)} custom-call(bf16[384,1280]{1,0:T(8,128)(2,1)} %get-tuple-element.15.pre_grad, bf16[384,640]{1,0:T(8,128)(2,1)} %bitcast.16, bf16[640,1280]{1,0:T(8,128)(2,1)} %w_in.3), custom_call_target="tpu_custom_call" | custom-call | flops 2000000000 | bytes 4000000 | tf_op jit(solution)/shard_map/pallas_call | solution.py:316
  35.3 9.7 %all-to-all-start = ((bf16[32,64,128]{2,1,0:T(8,128)(2,1)}), bf16[32,64,128]{2,1,0:T(8,128)(2,1)S(1)}, u32[]{:S(2)}, u32[]{:S(2)}) async-start(bf16[32,64,128]{2,1,0:T(8,128)(2,1)} %shard_map.140), calls=%async_computation | async-start | bytes 1048576 | tf_op jit(solution)/shard_map/all_to_all | solution.py:332
  45.0 0.6 pad_add_fusion.place
  45.6 0.0 copy-start.2
  45.6 5.7 %shard_map.141 = (bf16[5,1152,128]{2,1,0:T(8,128)(2,1)}, bf16[2304,640]{1,0:T(8,128)(2,1)}, f32[8,128]{1,0:T(8,128)}) custom-call(s32[2]{0:T(128)} %pad_add_fusion.place, f32[9,9,512]{2,1,0:T(8,128)} %bitcast.20, s32[9,512]{1,0:T(8,128)} %bitcast.21, s32[1,512]{1,0:T(1,128)} %bitcast.22, f32[9,640]{1,0:T(8,128)} %chan.1), custom_call_target="tpu_custom_call" | custom-call | flops 1000000000 | bytes 6000000 | tf_op jit(solution)/shard_map/pallas_call | solution.py:340
  51.3 9.6 %all-to-all-done.slabs = bf16[32,64,128]{2,1,0:T(8,128)(2,1)S(1)} async-done(((bf16[32,64,128]{2,1,0:T(8,128)(2,1)}), bf16[32,64,128]{2,1,0:T(8,128)(2,1)S(1)}, u32[]{:S(2)}, u32[]{:S(2)}) %all-to-all-start) | async-done | bytes 524320 | tf_op jit(solution)/shard_map/all_to_all | solution.py:332
  60.9 0.0 copy-done.2
  60.9 0.0 copy-start.3
  60.9 0.7 copy-done.3
  61.6 0.4 shard_map.142
  62.0 0.0 copy-start
  62.0 0.8 copy-done
  62.8 7.2 %collective-permute-start = (bf16[384,128]{1,0:T(8,128)(2,1)S(1)}, bf16[384,128]{1,0:T(8,128)(2,1)S(1)}, u32[]{:S(2)}, u32[]{:S(2)}) collective-permute-start(bf16[384,128]{1,0:T(8,128)(2,1)S(1)} %get-tuple-element.19), channel_id=1, source_target_pairs={{0,32},{32,64},{64,96},{96,128},{128,160},{160,192},{192,224},{224... | collective-permute-start | bytes 294920 | tf_op jit(solution)/shard_map/ppermute | solution.py:365
  70.0 2.1 %collective-permute-start.1 = (bf16[384,128]{1,0:T(8,128)(2,1)S(1)}, bf16[384,128]{1,0:T(8,128)(2,1)S(1)}, u32[]{:S(2)}, u32[]{:S(2)}) collective-permute-start(bf16[384,128]{1,0:T(8,128)(2,1)S(1)} %get-tuple-element.20), channel_id=1, source_target_pairs={{32,0},{64,32},{96,64},{128,96},{160,128},{192,160},{224,192},{256... | collective-permute-start | bytes 294920 | tf_op jit(solution)/shard_map/ppermute | solution.py:366
  72.1 6.5 %shard_map.143.filtered = f32[384,640]{1,0:T(8,128)} custom-call(bf16[384,640]{1,0:T(8,128)(2,1)} %copy-done, bf16[384,384]{1,0:T(8,128)(2,1)} %constant.31.clone.forward, f32[9,384]{1,0:T(8,128)} %basis.3, bf16[5,1152,128]{2,1,0:T(8,128)(2,1)} %get-tuple-element.18.own_mix), custom_call_target="tpu_custom_call" | custom-call | flops 800000000 | bytes 5000000 | tf_op jit(solution)/shard_map/pallas_call | solution.py:368
  78.6 0.0 collective-permute-done.before
  78.6 0.0 copy-start.5
  78.6 0.0 collective-permute-done.1.after
  78.6 0.0 copy-start.6
  78.6 0.6 copy-done.5
  79.3 0.0 copy-done.6
  79.3 7.8 %shard_map.144.answer = bf16[32,64,128]{2,1,0:T(8,128)(2,1)} custom-call(f32[384,640]{1,0:T(8,128)} %shard_map.143.filtered, bf16[384,128]{1,0:T(8,128)(2,1)} %copy-done.5, bf16[384,128]{1,0:T(8,128)(2,1)} %copy-done.6, bf16[384,384]{1,0:T(8,128)(2,1)} %constant.31.clone.forward, bf16[384,384]{1,0:T(8,128)(2,1)} %constant.32.clone.inverse, f32[9,384]{1,0:T(8,128)} %basis.3, ...), custom_call_target="tpu_custom_call" | custom-call | flops 1500000000 | bytes 7000000 | tf_op jit(solution)/shard_map/pallas_call | solution.py:382
  87.1 0.0 copy-start.1
  87.1 0.0 reduce-scatter.2.cloned.1.call-done.column
  87.1 2.2 %shard_map.146 = bf16[32,104,128]{2,1,0:T(8,128)(2,1)} custom-call(bf16[32,64,128]{2,1,0:T(8,128)(2,1)} %shard_map.144.answer, bf16[1,2,40,1280]{3,2,1,0:T(8,128)(2,1)} %reduce-scatter.2.cloned.1.call-done.column), custom_call_target="tpu_custom_call" | custom-call | flops 1000000 | bytes 2000000 | tf_op jit(solution)/shard_map/pallas_call | solution.py:397
  89.3 28.7 %all_to_all.10.slabs = bf16[32,104,128]{2,1,0:T(8,128)(2,1)S(1)} all-to-all(bf16[32,104,128]{2,1,0:T(8,128)(2,1)} %shard_map.146), channel_id=1, replica_groups=mesh['z'=8,'core'=2,'y'=8,'x'=4] {'y','x'}, dimensions={0} | all-to-all | bytes 1703936 | tf_op jit(solution)/shard_map/all_to_all | solution.py:398
  118.1 0.0 copy-done.1
  118.1 1.5 %shard_map.147 = (bf16[384,640]{1,0:T(8,128)(2,1)}, f32[40,40]{1,0:T(8,128)}, f32[40,40]{1,0:T(8,128)}) custom-call(bf16[32,104,128]{2,1,0:T(8,128)(2,1)S(1)} %all_to_all.10.slabs, bf16[384,640]{1,0:T(8,128)(2,1)S(1)} %bitcast.17), custom_call_target="tpu_custom_call" | custom-call | flops 100000000 | bytes 2000000 | tf_op jit(solution)/shard_map/pallas_call | solution.py:399
Async XLA Ops:
  7.2 80.0 %reduce-scatter.2.cloned.1.call-start = ((), (), s32[]{:S(2)}) async-start(), calls=%async_computation.3 | async-start | bytes 1843200 | tf_op jit(solution)/shard_map/reduce_scatter | solution.py:338
  16.0 5.9 %collective-permute-start.2 = (bf16[8,2,40,1280]{3,2,1,0:T(8,128)(2,1)}, bf16[8,2,40,1280]{3,2,1,0:T(8,128)(2,1)S(1)}, u32[]{:S(2)}, u32[]{:S(2)}) collective-permute-start(bf16[8,2,40,1280]{3,2,1,0:T(8,128)(2,1)} %get-tuple-element.23), channel_id=1, source_target_pairs={{0,32},{32,0},{1,33},{33,1},{2,34},{34,2},{3,35},{35,3},{4,36},{36... | collective-permute-start | bytes 4915208 | tf_op jit(solution)/shard_map/ppermute | solution.py:314
  21.9 1.2 copy-start.4
  35.3 25.6 %all-to-all-start = ((bf16[32,64,128]{2,1,0:T(8,128)(2,1)}), bf16[32,64,128]{2,1,0:T(8,128)(2,1)S(1)}, u32[]{:S(2)}, u32[]{:S(2)}) async-start(bf16[32,64,128]{2,1,0:T(8,128)(2,1)} %shard_map.140), calls=%async_computation | async-start | bytes 1048576 | tf_op jit(solution)/shard_map/all_to_all | solution.py:332
  45.6 15.3 %copy-start.2 = (bf16[640,256]{1,0:T(8,128)(2,1)S(1)}, bf16[640,256]{1,0:T(8,128)(2,1)}, u32[]{:S(2)}) copy-start(bf16[640,256]{1,0:T(8,128)(2,1)} %constant.33.clone.pick) | copy-start | bytes 983044
  60.9 0.7 copy-start.3
  62.0 0.8 copy-start
  62.8 15.8 %collective-permute-start = (bf16[384,128]{1,0:T(8,128)(2,1)S(1)}, bf16[384,128]{1,0:T(8,128)(2,1)S(1)}, u32[]{:S(2)}, u32[]{:S(2)}) collective-permute-start(bf16[384,128]{1,0:T(8,128)(2,1)S(1)} %get-tuple-element.19), channel_id=1, source_target_pairs={{0,32},{32,64},{64,96},{96,128},{128,160},{160,192},{192,224},{224... | collective-permute-start | bytes 294920 | tf_op jit(solution)/shard_map/ppermute | solution.py:365
  70.0 8.6 %collective-permute-start.1 = (bf16[384,128]{1,0:T(8,128)(2,1)S(1)}, bf16[384,128]{1,0:T(8,128)(2,1)S(1)}, u32[]{:S(2)}, u32[]{:S(2)}) collective-permute-start(bf16[384,128]{1,0:T(8,128)(2,1)S(1)} %get-tuple-element.20), channel_id=1, source_target_pairs={{32,0},{64,32},{96,64},{128,96},{160,128},{192,160},{224,192},{256... | collective-permute-start | bytes 294920 | tf_op jit(solution)/shard_map/ppermute | solution.py:366
  78.6 0.6 copy-start.5
  78.6 0.7 copy-start.6
  87.1 31.0 %copy-start.1 = (bf16[32,12,640]{2,0,1:T(8,128)(2,1)S(1)}, bf16[32,12,640]{2,0,1:T(8,128)(2,1)}, u32[]{:S(2)}) copy-start(bf16[32,12,640]{2,0,1:T(8,128)(2,1)} %param.13) | copy-start | bytes 1474564
Sparse Core Ops, SparseCore 0:
  29.3 40.9 reduce-scatter.1

commit v3 on v2

--- a/solution.py
+++ b/solution.py
@@ -104,13 +104,7 @@
         to_slabs(tall, send)
 
 
-def add_kernel(one, two, out):
-    for z in range(one.shape[0]):
-        for w in range(one.shape[1]):
-            out[z, w] = (one[z, w].astype(f32) + two[z, w].astype(f32)).astype(bf16)
-
-
-def prep_kernel(place, row_w, cols, widths, chan, own_mix, rim_mix, token):
+def prep_kernel(place, row_w, cols, widths, chan, basis, own_mix, rim_mix, spread, token):
     token[...] = jnp.zeros(token.shape, f32)
     row_start, lon = place[0], place[1]
     high = lax.Precision.HIGHEST
@@ -152,6 +146,7 @@
                 rim_mix[start : start + 16, 128 * j : 128 * (j + 1)] = jnp.where(
                     rim_quarter == rim_at, part, 0.0
                 ).astype(bf16)
+        spread[k] = jnp.broadcast_to(basis[k : k + 1, :], (128, NLON)).T
 
 
 def open_kernel(slabs, pick, _ready, moved, first, last, tall):
@@ -163,45 +158,29 @@
     first[...] = edges[:, 128:]
 
 
-def mix(spectra, basis_t, mixed, step, start):
+def own_kernel(moved, forward, spread, own_mix, filtered, mixed):
+    spectra = nn(forward[...], moved[...])
     first, second = spectra[:NF], spectra[NF:]
-    lanes = spectra.shape[1]
     for k in range(NB):
-        cosine = jnp.broadcast_to(basis_t[:NF, k : k + 1], (NF, lanes))
-        sine = jnp.broadcast_to(basis_t[NF:, k : k + 1], (NF, lanes))
-        at = start + step * k
-        mixed[:NF, at : at + lanes] = (cosine * first + sine * second).astype(bf16)
-        mixed[NF:, at : at + lanes] = (cosine * second - sine * first).astype(bf16)
-
-
-def turned_basis(basis):
-    return jnp.concatenate([basis[...], jnp.zeros((128 - NB, NLON), f32)], 0).T
-
-
-def own_kernel(moved, forward, basis, own_mix, filtered, mixed, held, sems):
-    copies = [pltpu.make_async_copy(own_mix.at[j], held.at[j], sems.at[j]) for j in range(GROUPS)]
-    for copy in copies:
-        copy.start()
-    basis_t = turned_basis(basis)
+        cosine, sine = spread[k, :NF], spread[k, NF:]
+        mixed[:NF, k * 128 : (k + 1) * 128] = (cosine * first + sine * second).astype(bf16)
+        mixed[NF:, k * 128 : (k + 1) * 128] = (cosine * second - sine * first).astype(bf16)
+    filtered[...] = nn(mixed[...], own_mix[0])
+
+
+def close_kernel(filtered, before, after, forward, inverse, spread, rim_mix, send, mixed, tall):
+    for side, rim in enumerate((before, after)):
+        spectra = nn(forward[...], rim[...])
+        first, second = spectra[:NF], spectra[NF:]
+        for k in range(NB):
+            cosine, sine = spread[k, :NF], spread[k, NF:]
+            at = (k * 2 + side) * 128
+            mixed[:NF, at : at + 128] = (cosine * first + sine * second).astype(bf16)
+            mixed[NF:, at : at + 128] = (cosine * second - sine * first).astype(bf16)
+    whole = (filtered[...] + nn(mixed[...], rim_mix[...])).astype(bf16)
+    tall[TALL - 8 :, :] = jnp.zeros((8, 128), f32)
     for j in range(GROUPS):
-        lanes = slice(128 * j, 128 * (j + 1))
-        mix(nn(forward[...], moved[:, lanes]), basis_t, mixed.at[j % 2], 128, 0)
-        copies[j].wait()
-        filtered[:, lanes] = nn(mixed[j % 2], held[j])
-
-
-def close_kernel(filtered, before, after, forward, inverse, basis, rim_mix, send, mixed, tall, held, sem):
-    copy = pltpu.make_async_copy(rim_mix, held, sem)
-    copy.start()
-    basis_t = turned_basis(basis)
-    for side, rim in enumerate((before, after)):
-        mix(nn(forward[...], rim[...]), basis_t, mixed, 256, 128 * side)
-    tall[TALL - 8 :, :] = jnp.zeros((8, 128), f32)
-    copy.wait()
-    for j in range(GROUPS):
-        lanes = slice(128 * j, 128 * (j + 1))
-        whole = (filtered[:, lanes] + nn(mixed[...], held[:, lanes])).astype(bf16)
-        tall[pl.ds(j, NLON, stride=GROUPS), :] = nn(inverse[...], whole)
+        tall[pl.ds(j, NLON, stride=GROUPS), :] = nn(inverse[...], whole[:, 128 * j : 128 * (j + 1)])
     to_slabs(tall, send)
 
 
@@ -262,7 +241,6 @@
 
 VMEM = pl.BlockSpec(memory_space=pltpu.VMEM)
 TOKEN = shape(8, 128, dtype=f32)
-HBM = pl.BlockSpec(memory_space=pltpu.HBM)
 SMEM = pl.BlockSpec(memory_space=pltpu.SMEM)
 
 
@@ -331,25 +309,22 @@
     )(pre_grad, cotangent, w_in)
     received = lax.all_to_all(send, LON, split_axis=0, concat_axis=0, tiled=True)
 
-    slab = pl.BlockSpec((1, 2, part, 1280), lambda i: (i, 0, 0, 0))
-    chip = call(
-        add_kernel, half, None, 1e6, 5e6, limit=62, grid=(depth,), in_specs=[slab] * 2, out_specs=slab
-    )(mine, partner)
+    chip = (mine.astype(f32) + partner.astype(f32)).astype(bf16)
     column = lax.psum_scatter(chip, "z", scatter_dimension=0, tiled=True)
 
-    own_mix, rim_mix, ready = call(
+    own_mix, rim_mix, spread, ready = call(
         prep_kernel,
-        (shape(GROUPS, NB * 128, 128), shape(NB * 256, 640), TOKEN),
-        [SMEM] + [VMEM] * 4,
+        (shape(GROUPS, NB * 128, 128), shape(NB * 256, 640), shape(NB, NLON, 128, dtype=f32), TOKEN),
+        [SMEM] + [VMEM] * 5,
         1e9,
         6e6,
-        limit=62,
     )(
         jnp.stack([lat * ROWS, lon]).astype(jnp.int32),
         row_weights.transpose(0, 2, 1),
         band_cols.T,
         band_widths.reshape(1, -1),
         chan_weights,
+        basis_spectra,
     )
 
     forward, inverse = tables()
@@ -368,31 +343,28 @@
     filtered = call(
         own_kernel,
         shape(NLON, 640, dtype=f32),
-        [VMEM] * 3 + [HBM],
+        None,
         8e8,
         5e6,
-        [
-            pltpu.VMEM((2, NLON, NB * 128), bf16),
-            pltpu.VMEM((GROUPS, NB * 128, 128), bf16),
-            pltpu.SemaphoreType.DMA((GROUPS,)),
+        [pltpu.VMEM((NLON, NB * 128), bf16)],
+        grid=(GROUPS,),
+        in_specs=[
+            pl.BlockSpec((NLON, 128), lambda j: (0, j)),
+            whole(NLON, NLON),
+            whole(NB, NLON, 128),
+            pl.BlockSpec((1, NB * 128, 128), lambda j: (j, 0, 0)),
         ],
-        limit=62,
-    )(moved, forward, basis_spectra, own_mix)
+        out_specs=pl.BlockSpec((NLON, 128), lambda j: (0, j)),
+    )(moved, forward, spread, own_mix)
 
     answer = call(
         close_kernel,
         shape(PEERS, PAD, 128),
-        [VMEM] * 6 + [HBM],
+        [VMEM] * 7,
         1.5e9,
         7e6,
-        [
-            pltpu.VMEM((NLON, NB * 256), bf16),
-            pltpu.VMEM((TALL, 128), f32),
-            pltpu.VMEM((NB * 256, 640), bf16),
-            pltpu.SemaphoreType.DMA,
-        ],
-        limit=62,
-    )(filtered, before, after, forward, inverse, basis_spectra, rim_mix)
+        [pltpu.VMEM((NLON, NB * 256), bf16), pltpu.VMEM((TALL, 128), f32)],
+    )(filtered, before, after, forward, inverse, spread, rim_mix)
     tall = PAD + 40 * -(-2 * part // 128)
     merged = call(merge_kernel, shape(PEERS, tall, 128), [VMEM] * 2, 1e6, 2e6, limit=62)(answer, column)
     returned = lax.all_to_all(merged, LON, split_axis=0, concat_axis=0, tiled=True)

time: 127 us -> 116 us (0.913)
  the two profiles are of different devices: /device:TPU:195 before, /device:TPU:194 now
where the time goes in v3:
time: 116 us; the launch traced here: 115 us
  blocking collectives  31.6 us (27%)
  Pallas kernels  28.8 us (25%)
  starting transfers between devices  17.8 us (15%)
  waiting for transfers between devices  14.6 us (13%)
  between operations  14.2 us (12%)
  local copies, waits for them, and re-layouts  4.95 us (4%)
  other arithmetic  3.09 us (3%)
    all_to_all x1, blocking collectives, body(): lax.all_to_all(merged, LON, split_axis=0, concat_axis=0, tiled=True)  31.6 us
    all_to_all x1, waiting for transfers between devices, body(): lax.all_to_all(send, LON, split_axis=0, concat_axis=0, tiled=True)  10.9 us
    all_to_all x1, starting transfers between devices, body(): lax.all_to_all(send, LON, split_axis=0, concat_axis=0, tiled=True)  10.3 us
    pallas_call x1, Pallas kernels, body(): call(head_kernel, (shape(tokens_n, 1280), half, half), None, 3000000000.0...  8.74 us
    pallas_call x1, Pallas kernels, body(): call(lift_kernel, shape(PEERS, PAD, 128), None, 2000000000.0, 4000000.0,...  6.22 us
    unnamed x28, local copies, waits for them, and re-layouts  4.95 us
    pallas_call x1, Pallas kernels, body(): call(own_kernel, shape(NLON, 640, dtype=f32), None, 800000000.0, 5000000....  3.9 us
    ppermute x1, waiting for transfers between devices, body(): partner = lax.ppermute(theirs, 'core', [(0, 1), (1, 0)])  3.68 us
  transfers between devices with their start and end apart: 5, of which 2 were waited for; matrix products, arithmetic and copies ran while one was open for 0% of the time, Pallas kernels for 14%

profile of v3, /device:TPU:194, one launch (start us, length us, event | category | flops | bytes accessed | tf_op | source)
XLA Modules:
  0.0 115.0 jit_solution(4603276897041862892)
XLA Ops:
  7.2 0.0 reduce-scatter.2.cloned.1.call-start
  7.2 8.7 %shard_map.139 = (bf16[384,1280]{1,0:T(8,128)(2,1)}, bf16[8,2,40,1280]{3,2,1,0:T(8,128)(2,1)}, bf16[8,2,40,1280]{3,2,1,0:T(8,128)(2,1)}) custom-call(s32[1]{0:T(128)} %bitcast.core, bf16[384,640]{1,0:T(8,128)(2,1)} %bitcast.21, bf16[384,640]{1,0:T(8,128)(2,1)} %bitcast.15, bf16[640,1280]{1,0:T(8,128)(2,1)} %w_in.3, bf16[1280,640]{1,0:T(8,128)(2,1)} %w_out.1), custom_call_target="tpu_custom_call" | custom-call | flops 3000000000 | bytes 8000000 | tf_op jit(solution)/shard_map/pallas_call | solution.py:274
  16.0 1.9 %collective-permute-start.2 = (bf16[8,2,40,1280]{3,2,1,0:T(8,128)(2,1)}, bf16[8,2,40,1280]{3,2,1,0:T(8,128)(2,1)S(1)}, u32[]{:S(2)}, u32[]{:S(2)}) collective-permute-start(bf16[8,2,40,1280]{3,2,1,0:T(8,128)(2,1)} %get-tuple-element.25), channel_id=1, source_target_pairs={{0,32},{32,0},{1,33},{33,1},{2,34},{34,2},{3,35},{35,3},{4,36},{36... | collective-permute-start | bytes 4915208 | tf_op jit(solution)/shard_map/ppermute | solution.py:292
  17.9 3.7 %collective-permute-done.2 = bf16[8,2,40,1280]{3,2,1,0:T(8,128)(2,1)S(1)} collective-permute-done((bf16[8,2,40,1280]{3,2,1,0:T(8,128)(2,1)}, bf16[8,2,40,1280]{3,2,1,0:T(8,128)(2,1)S(1)}, u32[]{:S(2)}, u32[]{:S(2)}) %collective-permute-start.2) | collective-permute-done | bytes 1638432 | tf_op jit(solution)/shard_map/ppermute | solution.py:292
  21.6 3.0 %add_convert_fusion = bf16[8,2,40,1280]{3,2,1,0:T(8,128)(2,1)} fusion(bf16[8,2,40,1280]{3,2,1,0:T(8,128)(2,1)S(1)} %collective-permute-done.2, bf16[8,2,40,1280]{3,2,1,0:T(8,128)(2,1)} %get-tuple-element.24), kind=kLoop, calls=%fused_computation | loop fusion | flops 3276800 | bytes 4915200 | tf_op jit(solution)/shard_map/convert_element_type | solution.py:312
  24.6 0.0 reduce-scatter.2.cloned.1.call-update
  24.6 0.0 copy-start.9
  24.6 0.0 copy-start.10
  24.6 0.0 copy-start.11
  24.6 0.0 copy-start.12
  24.6 0.0 copy-start.13
  24.7 6.2 %shard_map.140 = bf16[32,64,128]{2,1,0:T(8,128)(2,1)} custom-call(bf16[384,1280]{1,0:T(8,128)(2,1)} %get-tuple-element.16.pre_grad, bf16[384,640]{1,0:T(8,128)(2,1)} %bitcast.16, bf16[640,1280]{1,0:T(8,128)(2,1)} %w_in.3), custom_call_target="tpu_custom_call" | custom-call | flops 2000000000 | bytes 4000000 | tf_op jit(solution)/shard_map/pallas_call | solution.py:294
  30.9 10.3 %all-to-all-start = ((bf16[32,64,128]{2,1,0:T(8,128)(2,1)}), bf16[32,64,128]{2,1,0:T(8,128)(2,1)S(1)}, u32[]{:S(2)}, u32[]{:S(2)}) async-start(bf16[32,64,128]{2,1,0:T(8,128)(2,1)} %shard_map.140), calls=%async_computation | async-start | bytes 1048576 | tf_op jit(solution)/shard_map/all_to_all | solution.py:310
  41.1 0.1 pad_add_fusion.place
  41.2 0.0 copy-done.9
  41.2 0.0 copy-done.10
  41.2 0.0 copy-done.11
  41.2 0.0 copy-done.12
  41.2 0.0 copy-done.13
  41.2 0.0 copy-start.7
  41.3 0.0 copy-start.5
  41.3 3.4 %shard_map.141 = (bf16[5,1152,128]{2,1,0:T(8,128)(2,1)S(1)}, bf16[2304,640]{1,0:T(8,128)(2,1)S(1)}, f32[9,384,128]{2,1,0:T(8,128)S(1)}, f32[8,128]{1,0:T(8,128)S(1)}) custom-call(s32[2]{0:T(128)S(1)} %pad_add_fusion.place, f32[9,9,512]{2,1,0:T(8,128)S(1)} %bitcast.18, s32[9,512]{1,0:T(8,128)S(1)} %bitcast.19, s32[1,512]{1,0:T(1,128)S(1)} %bitcast.20, ...), custom_call_target="tpu_custom_call" | custom-call | flops 1000000000 | bytes 6000000 | tf_op jit(solution)/shard_map/pallas_call | solution.py:315
  44.6 0.0 copy-start
  44.6 1.6 %copy-done = bf16[2304,640]{1,0:T(8,128)(2,1)} copy-done((bf16[2304,640]{1,0:T(8,128)(2,1)}, bf16[2304,640]{1,0:T(8,128)(2,1)S(1)}, u32[]{:S(2)}) %copy-start) | copy-done | bytes 2949144
  46.2 0.0 copy-start.3
  46.2 1.1 copy-done.3
  47.3 10.9 %all-to-all-done.slabs = bf16[32,64,128]{2,1,0:T(8,128)(2,1)S(1)} async-done(((bf16[32,64,128]{2,1,0:T(8,128)(2,1)}), bf16[32,64,128]{2,1,0:T(8,128)(2,1)S(1)}, u32[]{:S(2)}, u32[]{:S(2)}) %all-to-all-start) | async-done | bytes 524320 | tf_op jit(solution)/shard_map/all_to_all | solution.py:310
  58.3 0.0 copy-done.7
  58.3 0.4 shard_map.142
  58.6 1.9 %collective-permute-start = (bf16[384,128]{1,0:T(8,128)(2,1)S(1)}, bf16[384,128]{1,0:T(8,128)(2,1)S(1)}, u32[]{:S(2)}, u32[]{:S(2)}) collective-permute-start(bf16[384,128]{1,0:T(8,128)(2,1)S(1)} %get-tuple-element.21), channel_id=1, source_target_pairs={{0,32},{32,64},{64,96},{96,128},{128,160},{160,192},{192,224},{224... | collective-permute-start | bytes 294920 | tf_op jit(solution)/shard_map/ppermute | solution.py:340
  60.6 3.6 %collective-permute-start.1 = (bf16[384,128]{1,0:T(8,128)(2,1)S(1)}, bf16[384,128]{1,0:T(8,128)(2,1)S(1)}, u32[]{:S(2)}, u32[]{:S(2)}) collective-permute-start(bf16[384,128]{1,0:T(8,128)(2,1)S(1)} %get-tuple-element.22), channel_id=1, source_target_pairs={{32,0},{64,32},{96,64},{128,96},{160,128},{192,160},{224,192},{256... | collective-permute-start | bytes 294920 | tf_op jit(solution)/shard_map/ppermute | solution.py:341
  64.2 0.0 copy-done.5
  64.2 0.0 copy-start.4
  64.2 1.4 %copy-done.4 = bf16[5,1152,128]{2,1,0:T(8,128)(2,1)S(1)} copy-done((bf16[5,1152,128]{2,1,0:T(8,128)(2,1)S(1)}, bf16[5,1152,128]{2,1,0:T(8,128)(2,1)}, u32[]{:S(2)}) %copy-start.4) | copy-done | bytes 1474584
  65.6 0.0 copy-start.1
  65.6 0.0 copy-start.8
  65.6 3.9 %shard_map.143.filtered = f32[384,640]{1,0:T(8,128)S(1)} custom-call(bf16[384,640]{1,0:T(8,128)(2,1)S(1)} %get-tuple-element.18.moved, bf16[384,384]{1,0:T(8,128)(2,1)S(1)} %copy-done.5, f32[9,384,128]{2,1,0:T(8,128)S(1)} %get-tuple-element.19.spread, bf16[5,1152,128]{2,1,0:T(8,128)(2,1)S(1)} %copy-done.4), custom_call_target="tpu_custom_call" | custom-call | flops 800000000 | bytes 5000000 | tf_op jit(solution)/shard_map/pallas_call | solution.py:343
  69.5 0.0 collective-permute-done.before
  69.6 0.0 collective-permute-done.1.after
  69.6 0.0 copy-done.1
  69.6 0.0 copy-done.8
  69.6 2.4 %shard_map.144.answer = bf16[32,64,128]{2,1,0:T(8,128)(2,1)S(1)} custom-call(f32[384,640]{1,0:T(8,128)S(1)} %shard_map.143.filtered, bf16[384,128]{1,0:T(8,128)(2,1)S(1)} %collective-permute-done.before, bf16[384,128]{1,0:T(8,128)(2,1)S(1)} %collective-permute-done.1.after, bf16[384,384]{1,0:T(8,128)(2,1)S(1)} %copy-done.5, bf16[384,384]{1,0:T(8,128)(2,1)S(1)} %copy-done.8, ...), custom_call_target="tpu_custom_call" | custom-call | flops 1500000000 | bytes 7000000 | tf_op jit(solution)/shard_map/pallas_call | solution.py:360
  72.0 0.0 copy-start.2
  72.0 0.8 copy-done.2
  72.9 2.2 %shard_map.145 = bf16[32,104,128]{2,1,0:T(8,128)(2,1)} custom-call(bf16[32,64,128]{2,1,0:T(8,128)(2,1)} %copy-done.2, bf16[1,2,40,1280]{3,2,1,0:T(8,128)(2,1)} %reduce-scatter.2.cloned.1.call-done.column), custom_call_target="tpu_custom_call" | custom-call | flops 1000000 | bytes 2000000 | tf_op jit(solution)/shard_map/pallas_call | solution.py:369
  75.1 31.6 %all_to_all.10.slabs = bf16[32,104,128]{2,1,0:T(8,128)(2,1)S(1)} all-to-all(bf16[32,104,128]{2,1,0:T(8,128)(2,1)} %shard_map.145), channel_id=1, replica_groups=mesh['z'=8,'core'=2,'y'=8,'x'=4] {'y','x'}, dimensions={0} | all-to-all | bytes 1703936 | tf_op jit(solution)/shard_map/all_to_all | solution.py:370
  106.7 0.0 copy-done.6
  106.7 1.5 %shard_map.146 = (bf16[384,640]{1,0:T(8,128)(2,1)}, f32[40,40]{1,0:T(8,128)}, f32[40,40]{1,0:T(8,128)}) custom-call(bf16[32,104,128]{2,1,0:T(8,128)(2,1)S(1)} %all_to_all.10.slabs, bf16[384,640]{1,0:T(8,128)(2,1)S(1)} %bitcast.17), custom_call_target="tpu_custom_call" | custom-call | flops 100000000 | bytes 2000000 | tf_op jit(solution)/shard_map/pallas_call | solution.py:371
  (2 shorter events, 0.0 us)
Async XLA Ops:
  7.2 65.7 %reduce-scatter.2.cloned.1.call-start = ((), (), s32[]{:S(2)}) async-start(), calls=%async_computation.3 | async-start | bytes 1843200 | tf_op jit(solution)/shard_map/reduce_scatter | solution.py:313
  16.0 5.6 %collective-permute-start.2 = (bf16[8,2,40,1280]{3,2,1,0:T(8,128)(2,1)}, bf16[8,2,40,1280]{3,2,1,0:T(8,128)(2,1)S(1)}, u32[]{:S(2)}, u32[]{:S(2)}) collective-permute-start(bf16[8,2,40,1280]{3,2,1,0:T(8,128)(2,1)} %get-tuple-element.25), channel_id=1, source_target_pairs={{0,32},{32,0},{1,33},{33,1},{2,34},{34,2},{3,35},{35,3},{4,36},{36... | collective-permute-start | bytes 4915208 | tf_op jit(solution)/shard_map/ppermute | solution.py:292
  24.6 16.6 %copy-start.9 = (f32[9,512,9]{1,2,0:T(8,128)S(1)}, f32[9,512,9]{1,2,0:T(8,128)}, u32[]{:S(2)}) copy-start(f32[9,512,9]{1,2,0:T(8,128)} %param.17) | copy-start | bytes 497668
  24.6 16.6 %copy-start.10 = (f32[9,640]{1,0:T(8,128)S(1)}, f32[9,640]{1,0:T(8,128)}, u32[]{:S(2)}) copy-start(f32[9,640]{1,0:T(8,128)} %chan.1) | copy-start | bytes 69124
  24.6 16.6 %copy-start.11 = (s32[512,9]{0,1:T(8,128)S(1)}, s32[512,9]{0,1:T(8,128)}, u32[]{:S(2)}) copy-start(s32[512,9]{0,1:T(8,128)} %param.19) | copy-start | bytes 55300
  24.6 16.6 %copy-start.12 = (f32[9,384]{1,0:T(8,128)S(1)}, f32[9,384]{1,0:T(8,128)}, u32[]{:S(2)}) copy-start(f32[9,384]{1,0:T(8,128)} %basis.1) | copy-start | bytes 41476
  24.6 16.6 %copy-start.13 = (s32[512]{0:T(512)S(1)}, s32[512]{0:T(512)}, u32[]{:S(2)}) copy-start(s32[512]{0:T(512)} %param.20) | copy-start | bytes 6148
  30.9 27.4 %all-to-all-start = ((bf16[32,64,128]{2,1,0:T(8,128)(2,1)}), bf16[32,64,128]{2,1,0:T(8,128)(2,1)S(1)}, u32[]{:S(2)}, u32[]{:S(2)}) async-start(bf16[32,64,128]{2,1,0:T(8,128)(2,1)} %shard_map.140), calls=%async_computation | async-start | bytes 1048576 | tf_op jit(solution)/shard_map/all_to_all | solution.py:310
  41.2 17.0 %copy-start.7 = (bf16[640,256]{1,0:T(8,128)(2,1)S(1)}, bf16[640,256]{1,0:T(8,128)(2,1)}, u32[]{:S(2)}) copy-start(bf16[640,256]{1,0:T(8,128)(2,1)} %constant.33.clone.pick) | copy-start | bytes 983044
  41.3 23.0 %copy-start.5 = (bf16[384,384]{1,0:T(8,128)(2,1)S(1)}, bf16[384,384]{1,0:T(8,128)(2,1)}, u32[]{:S(2)}) copy-start(bf16[384,384]{1,0:T(8,128)(2,1)} %constant.31.clone.forward) | copy-start | bytes 884740
  44.6 1.6 %copy-start = (bf16[2304,640]{1,0:T(8,128)(2,1)}, bf16[2304,640]{1,0:T(8,128)(2,1)S(1)}, u32[]{:S(2)}) copy-start(bf16[2304,640]{1,0:T(8,128)(2,1)S(1)} %get-tuple-element.23.rim_mix) | copy-start | bytes 8847364
  46.2 1.1 copy-start.3
  58.6 10.9 %collective-permute-start = (bf16[384,128]{1,0:T(8,128)(2,1)S(1)}, bf16[384,128]{1,0:T(8,128)(2,1)S(1)}, u32[]{:S(2)}, u32[]{:S(2)}) collective-permute-start(bf16[384,128]{1,0:T(8,128)(2,1)S(1)} %get-tuple-element.21), channel_id=1, source_target_pairs={{0,32},{32,64},{64,96},{96,128},{128,160},{160,192},{192,224},{224... | collective-permute-start | bytes 294920 | tf_op jit(solution)/shard_map/ppermute | solution.py:340
  60.6 9.0 %collective-permute-start.1 = (bf16[384,128]{1,0:T(8,128)(2,1)S(1)}, bf16[384,128]{1,0:T(8,128)(2,1)S(1)}, u32[]{:S(2)}, u32[]{:S(2)}) collective-permute-start(bf16[384,128]{1,0:T(8,128)(2,1)S(1)} %get-tuple-element.22), channel_id=1, source_target_pairs={{32,0},{64,32},{96,64},{128,96},{160,128},{192,160},{224,192},{256... | collective-permute-start | bytes 294920 | tf_op jit(solution)/shard_map/ppermute | solution.py:341
  64.2 1.4 %copy-start.4 = (bf16[5,1152,128]{2,1,0:T(8,128)(2,1)S(1)}, bf16[5,1152,128]{2,1,0:T(8,128)(2,1)}, u32[]{:S(2)}) copy-start(bf16[5,1152,128]{2,1,0:T(8,128)(2,1)} %copy-done.3) | copy-start | bytes 4423684
  65.6 3.9 %copy-start.1 = (bf16[2304,640]{1,0:T(8,128)(2,1)S(1)}, bf16[2304,640]{1,0:T(8,128)(2,1)}, u32[]{:S(2)}) copy-start(bf16[2304,640]{1,0:T(8,128)(2,1)} %copy-done) | copy-start | bytes 8847364
  65.6 3.9 %copy-start.8 = (bf16[384,384]{1,0:T(8,128)(2,1)S(1)}, bf16[384,384]{1,0:T(8,128)(2,1)}, u32[]{:S(2)}) copy-start(bf16[384,384]{1,0:T(8,128)(2,1)} %constant.32.clone.inverse) | copy-start | bytes 884740
  72.0 0.8 copy-start.2
  72.9 33.8 %copy-start.6 = (bf16[32,12,640]{2,0,1:T(8,128)(2,1)S(1)}, bf16[32,12,640]{2,0,1:T(8,128)(2,1)}, u32[]{:S(2)}) copy-start(bf16[32,12,640]{2,0,1:T(8,128)(2,1)} %param.13) | copy-start | bytes 1474564
Sparse Core Ops, SparseCore 0:
  24.7 45.4 reduce-scatter.1

commit v4 on v3

--- a/solution.py
+++ b/solution.py
@@ -278,7 +278,7 @@
         3e9,
         8e6,
         [pltpu.VMEM((640, tokens_n), bf16), pltpu.VMEM((640, tokens_n), bf16), pltpu.VMEM((2, 640, 256), f32)],
-        limit=62,
+        limit=48,
         grid=(5,),
         in_specs=[
             SMEM,
@@ -298,7 +298,7 @@
         2e9,
         4e6,
         [pltpu.VMEM((TALL, 128), f32)],
-        limit=62,
+        limit=48,
         grid=(GROUPS,),
         in_specs=[
             whole(tokens_n, 1280),
@@ -309,6 +309,7 @@
     )(pre_grad, cotangent, w_in)
     received = lax.all_to_all(send, LON, split_axis=0, concat_axis=0, tiled=True)
 
+    mine, send = lax.optimization_barrier((mine, send))
     chip = (mine.astype(f32) + partner.astype(f32)).astype(bf16)
     column = lax.psum_scatter(chip, "z", scatter_dimension=0, tiled=True)
 

time: 116 us -> 114 us (0.983)
  the two profiles are of different devices: /device:TPU:194 before, /device:TPU:2 now
where the time goes in v4:
time: 114 us
  blocking collectives  29.4 us (26%)
  Pallas kernels  25.9 us (23%)
  waiting for transfers between devices  19.6 us (17%)
  starting transfers between devices  14.9 us (13%)
  between operations  14.2 us (12%)
  local copies, waits for them, and re-layouts  7.94 us (7%)
  other arithmetic  1.65 us (1%)
    all_to_all x1, blocking collectives, body(): lax.all_to_all(merged, LON, split_axis=0, concat_axis=0, tiled=True)  29.4 us
    all_to_all x1, starting transfers between devices, body(): lax.all_to_all(send, LON, split_axis=0, concat_axis=0, tiled=True)  10.4 us
    all_to_all x1, waiting for transfers between devices, body(): lax.all_to_all(send, LON, split_axis=0, concat_axis=0, tiled=True)  10.4 us
    reduce_scatter x1, waiting for transfers between devices, body(): column = lax.psum_scatter(chip, 'z', scatter_dimension=0, tiled=True)  9.21 us
    unnamed x34, local copies, waits for them, and re-layouts  7.94 us
    pallas_call x1, Pallas kernels, body(): call(head_kernel, (shape(tokens_n, 1280), half, half), None, 3000000000.0...  7.78 us
    pallas_call x1, Pallas kernels, body(): call(own_kernel, shape(NLON, 640, dtype=f32), None, 800000000.0, 5000000....  4.07 us
    pallas_call x1, Pallas kernels, body(): call(lift_kernel, shape(PEERS, PAD, 128), None, 2000000000.0, 4000000.0,...  3.99 us
  transfers between devices with their start and end apart: 5, of which 2 were waited for; matrix products, arithmetic and copies ran while one was open for 0% of the time, Pallas kernels for 13%

profile of v4, /device:TPU:2, one launch (start us, length us, event | category | flops | bytes accessed | tf_op | source)
XLA Modules:
  0.0 113.6 jit_solution(16687842419468028140)
XLA Ops:
  7.2 0.0 reduce-scatter.2.cloned.1.call-start
  7.2 0.0 copy-start.6
  7.2 1.0 copy-done.6
  8.2 0.0 copy-start.11
  8.2 1.0 copy-done.11
  9.3 0.0 copy-start.7
  9.3 0.0 copy-start.10
  9.3 7.8 %shard_map.139 = (bf16[384,1280]{1,0:T(8,128)(2,1)S(1)}, bf16[8,2,40,1280]{3,2,1,0:T(8,128)(2,1)S(1)}, bf16[8,2,40,1280]{3,2,1,0:T(8,128)(2,1)S(1)}) custom-call(s32[1]{0:T(128)} %bitcast.core, bf16[384,640]{1,0:T(8,128)(2,1)S(1)} %bitcast.18, bf16[384,640]{1,0:T(8,128)(2,1)S(1)} %bitcast.15, bf16[640,1280]{1,0:T(8,128)(2,1)} %w_in.3, bf16[1280,640]{1,0:T(8,128)(2,1)} %w_out.1), custom_call_target="tpu_custom_call" | custom-call | flops 3000000000 | bytes 8000000 | tf_op jit(solution)/shard_map/pallas_call | solution.py:274
  17.1 1.9 %collective-permute-start.2 = (bf16[8,2,40,1280]{3,2,1,0:T(8,128)(2,1)S(1)}, bf16[8,2,40,1280]{3,2,1,0:T(8,128)(2,1)S(1)}, u32[]{:S(2)}, u32[]{:S(2)}) collective-permute-start(bf16[8,2,40,1280]{3,2,1,0:T(8,128)(2,1)S(1)} %get-tuple-element.27), channel_id=1, source_target_pairs={{0,32},{32,0},{1,33},{33,1},{2,34},{34,2},{3,35},{35,3},{4,36},{36... | collective-permute-start | bytes 4915208 | tf_op jit(solution)/shard_map/ppermute | solution.py:292
  19.0 0.0 copy-done.7
  19.0 0.0 copy-done.10
  19.0 4.0 %shard_map.140 = bf16[32,64,128]{2,1,0:T(8,128)(2,1)} custom-call(bf16[384,1280]{1,0:T(8,128)(2,1)S(1)} %get-tuple-element.17.pre_grad, bf16[384,640]{1,0:T(8,128)(2,1)S(1)} %bitcast.16, bf16[640,1280]{1,0:T(8,128)(2,1)S(1)} %copy-done.10), custom_call_target="tpu_custom_call" | custom-call | flops 2000000000 | bytes 4000000 | tf_op jit(solution)/shard_map/pallas_call | solution.py:294
  23.0 0.0 collective-permute-done.2
  23.0 1.6 %add_convert_fusion = bf16[8,2,40,1280]{3,2,1,0:T(8,128)(2,1)} fusion(bf16[8,2,40,1280]{3,2,1,0:T(8,128)(2,1)S(1)} %collective-permute-done.2, bf16[8,2,40,1280]{3,2,1,0:T(8,128)(2,1)S(1)} %get-tuple-element.26), kind=kLoop, calls=%fused_computation | loop fusion | flops 3276800 | bytes 4915200 | tf_op jit(solution)/shard_map/convert_element_type | solution.py:313
  24.6 0.0 copy-start.13
  24.6 0.0 copy-start.14
  24.6 0.0 reduce-scatter.2.cloned.1.call-update
  24.6 10.4 %all-to-all-start = ((bf16[32,64,128]{2,1,0:T(8,128)(2,1)}), bf16[32,64,128]{2,1,0:T(8,128)(2,1)S(1)}, u32[]{:S(2)}, u32[]{:S(2)}) async-start(bf16[32,64,128]{2,1,0:T(8,128)(2,1)} %shard_map.140), calls=%async_computation | async-start | bytes 1048576 | tf_op jit(solution)/shard_map/all_to_all | solution.py:310
  35.0 0.1 pad_add_fusion.place
  35.1 0.0 copy-done.13
  35.1 0.0 copy-done.14
  35.1 0.0 copy-done.15
  35.1 0.0 copy-done.16
  35.1 0.0 copy-start.12
  35.1 1.0 copy-done.12
  36.1 3.4 %shard_map.141 = (bf16[5,1152,128]{2,1,0:T(8,128)(2,1)S(1)}, bf16[2304,640]{1,0:T(8,128)(2,1)S(1)}, f32[9,384,128]{2,1,0:T(8,128)S(1)}, f32[8,128]{1,0:T(8,128)S(1)}) custom-call(s32[2]{0:T(128)S(1)} %pad_add_fusion.place, f32[9,9,512]{2,1,0:T(8,128)S(1)} %bitcast.19, s32[9,512]{1,0:T(8,128)S(1)} %bitcast.20, s32[1,512]{1,0:T(1,128)S(1)} %bitcast.21, ...), custom_call_target="tpu_custom_call" | custom-call | flops 1000000000 | bytes 6000000 | tf_op jit(solution)/shard_map/pallas_call | solution.py:316
  39.5 1.6 %copy-done = bf16[2304,640]{1,0:T(8,128)(2,1)} copy-done((bf16[2304,640]{1,0:T(8,128)(2,1)}, bf16[2304,640]{1,0:T(8,128)(2,1)S(1)}, u32[]{:S(2)}) %copy-start) | copy-done | bytes 2949144
  41.0 1.1 copy-done.3
  42.2 10.4 %all-to-all-done.slabs = bf16[32,64,128]{2,1,0:T(8,128)(2,1)S(1)} async-done(((bf16[32,64,128]{2,1,0:T(8,128)(2,1)}), bf16[32,64,128]{2,1,0:T(8,128)(2,1)S(1)}, u32[]{:S(2)}, u32[]{:S(2)}) %all-to-all-start) | async-done | bytes 524320 | tf_op jit(solution)/shard_map/all_to_all | solution.py:310
  52.5 0.0 copy-done.8
  52.5 0.4 shard_map.142
  52.9 1.3 %collective-permute-start = (bf16[384,128]{1,0:T(8,128)(2,1)S(1)}, bf16[384,128]{1,0:T(8,128)(2,1)S(1)}, u32[]{:S(2)}, u32[]{:S(2)}) collective-permute-start(bf16[384,128]{1,0:T(8,128)(2,1)S(1)} %get-tuple-element.22), channel_id=1, source_target_pairs={{0,32},{32,64},{64,96},{96,128},{128,160},{160,192},{192,224},{224... | collective-permute-start | bytes 294920 | tf_op jit(solution)/shard_map/ppermute | solution.py:341
  54.2 1.3 %collective-permute-start.1 = (bf16[384,128]{1,0:T(8,128)(2,1)S(1)}, bf16[384,128]{1,0:T(8,128)(2,1)S(1)}, u32[]{:S(2)}, u32[]{:S(2)}) collective-permute-start(bf16[384,128]{1,0:T(8,128)(2,1)S(1)} %get-tuple-element.23), channel_id=1, source_target_pairs={{32,0},{64,32},{96,64},{128,96},{160,128},{192,160},{224,192},{256... | collective-permute-start | bytes 294920 | tf_op jit(solution)/shard_map/ppermute | solution.py:342
  55.5 0.0 copy-done.5
  55.5 0.0 copy-start.4
  55.5 1.4 %copy-done.4 = bf16[5,1152,128]{2,1,0:T(8,128)(2,1)S(1)} copy-done((bf16[5,1152,128]{2,1,0:T(8,128)(2,1)S(1)}, bf16[5,1152,128]{2,1,0:T(8,128)(2,1)}, u32[]{:S(2)}) %copy-start.4) | copy-done | bytes 1474584
  56.9 4.1 %shard_map.143.filtered = f32[384,640]{1,0:T(8,128)S(1)} custom-call(bf16[384,640]{1,0:T(8,128)(2,1)S(1)} %get-tuple-element.19.moved, bf16[384,384]{1,0:T(8,128)(2,1)S(1)} %copy-done.5, f32[9,384,128]{2,1,0:T(8,128)S(1)} %get-tuple-element.20.spread, bf16[5,1152,128]{2,1,0:T(8,128)(2,1)S(1)} %copy-done.4), custom_call_target="tpu_custom_call" | custom-call | flops 800000000 | bytes 5000000 | tf_op jit(solution)/shard_map/pallas_call | solution.py:344
  61.0 0.0 collective-permute-done.before
  61.0 0.0 collective-permute-done.1.after
  61.0 0.0 copy-done.1
  61.0 0.0 copy-done.9
  61.0 2.6 %shard_map.144.answer = bf16[32,64,128]{2,1,0:T(8,128)(2,1)S(1)} custom-call(f32[384,640]{1,0:T(8,128)S(1)} %shard_map.143.filtered, bf16[384,128]{1,0:T(8,128)(2,1)S(1)} %collective-permute-done.before, bf16[384,128]{1,0:T(8,128)(2,1)S(1)} %collective-permute-done.1.after, bf16[384,384]{1,0:T(8,128)(2,1)S(1)} %copy-done.5, bf16[384,384]{1,0:T(8,128)(2,1)S(1)} %copy-done.9, ...), custom_call_target="tpu_custom_call" | custom-call | flops 1500000000 | bytes 7000000 | tf_op jit(solution)/shard_map/pallas_call | solution.py:361
  63.6 0.0 copy-start.2
  63.6 0.8 copy-done.2
  64.5 9.2 %reduce-scatter.2.cloned.1.call-done.column = bf16[1,2,40,1280]{3,2,1,0:T(8,128)(2,1)} async-done(((bf16[8,2,40,1280]{3,2,1,0:T(8,128)(2,1)}), bf16[1,2,40,1280]{3,2,1,0:T(8,128)(2,1)}) %reduce-scatter.2.cloned.1.call-update) | async-done | bytes 204816 | tf_op jit(solution)/shard_map/reduce_scatter | solution.py:314
  73.7 2.2 %shard_map.145 = bf16[32,104,128]{2,1,0:T(8,128)(2,1)} custom-call(bf16[32,64,128]{2,1,0:T(8,128)(2,1)} %copy-done.2, bf16[1,2,40,1280]{3,2,1,0:T(8,128)(2,1)} %reduce-scatter.2.cloned.1.call-done.column), custom_call_target="tpu_custom_call" | custom-call | flops 1000000 | bytes 2000000 | tf_op jit(solution)/shard_map/pallas_call | solution.py:370
  75.9 29.4 %all_to_all.10.slabs = bf16[32,104,128]{2,1,0:T(8,128)(2,1)S(1)} all-to-all(bf16[32,104,128]{2,1,0:T(8,128)(2,1)} %shard_map.145), channel_id=1, replica_groups=mesh['z'=8,'core'=2,'y'=8,'x'=4] {'y','x'}, dimensions={0} | all-to-all | bytes 1703936 | tf_op jit(solution)/shard_map/all_to_all | solution.py:371
  105.3 1.5 %shard_map.146 = (bf16[384,640]{1,0:T(8,128)(2,1)}, f32[40,40]{1,0:T(8,128)}, f32[40,40]{1,0:T(8,128)}) custom-call(bf16[32,104,128]{2,1,0:T(8,128)(2,1)S(1)} %all_to_all.10.slabs, bf16[384,640]{1,0:T(8,128)(2,1)S(1)} %bitcast.17), custom_call_target="tpu_custom_call" | custom-call | flops 100000000 | bytes 2000000 | tf_op jit(solution)/shard_map/pallas_call | solution.py:372
  (8 shorter events, 0.0 us)
Async XLA Ops:
  7.2 66.5 %reduce-scatter.2.cloned.1.call-start = ((), (), s32[]{:S(2)}) async-start(), calls=%async_computation.3 | async-start | bytes 1843200 | tf_op jit(solution)/shard_map/reduce_scatter | solution.py:314
  7.2 1.0 copy-start.6
  8.2 1.0 copy-start.11
  9.3 9.7 %copy-start.7 = (bf16[32,12,640]{2,0,1:T(8,128)(2,1)S(1)}, bf16[32,12,640]{2,0,1:T(8,128)(2,1)}, u32[]{:S(2)}) copy-start(bf16[32,12,640]{2,0,1:T(8,128)(2,1)} %param.13) | copy-start | bytes 1474564
  9.3 9.7 %copy-start.10 = (bf16[640,1280]{1,0:T(8,128)(2,1)S(1)}, bf16[640,1280]{1,0:T(8,128)(2,1)}, u32[]{:S(2)}) copy-start(bf16[640,1280]{1,0:T(8,128)(2,1)} %w_in.3) | copy-start | bytes 4915204
  17.1 5.9 %collective-permute-start.2 = (bf16[8,2,40,1280]{3,2,1,0:T(8,128)(2,1)S(1)}, bf16[8,2,40,1280]{3,2,1,0:T(8,128)(2,1)S(1)}, u32[]{:S(2)}, u32[]{:S(2)}) collective-permute-start(bf16[8,2,40,1280]{3,2,1,0:T(8,128)(2,1)S(1)} %get-tuple-element.27), channel_id=1, source_target_pairs={{0,32},{32,0},{1,33},{33,1},{2,34},{34,2},{3,35},{35,3},{4,36},{36... | collective-permute-start | bytes 4915208 | tf_op jit(solution)/shard_map/ppermute | solution.py:292
  24.6 10.5 %copy-start.13 = (f32[9,640]{1,0:T(8,128)S(1)}, f32[9,640]{1,0:T(8,128)}, u32[]{:S(2)}) copy-start(f32[9,640]{1,0:T(8,128)} %chan.1) | copy-start | bytes 69124
  24.6 10.5 %copy-start.14 = (s32[512,9]{0,1:T(8,128)S(1)}, s32[512,9]{0,1:T(8,128)}, u32[]{:S(2)}) copy-start(s32[512,9]{0,1:T(8,128)} %param.19) | copy-start | bytes 55300
  24.6 10.5 %copy-start.15 = (f32[9,384]{1,0:T(8,128)S(1)}, f32[9,384]{1,0:T(8,128)}, u32[]{:S(2)}) copy-start(f32[9,384]{1,0:T(8,128)} %basis.1) | copy-start | bytes 41476
  24.6 10.5 %copy-start.16 = (s32[512]{0:T(512)S(1)}, s32[512]{0:T(512)}, u32[]{:S(2)}) copy-start(s32[512]{0:T(512)} %param.20) | copy-start | bytes 6148
  24.6 27.9 %all-to-all-start = ((bf16[32,64,128]{2,1,0:T(8,128)(2,1)}), bf16[32,64,128]{2,1,0:T(8,128)(2,1)S(1)}, u32[]{:S(2)}, u32[]{:S(2)}) async-start(bf16[32,64,128]{2,1,0:T(8,128)(2,1)} %shard_map.140), calls=%async_computation | async-start | bytes 1048576 | tf_op jit(solution)/shard_map/all_to_all | solution.py:310
  35.1 1.0 copy-start.12
  36.1 16.4 %copy-start.8 = (bf16[640,256]{1,0:T(8,128)(2,1)S(1)}, bf16[640,256]{1,0:T(8,128)(2,1)}, u32[]{:S(2)}) copy-start(bf16[640,256]{1,0:T(8,128)(2,1)} %constant.33.clone.pick) | copy-start | bytes 983044
  36.1 19.4 %copy-start.5 = (bf16[384,384]{1,0:T(8,128)(2,1)S(1)}, bf16[384,384]{1,0:T(8,128)(2,1)}, u32[]{:S(2)}) copy-start(bf16[384,384]{1,0:T(8,128)(2,1)} %constant.31.clone.forward) | copy-start | bytes 884740
  39.4 1.6 %copy-start = (bf16[2304,640]{1,0:T(8,128)(2,1)}, bf16[2304,640]{1,0:T(8,128)(2,1)S(1)}, u32[]{:S(2)}) copy-start(bf16[2304,640]{1,0:T(8,128)(2,1)S(1)} %get-tuple-element.24.rim_mix) | copy-start | bytes 8847364
  41.0 1.1 copy-start.3
  52.9 8.1 %collective-permute-start = (bf16[384,128]{1,0:T(8,128)(2,1)S(1)}, bf16[384,128]{1,0:T(8,128)(2,1)S(1)}, u32[]{:S(2)}, u32[]{:S(2)}) collective-permute-start(bf16[384,128]{1,0:T(8,128)(2,1)S(1)} %get-tuple-element.22), channel_id=1, source_target_pairs={{0,32},{32,64},{64,96},{96,128},{128,160},{160,192},{192,224},{224... | collective-permute-start | bytes 294920 | tf_op jit(solution)/shard_map/ppermute | solution.py:341
  54.2 6.8 %collective-permute-start.1 = (bf16[384,128]{1,0:T(8,128)(2,1)S(1)}, bf16[384,128]{1,0:T(8,128)(2,1)S(1)}, u32[]{:S(2)}, u32[]{:S(2)}) collective-permute-start(bf16[384,128]{1,0:T(8,128)(2,1)S(1)} %get-tuple-element.23), channel_id=1, source_target_pairs={{32,0},{64,32},{96,64},{128,96},{160,128},{192,160},{224,192},{256... | collective-permute-start | bytes 294920 | tf_op jit(solution)/shard_map/ppermute | solution.py:342
  55.5 1.4 %copy-start.4 = (bf16[5,1152,128]{2,1,0:T(8,128)(2,1)S(1)}, bf16[5,1152,128]{2,1,0:T(8,128)(2,1)}, u32[]{:S(2)}) copy-start(bf16[5,1152,128]{2,1,0:T(8,128)(2,1)} %copy-done.3) | copy-start | bytes 4423684
  56.9 4.1 %copy-start.1 = (bf16[2304,640]{1,0:T(8,128)(2,1)S(1)}, bf16[2304,640]{1,0:T(8,128)(2,1)}, u32[]{:S(2)}) copy-start(bf16[2304,640]{1,0:T(8,128)(2,1)} %copy-done) | copy-start | bytes 8847364
  56.9 4.1 %copy-start.9 = (bf16[384,384]{1,0:T(8,128)(2,1)S(1)}, bf16[384,384]{1,0:T(8,128)(2,1)}, u32[]{:S(2)}) copy-start(bf16[384,384]{1,0:T(8,128)(2,1)} %constant.32.clone.inverse) | copy-start | bytes 884740
  63.6 0.8 copy-start.2
Sparse Core Ops, SparseCore 0:
  24.7 48.8 reduce-scatter.1

commit v5 on v4

--- a/solution.py
+++ b/solution.py
@@ -184,14 +184,30 @@
     to_slabs(tall, send)
 
 
-def merge_kernel(answer, column, out):
+def merge_kernel(answer, column, out, piece, sem):
     rows = column[0, 0].astype(f32), column[0, 1].astype(f32)
-    fill = jnp.zeros((-(2 * rows[0].shape[0]) % 128, rows[0].shape[1]), f32)
+    filled = 2 * rows[0].shape[0]
+    fill = jnp.zeros((-filled % 128, rows[0].shape[1]), f32)
     turned = jnp.concatenate([rows[0], rows[1], fill], 0).T
+    lane = lax.broadcasted_iota(jnp.int32, (8, 128), 1)
     for d in range(PEERS):
-        out[d, :PAD] = answer[d]
-        for i in range(turned.shape[1] // 128):
-            out[d, PAD + 40 * i : PAD + 40 * (i + 1)] = turned[40 * d : 40 * (d + 1), 128 * i : 128 * (i + 1)].astype(bf16)
+        own = turned[40 * d : 40 * (d + 1)]
+        if filled == 80:
+            end = own[32:]
+            piece[d] = jnp.concatenate(
+                [
+                    own[:8] + pltpu.roll(jnp.where(lane < 48, end, 0.0), 80, 1),
+                    own[8:16] + pltpu.roll(jnp.where(lane < 48, 0.0, end), 32, 1),
+                    own[16:32],
+                ],
+                0,
+            ).astype(bf16)
+        else:
+            for i in range(turned.shape[1] // 128):
+                piece[d, 40 * i : 40 * (i + 1)] = own[:, 128 * i : 128 * (i + 1)].astype(bf16)
+    copy = pltpu.make_async_copy(piece, out.at[:, PAD : PAD + piece.shape[1]], sem)
+    copy.start()
+    copy.wait()
 
 
 def final_kernel(slabs, cot, out, grad_in, grad_out, tall):
@@ -209,7 +225,11 @@
     total = slabs[0, PAD:].astype(f32)
     for d in range(1, PEERS):
         total = total + slabs[d, PAD:].astype(f32)
-    if total.shape[0] > 40:
+    if total.shape[0] == 32:
+        lane = lax.broadcasted_iota(jnp.int32, (8, 128), 1)
+        end = jnp.where(lane < 48, pltpu.roll(total[:8], 48, 1), pltpu.roll(total[8:16], 96, 1))
+        total = jnp.concatenate([total, end], 0)
+    elif total.shape[0] > 40:
         total = jnp.concatenate([total[i : i + 40] for i in range(0, total.shape[0], 40)], 1)
     lanes = total.shape[1]
     filled = jnp.concatenate([total, jnp.zeros((128 - 40, lanes), f32)], 0)
@@ -241,6 +261,7 @@
 
 VMEM = pl.BlockSpec(memory_space=pltpu.VMEM)
 TOKEN = shape(8, 128, dtype=f32)
+ANY = pl.BlockSpec(memory_space=pl.ANY)
 SMEM = pl.BlockSpec(memory_space=pltpu.SMEM)
 
 
@@ -248,7 +269,7 @@
     options = dict(grid)
     if "grid" not in options:
         options["in_specs"] = ins
-        options["out_specs"] = jax.tree.map(lambda _: VMEM, out)
+        options.setdefault("out_specs", jax.tree.map(lambda _: VMEM, out))
     return pl.pallas_call(
         kernel,
         out_shape=out,
@@ -270,24 +291,24 @@
     whole = lambda *dims: pl.BlockSpec(dims, lambda i: (0,) * len(dims))
 
     half = shape(depth, 2, part, 1280)
-    half_spec = pl.BlockSpec((depth, 2, part, 256), lambda i: (0, 0, 0, i))
+    half_spec = pl.BlockSpec((depth, 2, part, 640), lambda i: (0, 0, 0, i))
     pre_grad, mine, theirs = call(
         head_kernel,
         (shape(tokens_n, 1280), half, half),
         None,
         3e9,
         8e6,
-        [pltpu.VMEM((640, tokens_n), bf16), pltpu.VMEM((640, tokens_n), bf16), pltpu.VMEM((2, 640, 256), f32)],
+        [pltpu.VMEM((640, tokens_n), bf16), pltpu.VMEM((640, tokens_n), bf16), pltpu.VMEM((2, 640, 640), f32)],
         limit=48,
-        grid=(5,),
+        grid=(2,),
         in_specs=[
             SMEM,
             whole(tokens_n, 640),
             whole(tokens_n, 640),
-            pl.BlockSpec((640, 256), lambda i: (0, i)),
-            pl.BlockSpec((256, 640), lambda i: (i, 0)),
+            pl.BlockSpec((640, 640), lambda i: (0, i)),
+            pl.BlockSpec((640, 640), lambda i: (i, 0)),
         ],
-        out_specs=[pl.BlockSpec((tokens_n, 256), lambda i: (0, i)), half_spec, half_spec],
+        out_specs=[pl.BlockSpec((tokens_n, 640), lambda i: (0, i)), half_spec, half_spec],
     )(core.reshape(1), tokens, cotangent, w_in, w_out)
     partner = lax.ppermute(theirs, "core", [(0, 1), (1, 0)])
 
@@ -358,16 +379,28 @@
         out_specs=pl.BlockSpec((NLON, 128), lambda j: (0, j)),
     )(moved, forward, spread, own_mix)
 
+    extra = 32 if part == 40 else 40 * -(-2 * part // 128)
     answer = call(
         close_kernel,
-        shape(PEERS, PAD, 128),
-        [VMEM] * 7,
+        shape(PEERS, PAD + extra, 128),
+        None,
         1.5e9,
         7e6,
         [pltpu.VMEM((NLON, NB * 256), bf16), pltpu.VMEM((TALL, 128), f32)],
+        grid=(1,),
+        in_specs=[VMEM] * 7,
+        out_specs=whole(PEERS, PAD, 128),
     )(filtered, before, after, forward, inverse, spread, rim_mix)
-    tall = PAD + 40 * -(-2 * part // 128)
-    merged = call(merge_kernel, shape(PEERS, tall, 128), [VMEM] * 2, 1e6, 2e6, limit=62)(answer, column)
+    merged = call(
+        merge_kernel,
+        shape(PEERS, PAD + extra, 128),
+        [ANY, VMEM],
+        1e6,
+        2e6,
+        [pltpu.VMEM((PEERS, extra, 128), bf16), pltpu.SemaphoreType.DMA],
+        out_specs=ANY,
+        input_output_aliases={0: 0},
+    )(answer, column)
     returned = lax.all_to_all(merged, LON, split_axis=0, concat_axis=0, tiled=True)
     grid_grad, grad_in, grad_out = call(
         final_kernel,

time: 114 us -> 111 us (0.974)
  Pallas kernels: 25.9 us -> 22.8 us
  blocking collectives: 29.4 us -> 27.6 us
    pallas_call x2, Pallas kernels: 4.8 us -> 2.74 us  [the longest x1 2.47 us: body(): call(close_kernel, shape(PEERS, PAD + extra, 128), None, 1500000000.0, 70...]
    all_to_all x1, blocking collectives: 29.4 us -> 27.6 us  [body(): lax.all_to_all(merged, LON, split_axis=0, concat_axis=0, tiled=True)]
where the time goes in v5:
time: 111 us; the launch traced here: 110 us
  blocking collectives  27.6 us (25%)
  Pallas kernels  22.8 us (21%)
  waiting for transfers between devices  19.7 us (18%)
  starting transfers between devices  14.9 us (13%)
  between operations  14.2 us (13%)
  local copies, waits for them, and re-layouts  9.03 us (8%)
  other arithmetic  1.68 us (2%)
    all_to_all x1, blocking collectives, body(): lax.all_to_all(merged, LON, split_axis=0, concat_axis=0, tiled=True)  27.6 us
    all_to_all x1, starting transfers between devices, body(): lax.all_to_all(send, LON, split_axis=0, concat_axis=0, tiled=True)  10.4 us
    all_to_all x1, waiting for transfers between devices, body(): lax.all_to_all(send, LON, split_axis=0, concat_axis=0, tiled=True)  10.3 us
    reduce_scatter x1, waiting for transfers between devices, body(): column = lax.psum_scatter(chip, 'z', scatter_dimension=0, tiled=True)  9.37 us
    unnamed x34, local copies, waits for them, and re-layouts  9.03 us
    pallas_call x1, Pallas kernels, body(): call(head_kernel, (shape(tokens_n, 1280), half, half), None, 3000000000.0...  6.93 us
    pallas_call x1, Pallas kernels, body(): call(lift_kernel, shape(PEERS, PAD, 128), None, 2000000000.0, 4000000.0,...  3.99 us
    pallas_call x1, Pallas kernels, body(): call(own_kernel, shape(NLON, 640, dtype=f32), None, 800000000.0, 5000000....  3.89 us
  transfers between devices with their start and end apart: 5, of which 2 were waited for; matrix products, arithmetic and copies ran while one was open for 0% of the time, Pallas kernels for 13%

profile of v5, /device:TPU:2, one launch (start us, length us, event | category | flops | bytes accessed | tf_op | source)
XLA Modules:
  0.0 110.0 jit_solution(14915852729708021272)
XLA Ops:
  7.2 0.0 reduce-scatter.2.cloned.1.call-start
  7.2 0.0 copy-start.5
  7.2 1.0 copy-done.5
  8.2 0.0 copy-start.11
  8.2 1.0 copy-done.11
  9.3 0.0 copy-start.6
  9.3 0.0 copy-start.10
  9.3 6.9 %shard_map.139 = (bf16[384,1280]{1,0:T(8,128)(2,1)S(1)}, bf16[8,2,40,1280]{3,2,1,0:T(8,128)(2,1)S(1)}, bf16[8,2,40,1280]{3,2,1,0:T(8,128)(2,1)S(1)}) custom-call(s32[1]{0:T(128)} %bitcast.core, bf16[384,640]{1,0:T(8,128)(2,1)S(1)} %bitcast.18, bf16[384,640]{1,0:T(8,128)(2,1)S(1)} %bitcast.15, bf16[640,1280]{1,0:T(8,128)(2,1)} %w_in.3, bf16[1280,640]{1,0:T(8,128)(2,1)} %w_out.1), custom_call_target="tpu_custom_call" | custom-call | flops 3000000000 | bytes 8000000 | tf_op jit(solution)/shard_map/pallas_call | solution.py:295
  16.2 1.9 %collective-permute-start.2 = (bf16[8,2,40,1280]{3,2,1,0:T(8,128)(2,1)S(1)}, bf16[8,2,40,1280]{3,2,1,0:T(8,128)(2,1)S(1)}, u32[]{:S(2)}, u32[]{:S(2)}) collective-permute-start(bf16[8,2,40,1280]{3,2,1,0:T(8,128)(2,1)S(1)} %get-tuple-element.27), channel_id=1, source_target_pairs={{0,32},{32,0},{1,33},{33,1},{2,34},{34,2},{3,35},{35,3},{4,36},{36... | collective-permute-start | bytes 4915208 | tf_op jit(solution)/shard_map/ppermute | solution.py:313
  18.1 0.0 copy-done.6
  18.2 0.0 copy-done.10
  18.2 4.0 %shard_map.140 = bf16[32,64,128]{2,1,0:T(8,128)(2,1)} custom-call(bf16[384,1280]{1,0:T(8,128)(2,1)S(1)} %get-tuple-element.17.pre_grad, bf16[384,640]{1,0:T(8,128)(2,1)S(1)} %bitcast.16, bf16[640,1280]{1,0:T(8,128)(2,1)S(1)} %copy-done.10), custom_call_target="tpu_custom_call" | custom-call | flops 2000000000 | bytes 4000000 | tf_op jit(solution)/shard_map/pallas_call | solution.py:315
  22.2 0.0 collective-permute-done.2
  22.2 1.6 %add_convert_fusion = bf16[8,2,40,1280]{3,2,1,0:T(8,128)(2,1)} fusion(bf16[8,2,40,1280]{3,2,1,0:T(8,128)(2,1)S(1)} %collective-permute-done.2, bf16[8,2,40,1280]{3,2,1,0:T(8,128)(2,1)S(1)} %get-tuple-element.26), kind=kLoop, calls=%fused_computation | loop fusion | flops 3276800 | bytes 4915200 | tf_op jit(solution)/shard_map/convert_element_type | solution.py:334
  23.8 0.0 copy-start.13
  23.8 0.0 copy-start.14
  23.8 0.0 copy-start.15
  23.8 0.0 reduce-scatter.2.cloned.1.call-update
  23.8 10.4 %all-to-all-start = ((bf16[32,64,128]{2,1,0:T(8,128)(2,1)}), bf16[32,64,128]{2,1,0:T(8,128)(2,1)S(1)}, u32[]{:S(2)}, u32[]{:S(2)}) async-start(bf16[32,64,128]{2,1,0:T(8,128)(2,1)} %shard_map.140), calls=%async_computation | async-start | bytes 1048576 | tf_op jit(solution)/shard_map/all_to_all | solution.py:331
  34.2 0.1 pad_add_fusion.place
  34.3 0.0 copy-done.13
  34.3 0.0 copy-done.14
  34.3 0.0 copy-done.15
  34.3 0.0 copy-done.16
  34.3 0.0 copy-start.12
  34.3 1.0 copy-done.12
  35.3 3.4 %shard_map.141 = (bf16[5,1152,128]{2,1,0:T(8,128)(2,1)S(1)}, bf16[2304,640]{1,0:T(8,128)(2,1)S(1)}, f32[9,384,128]{2,1,0:T(8,128)S(1)}, f32[8,128]{1,0:T(8,128)S(1)}) custom-call(s32[2]{0:T(128)S(1)} %pad_add_fusion.place, f32[9,9,512]{2,1,0:T(8,128)S(1)} %bitcast.19, s32[9,512]{1,0:T(8,128)S(1)} %bitcast.20, s32[1,512]{1,0:T(1,128)S(1)} %bitcast.21, ...), custom_call_target="tpu_custom_call" | custom-call | flops 1000000000 | bytes 6000000 | tf_op jit(solution)/shard_map/pallas_call | solution.py:337
  38.6 1.6 %copy-done = bf16[2304,640]{1,0:T(8,128)(2,1)} copy-done((bf16[2304,640]{1,0:T(8,128)(2,1)}, bf16[2304,640]{1,0:T(8,128)(2,1)S(1)}, u32[]{:S(2)}) %copy-start) | copy-done | bytes 2949144
  40.2 1.1 %copy-done.2 = bf16[5,1152,128]{2,1,0:T(8,128)(2,1)} copy-done((bf16[5,1152,128]{2,1,0:T(8,128)(2,1)}, bf16[5,1152,128]{2,1,0:T(8,128)(2,1)S(1)}, u32[]{:S(2)}) %copy-start.2) | copy-done | bytes 1474584
  41.3 10.3 %all-to-all-done.slabs = bf16[32,64,128]{2,1,0:T(8,128)(2,1)S(1)} async-done(((bf16[32,64,128]{2,1,0:T(8,128)(2,1)}), bf16[32,64,128]{2,1,0:T(8,128)(2,1)S(1)}, u32[]{:S(2)}, u32[]{:S(2)}) %all-to-all-start) | async-done | bytes 524320 | tf_op jit(solution)/shard_map/all_to_all | solution.py:331
  51.7 1.0 copy-done.7
  52.7 0.4 shard_map.142
  53.1 1.3 %collective-permute-start = (bf16[384,128]{1,0:T(8,128)(2,1)S(1)}, bf16[384,128]{1,0:T(8,128)(2,1)S(1)}, u32[]{:S(2)}, u32[]{:S(2)}) collective-permute-start(bf16[384,128]{1,0:T(8,128)(2,1)S(1)} %get-tuple-element.22), channel_id=1, source_target_pairs={{0,32},{32,64},{64,96},{96,128},{128,160},{160,192},{192,224},{224... | collective-permute-start | bytes 294920 | tf_op jit(solution)/shard_map/ppermute | solution.py:362
  54.4 1.3 %collective-permute-start.1 = (bf16[384,128]{1,0:T(8,128)(2,1)S(1)}, bf16[384,128]{1,0:T(8,128)(2,1)S(1)}, u32[]{:S(2)}, u32[]{:S(2)}) collective-permute-start(bf16[384,128]{1,0:T(8,128)(2,1)S(1)} %get-tuple-element.23), channel_id=1, source_target_pairs={{32,0},{64,32},{96,64},{128,96},{160,128},{192,160},{224,192},{256... | collective-permute-start | bytes 294920 | tf_op jit(solution)/shard_map/ppermute | solution.py:363
  55.7 0.0 copy-done.4
  55.7 0.0 copy-start.3
  55.7 1.4 %copy-done.3 = bf16[5,1152,128]{2,1,0:T(8,128)(2,1)S(1)} copy-done((bf16[5,1152,128]{2,1,0:T(8,128)(2,1)S(1)}, bf16[5,1152,128]{2,1,0:T(8,128)(2,1)}, u32[]{:S(2)}) %copy-start.3) | copy-done | bytes 1474584
  57.1 3.9 %shard_map.143.filtered = f32[384,640]{1,0:T(8,128)S(1)} custom-call(bf16[384,640]{1,0:T(8,128)(2,1)S(1)} %get-tuple-element.19.moved, bf16[384,384]{1,0:T(8,128)(2,1)S(1)} %copy-done.4, f32[9,384,128]{2,1,0:T(8,128)S(1)} %get-tuple-element.20.spread, bf16[5,1152,128]{2,1,0:T(8,128)(2,1)S(1)} %copy-done.3), custom_call_target="tpu_custom_call" | custom-call | flops 800000000 | bytes 5000000 | tf_op jit(solution)/shard_map/pallas_call | solution.py:365
  61.0 0.0 collective-permute-done.before
  61.0 0.0 collective-permute-done.1.after
  61.0 0.0 copy-done.1
  61.0 0.0 copy-done.8
  61.0 2.5 %shard_map.144.answer = bf16[32,96,128]{2,1,0:T(8,128)(2,1)S(1)} custom-call(f32[384,640]{1,0:T(8,128)S(1)} %shard_map.143.filtered, bf16[384,128]{1,0:T(8,128)(2,1)S(1)} %collective-permute-done.before, bf16[384,128]{1,0:T(8,128)(2,1)S(1)} %collective-permute-done.1.after, bf16[384,384]{1,0:T(8,128)(2,1)S(1)} %copy-done.4, bf16[384,384]{1,0:T(8,128)(2,1)S(1)} %copy-done.8, ...), custom_call_target="tpu_custom_call" | custom-call | flops 1500000000 | bytes 7000000 | tf_op jit(solution)/shard_map/pallas_call | solution.py:383
  63.5 9.4 %reduce-scatter.2.cloned.1.call-done.column = bf16[1,2,40,1280]{3,2,1,0:T(8,128)(2,1)} async-done(((bf16[8,2,40,1280]{3,2,1,0:T(8,128)(2,1)}), bf16[1,2,40,1280]{3,2,1,0:T(8,128)(2,1)}) %reduce-scatter.2.cloned.1.call-update) | async-done | bytes 204816 | tf_op jit(solution)/shard_map/reduce_scatter | solution.py:335
  72.9 0.9 copy-done.9
  73.8 0.3 shard_map.145
  74.1 27.6 %all_to_all.10.slabs = bf16[32,96,128]{2,1,0:T(8,128)(2,1)S(1)} all-to-all(bf16[32,96,128]{2,1,0:T(8,128)(2,1)S(1)} %shard_map.145), channel_id=1, replica_groups=mesh['z'=8,'core'=2,'y'=8,'x'=4] {'y','x'}, dimensions={0} | all-to-all | bytes 1572864 | tf_op jit(solution)/shard_map/all_to_all | solution.py:404
  101.6 1.5 %shard_map.146 = (bf16[384,640]{1,0:T(8,128)(2,1)}, f32[40,40]{1,0:T(8,128)}, f32[40,40]{1,0:T(8,128)}) custom-call(bf16[32,96,128]{2,1,0:T(8,128)(2,1)S(1)} %all_to_all.10.slabs, bf16[384,640]{1,0:T(8,128)(2,1)S(1)} %bitcast.17), custom_call_target="tpu_custom_call" | custom-call | flops 100000000 | bytes 2000000 | tf_op jit(solution)/shard_map/pallas_call | solution.py:405
  (8 shorter events, 0.0 us)
Async XLA Ops:
  7.2 65.7 %reduce-scatter.2.cloned.1.call-start = ((), (), s32[]{:S(2)}) async-start(), calls=%async_computation.3 | async-start | bytes 1843200 | tf_op jit(solution)/shard_map/reduce_scatter | solution.py:335
  7.2 1.0 copy-start.5
  8.2 1.0 copy-start.11
  9.3 8.9 %copy-start.6 = (bf16[32,12,640]{2,0,1:T(8,128)(2,1)S(1)}, bf16[32,12,640]{2,0,1:T(8,128)(2,1)}, u32[]{:S(2)}) copy-start(bf16[32,12,640]{2,0,1:T(8,128)(2,1)} %param.13) | copy-start | bytes 1474564
  9.3 8.9 %copy-start.10 = (bf16[640,1280]{1,0:T(8,128)(2,1)S(1)}, bf16[640,1280]{1,0:T(8,128)(2,1)}, u32[]{:S(2)}) copy-start(bf16[640,1280]{1,0:T(8,128)(2,1)} %w_in.3) | copy-start | bytes 4915204
  16.2 5.9 %collective-permute-start.2 = (bf16[8,2,40,1280]{3,2,1,0:T(8,128)(2,1)S(1)}, bf16[8,2,40,1280]{3,2,1,0:T(8,128)(2,1)S(1)}, u32[]{:S(2)}, u32[]{:S(2)}) collective-permute-start(bf16[8,2,40,1280]{3,2,1,0:T(8,128)(2,1)S(1)} %get-tuple-element.27), channel_id=1, source_target_pairs={{0,32},{32,0},{1,33},{33,1},{2,34},{34,2},{3,35},{35,3},{4,36},{36... | collective-permute-start | bytes 4915208 | tf_op jit(solution)/shard_map/ppermute | solution.py:313
  23.8 10.5 %copy-start.13 = (f32[9,640]{1,0:T(8,128)S(1)}, f32[9,640]{1,0:T(8,128)}, u32[]{:S(2)}) copy-start(f32[9,640]{1,0:T(8,128)} %chan.1) | copy-start | bytes 69124
  23.8 10.5 %copy-start.14 = (s32[512,9]{0,1:T(8,128)S(1)}, s32[512,9]{0,1:T(8,128)}, u32[]{:S(2)}) copy-start(s32[512,9]{0,1:T(8,128)} %param.19) | copy-start | bytes 55300
  23.8 10.5 %copy-start.15 = (f32[9,384]{1,0:T(8,128)S(1)}, f32[9,384]{1,0:T(8,128)}, u32[]{:S(2)}) copy-start(f32[9,384]{1,0:T(8,128)} %basis.1) | copy-start | bytes 41476
  23.8 10.5 %copy-start.16 = (s32[512]{0:T(512)S(1)}, s32[512]{0:T(512)}, u32[]{:S(2)}) copy-start(s32[512]{0:T(512)} %param.20) | copy-start | bytes 6148
  23.8 27.9 %all-to-all-start = ((bf16[32,64,128]{2,1,0:T(8,128)(2,1)}), bf16[32,64,128]{2,1,0:T(8,128)(2,1)S(1)}, u32[]{:S(2)}, u32[]{:S(2)}) async-start(bf16[32,64,128]{2,1,0:T(8,128)(2,1)} %shard_map.140), calls=%async_computation | async-start | bytes 1048576 | tf_op jit(solution)/shard_map/all_to_all | solution.py:331
  34.3 1.0 copy-start.12
  35.3 20.4 %copy-start.4 = (bf16[384,384]{1,0:T(8,128)(2,1)S(1)}, bf16[384,384]{1,0:T(8,128)(2,1)}, u32[]{:S(2)}) copy-start(bf16[384,384]{1,0:T(8,128)(2,1)} %constant.31.clone.forward) | copy-start | bytes 884740
  38.6 1.6 %copy-start = (bf16[2304,640]{1,0:T(8,128)(2,1)}, bf16[2304,640]{1,0:T(8,128)(2,1)S(1)}, u32[]{:S(2)}) copy-start(bf16[2304,640]{1,0:T(8,128)(2,1)S(1)} %get-tuple-element.24.rim_mix) | copy-start | bytes 8847364
  40.2 1.1 %copy-start.2 = (bf16[5,1152,128]{2,1,0:T(8,128)(2,1)}, bf16[5,1152,128]{2,1,0:T(8,128)(2,1)S(1)}, u32[]{:S(2)}) copy-start(bf16[5,1152,128]{2,1,0:T(8,128)(2,1)S(1)} %get-tuple-element.21.own_mix) | copy-start | bytes 4423684
  51.7 1.0 copy-start.7
  53.1 7.9 %collective-permute-start = (bf16[384,128]{1,0:T(8,128)(2,1)S(1)}, bf16[384,128]{1,0:T(8,128)(2,1)S(1)}, u32[]{:S(2)}, u32[]{:S(2)}) collective-permute-start(bf16[384,128]{1,0:T(8,128)(2,1)S(1)} %get-tuple-element.22), channel_id=1, source_target_pairs={{0,32},{32,64},{64,96},{96,128},{128,160},{160,192},{192,224},{224... | collective-permute-start | bytes 294920 | tf_op jit(solution)/shard_map/ppermute | solution.py:362
  54.4 6.6 %collective-permute-start.1 = (bf16[384,128]{1,0:T(8,128)(2,1)S(1)}, bf16[384,128]{1,0:T(8,128)(2,1)S(1)}, u32[]{:S(2)}, u32[]{:S(2)}) collective-permute-start(bf16[384,128]{1,0:T(8,128)(2,1)S(1)} %get-tuple-element.23), channel_id=1, source_target_pairs={{32,0},{64,32},{96,64},{128,96},{160,128},{192,160},{224,192},{256... | collective-permute-start | bytes 294920 | tf_op jit(solution)/shard_map/ppermute | solution.py:363
  55.7 1.4 %copy-start.3 = (bf16[5,1152,128]{2,1,0:T(8,128)(2,1)S(1)}, bf16[5,1152,128]{2,1,0:T(8,128)(2,1)}, u32[]{:S(2)}) copy-start(bf16[5,1152,128]{2,1,0:T(8,128)(2,1)} %copy-done.2) | copy-start | bytes 4423684
  57.1 3.9 %copy-start.1 = (bf16[2304,640]{1,0:T(8,128)(2,1)S(1)}, bf16[2304,640]{1,0:T(8,128)(2,1)}, u32[]{:S(2)}) copy-start(bf16[2304,640]{1,0:T(8,128)(2,1)} %copy-done) | copy-start | bytes 8847364
  57.1 3.9 %copy-start.8 = (bf16[384,384]{1,0:T(8,128)(2,1)S(1)}, bf16[384,384]{1,0:T(8,128)(2,1)}, u32[]{:S(2)}) copy-start(bf16[384,384]{1,0:T(8,128)(2,1)} %constant.32.clone.inverse) | copy-start | bytes 884740
  72.9 0.9 copy-start.9
Sparse Core Ops, SparseCore 0:
  23.9 48.8 reduce-scatter.1

commit v6 on v5

--- a/solution.py
+++ b/solution.py
@@ -294,12 +294,12 @@
     half_spec = pl.BlockSpec((depth, 2, part, 640), lambda i: (0, 0, 0, i))
     pre_grad, mine, theirs = call(
         head_kernel,
-        (shape(tokens_n, 1280), half, half),
+        (pltpu.VMEM((tokens_n, 1280), bf16), pltpu.VMEM(half.shape, bf16), pltpu.VMEM(half.shape, bf16)),
         None,
         3e9,
         8e6,
         [pltpu.VMEM((640, tokens_n), bf16), pltpu.VMEM((640, tokens_n), bf16), pltpu.VMEM((2, 640, 640), f32)],
-        limit=48,
+        limit=56,
         grid=(2,),
         in_specs=[
             SMEM,

time: 111 us -> 109 us (0.982)
  local copies, waits for them, and re-layouts: 9.03 us -> 6.98 us
    unnamed x34 -> x30, local copies, waits for them, and re-layouts: 9.03 us -> 6.98 us
where the time goes in v6:
time: 109 us; the launch traced here: 108 us
  blocking collectives  27.8 us (26%)
  Pallas kernels  23 us (21%)
  waiting for transfers between devices  19.8 us (18%)
  starting transfers between devices  14.9 us (14%)
  between operations  14.2 us (13%)
  local copies, waits for them, and re-layouts  6.98 us (6%)
  other arithmetic  1.64 us (2%)
    all_to_all x1, blocking collectives, body(): lax.all_to_all(merged, LON, split_axis=0, concat_axis=0, tiled=True)  27.8 us
    all_to_all x1, starting transfers between devices, body(): lax.all_to_all(send, LON, split_axis=0, concat_axis=0, tiled=True)  10.4 us
    all_to_all x1, waiting for transfers between devices, body(): lax.all_to_all(send, LON, split_axis=0, concat_axis=0, tiled=True)  10.4 us
    reduce_scatter x1, waiting for transfers between devices, body(): column = lax.psum_scatter(chip, 'z', scatter_dimension=0, tiled=True)  9.43 us
    pallas_call x1, Pallas kernels, body(): call(head_kernel, (pltpu.VMEM((tokens_n, 1280), bf16), pltpu.VMEM(half.sh...  7.12 us
    unnamed x30, local copies, waits for them, and re-layouts  6.98 us
    pallas_call x1, Pallas kernels, body(): call(lift_kernel, shape(PEERS, PAD, 128), None, 2000000000.0, 4000000.0,...  4 us
    pallas_call x1, Pallas kernels, body(): call(own_kernel, shape(NLON, 640, dtype=f32), None, 800000000.0, 5000000....  3.9 us
  transfers between devices with their start and end apart: 5, of which 2 were waited for; matrix products, arithmetic and copies ran while one was open for 0% of the time, Pallas kernels for 13%

profile of v6, /device:TPU:2, one launch (start us, length us, event | category | flops | bytes accessed | tf_op | source)
XLA Modules:
  0.0 108.3 jit_solution(17558600779265363126)
XLA Ops:
  7.2 0.0 reduce-scatter.2.cloned.1.call-start
  7.2 0.0 copy-start.5
  7.2 0.0 copy-start.9
  7.2 7.1 %shard_map.139 = (bf16[384,1280]{1,0:T(8,128)(2,1)S(1)}, bf16[8,2,40,1280]{3,2,1,0:T(8,128)(2,1)S(1)}, bf16[8,2,40,1280]{3,2,1,0:T(8,128)(2,1)S(1)}) custom-call(s32[1]{0:T(128)} %bitcast.core, bf16[384,640]{1,0:T(8,128)(2,1)} %bitcast.21, bf16[384,640]{1,0:T(8,128)(2,1)} %bitcast.15, bf16[640,1280]{1,0:T(8,128)(2,1)} %w_in.3, bf16[1280,640]{1,0:T(8,128)(2,1)} %w_out.1), custom_call_target="tpu_custom_call" | custom-call | flops 3000000000 | bytes 8000000 | tf_op jit(solution)/shard_map/pallas_call | solution.py:295
  14.4 1.9 %collective-permute-start.2 = (bf16[8,2,40,1280]{3,2,1,0:T(8,128)(2,1)S(1)}, bf16[8,2,40,1280]{3,2,1,0:T(8,128)(2,1)S(1)}, u32[]{:S(2)}, u32[]{:S(2)}) collective-permute-start(bf16[8,2,40,1280]{3,2,1,0:T(8,128)(2,1)S(1)} %get-tuple-element.27), channel_id=1, source_target_pairs={{0,32},{32,0},{1,33},{33,1},{2,34},{34,2},{3,35},{35,3},{4,36},{36... | collective-permute-start | bytes 4915208 | tf_op jit(solution)/shard_map/ppermute | solution.py:313
  16.3 0.0 copy-done.5
  16.3 0.0 copy-done.9
  16.3 4.0 %shard_map.140 = bf16[32,64,128]{2,1,0:T(8,128)(2,1)} custom-call(bf16[384,1280]{1,0:T(8,128)(2,1)S(1)} %get-tuple-element.17.pre_grad, bf16[384,640]{1,0:T(8,128)(2,1)S(1)} %bitcast.16, bf16[640,1280]{1,0:T(8,128)(2,1)S(1)} %copy-done.9), custom_call_target="tpu_custom_call" | custom-call | flops 2000000000 | bytes 4000000 | tf_op jit(solution)/shard_map/pallas_call | solution.py:315
  20.3 0.0 collective-permute-done.2
  20.3 1.6 %add_convert_fusion = bf16[8,2,40,1280]{3,2,1,0:T(8,128)(2,1)} fusion(bf16[8,2,40,1280]{3,2,1,0:T(8,128)(2,1)S(1)} %collective-permute-done.2, bf16[8,2,40,1280]{3,2,1,0:T(8,128)(2,1)S(1)} %get-tuple-element.26), kind=kLoop, calls=%fused_computation | loop fusion | flops 3276800 | bytes 4915200 | tf_op jit(solution)/shard_map/convert_element_type | solution.py:334
  21.9 0.0 copy-start.11
  21.9 0.0 copy-start.12
  21.9 0.0 copy-start.14
  21.9 0.0 reduce-scatter.2.cloned.1.call-update
  21.9 10.4 %all-to-all-start = ((bf16[32,64,128]{2,1,0:T(8,128)(2,1)}), bf16[32,64,128]{2,1,0:T(8,128)(2,1)S(1)}, u32[]{:S(2)}, u32[]{:S(2)}) async-start(bf16[32,64,128]{2,1,0:T(8,128)(2,1)} %shard_map.140), calls=%async_computation | async-start | bytes 1048576 | tf_op jit(solution)/shard_map/all_to_all | solution.py:331
  32.3 0.1 pad_add_fusion.place
  32.4 0.0 copy-done.11
  32.4 0.0 copy-done.12
  32.4 0.0 copy-done.13
  32.4 0.0 copy-done.14
  32.4 0.0 copy-start.10
  32.4 1.0 copy-done.10
  33.4 0.0 copy-start.4
  33.4 3.4 %shard_map.141 = (bf16[5,1152,128]{2,1,0:T(8,128)(2,1)S(1)}, bf16[2304,640]{1,0:T(8,128)(2,1)S(1)}, f32[9,384,128]{2,1,0:T(8,128)S(1)}, f32[8,128]{1,0:T(8,128)S(1)}) custom-call(s32[2]{0:T(128)S(1)} %pad_add_fusion.place, f32[9,9,512]{2,1,0:T(8,128)S(1)} %bitcast.18, s32[9,512]{1,0:T(8,128)S(1)} %bitcast.19, s32[1,512]{1,0:T(1,128)S(1)} %bitcast.20, ...), custom_call_target="tpu_custom_call" | custom-call | flops 1000000000 | bytes 6000000 | tf_op jit(solution)/shard_map/pallas_call | solution.py:337
  36.7 0.0 copy-start
  36.7 1.6 %copy-done = bf16[2304,640]{1,0:T(8,128)(2,1)} copy-done((bf16[2304,640]{1,0:T(8,128)(2,1)}, bf16[2304,640]{1,0:T(8,128)(2,1)S(1)}, u32[]{:S(2)}) %copy-start) | copy-done | bytes 2949144
  38.3 0.0 copy-start.2
  38.3 1.1 %copy-done.2 = bf16[5,1152,128]{2,1,0:T(8,128)(2,1)} copy-done((bf16[5,1152,128]{2,1,0:T(8,128)(2,1)}, bf16[5,1152,128]{2,1,0:T(8,128)(2,1)S(1)}, u32[]{:S(2)}) %copy-start.2) | copy-done | bytes 1474584
  39.5 10.4 %all-to-all-done.slabs = bf16[32,64,128]{2,1,0:T(8,128)(2,1)S(1)} async-done(((bf16[32,64,128]{2,1,0:T(8,128)(2,1)}), bf16[32,64,128]{2,1,0:T(8,128)(2,1)S(1)}, u32[]{:S(2)}, u32[]{:S(2)}) %all-to-all-start) | async-done | bytes 524320 | tf_op jit(solution)/shard_map/all_to_all | solution.py:331
  49.8 0.0 copy-start.6
  49.8 1.0 copy-done.6
  50.8 0.4 shard_map.142
  51.2 1.3 %collective-permute-start = (bf16[384,128]{1,0:T(8,128)(2,1)S(1)}, bf16[384,128]{1,0:T(8,128)(2,1)S(1)}, u32[]{:S(2)}, u32[]{:S(2)}) collective-permute-start(bf16[384,128]{1,0:T(8,128)(2,1)S(1)} %get-tuple-element.22), channel_id=1, source_target_pairs={{0,32},{32,64},{64,96},{96,128},{128,160},{160,192},{192,224},{224... | collective-permute-start | bytes 294920 | tf_op jit(solution)/shard_map/ppermute | solution.py:362
  52.5 1.3 %collective-permute-start.1 = (bf16[384,128]{1,0:T(8,128)(2,1)S(1)}, bf16[384,128]{1,0:T(8,128)(2,1)S(1)}, u32[]{:S(2)}, u32[]{:S(2)}) collective-permute-start(bf16[384,128]{1,0:T(8,128)(2,1)S(1)} %get-tuple-element.23), channel_id=1, source_target_pairs={{32,0},{64,32},{96,64},{128,96},{160,128},{192,160},{224,192},{256... | collective-permute-start | bytes 294920 | tf_op jit(solution)/shard_map/ppermute | solution.py:363
  53.8 0.0 copy-done.4
  53.8 0.0 copy-start.3
  53.8 1.4 %copy-done.3 = bf16[5,1152,128]{2,1,0:T(8,128)(2,1)S(1)} copy-done((bf16[5,1152,128]{2,1,0:T(8,128)(2,1)S(1)}, bf16[5,1152,128]{2,1,0:T(8,128)(2,1)}, u32[]{:S(2)}) %copy-start.3) | copy-done | bytes 1474584
  55.2 3.9 %shard_map.143.filtered = f32[384,640]{1,0:T(8,128)S(1)} custom-call(bf16[384,640]{1,0:T(8,128)(2,1)S(1)} %get-tuple-element.19.moved, bf16[384,384]{1,0:T(8,128)(2,1)S(1)} %copy-done.4, f32[9,384,128]{2,1,0:T(8,128)S(1)} %get-tuple-element.20.spread, bf16[5,1152,128]{2,1,0:T(8,128)(2,1)S(1)} %copy-done.3), custom_call_target="tpu_custom_call" | custom-call | flops 800000000 | bytes 5000000 | tf_op jit(solution)/shard_map/pallas_call | solution.py:365
  59.1 0.0 collective-permute-done.before
  59.1 0.0 collective-permute-done.1.after
  59.1 0.0 copy-done.1
  59.1 0.0 copy-done.7
  59.1 2.5 %shard_map.144.answer = bf16[32,96,128]{2,1,0:T(8,128)(2,1)S(1)} custom-call(f32[384,640]{1,0:T(8,128)S(1)} %shard_map.143.filtered, bf16[384,128]{1,0:T(8,128)(2,1)S(1)} %collective-permute-done.before, bf16[384,128]{1,0:T(8,128)(2,1)S(1)} %collective-permute-done.1.after, bf16[384,384]{1,0:T(8,128)(2,1)S(1)} %copy-done.4, bf16[384,384]{1,0:T(8,128)(2,1)S(1)} %copy-done.7, ...), custom_call_target="tpu_custom_call" | custom-call | flops 1500000000 | bytes 7000000 | tf_op jit(solution)/shard_map/pallas_call | solution.py:383
  61.6 9.4 %reduce-scatter.2.cloned.1.call-done.column = bf16[1,2,40,1280]{3,2,1,0:T(8,128)(2,1)} async-done(((bf16[8,2,40,1280]{3,2,1,0:T(8,128)(2,1)}), bf16[1,2,40,1280]{3,2,1,0:T(8,128)(2,1)}) %reduce-scatter.2.cloned.1.call-update) | async-done | bytes 204816 | tf_op jit(solution)/shard_map/reduce_scatter | solution.py:335
  71.0 0.9 copy-done.8
  72.0 0.3 shard_map.145
  72.2 27.8 %all_to_all.10.slabs = bf16[32,96,128]{2,1,0:T(8,128)(2,1)S(1)} all-to-all(bf16[32,96,128]{2,1,0:T(8,128)(2,1)S(1)} %shard_map.145), channel_id=1, replica_groups=mesh['z'=8,'core'=2,'y'=8,'x'=4] {'y','x'}, dimensions={0} | all-to-all | bytes 1572864 | tf_op jit(solution)/shard_map/all_to_all | solution.py:404
  100.0 1.5 %shard_map.146 = (bf16[384,640]{1,0:T(8,128)(2,1)}, f32[40,40]{1,0:T(8,128)}, f32[40,40]{1,0:T(8,128)}) custom-call(bf16[32,96,128]{2,1,0:T(8,128)(2,1)S(1)} %all_to_all.10.slabs, bf16[384,640]{1,0:T(8,128)(2,1)S(1)} %bitcast.17), custom_call_target="tpu_custom_call" | custom-call | flops 100000000 | bytes 2000000 | tf_op jit(solution)/shard_map/pallas_call | solution.py:405
  (4 shorter events, 0.0 us)
Async XLA Ops:
  7.2 63.9 %reduce-scatter.2.cloned.1.call-start = ((), (), s32[]{:S(2)}) async-start(), calls=%async_computation.3 | async-start | bytes 1843200 | tf_op jit(solution)/shard_map/reduce_scatter | solution.py:335
  7.2 9.1 %copy-start.5 = (bf16[32,12,640]{2,0,1:T(8,128)(2,1)S(1)}, bf16[32,12,640]{2,0,1:T(8,128)(2,1)}, u32[]{:S(2)}) copy-start(bf16[32,12,640]{2,0,1:T(8,128)(2,1)} %param.13) | copy-start | bytes 1474564
  7.2 9.1 %copy-start.9 = (bf16[640,1280]{1,0:T(8,128)(2,1)S(1)}, bf16[640,1280]{1,0:T(8,128)(2,1)}, u32[]{:S(2)}) copy-start(bf16[640,1280]{1,0:T(8,128)(2,1)} %w_in.3) | copy-start | bytes 4915204
  14.4 5.9 %collective-permute-start.2 = (bf16[8,2,40,1280]{3,2,1,0:T(8,128)(2,1)S(1)}, bf16[8,2,40,1280]{3,2,1,0:T(8,128)(2,1)S(1)}, u32[]{:S(2)}, u32[]{:S(2)}) collective-permute-start(bf16[8,2,40,1280]{3,2,1,0:T(8,128)(2,1)S(1)} %get-tuple-element.27), channel_id=1, source_target_pairs={{0,32},{32,0},{1,33},{33,1},{2,34},{34,2},{3,35},{35,3},{4,36},{36... | collective-permute-start | bytes 4915208 | tf_op jit(solution)/shard_map/ppermute | solution.py:313
  21.9 10.5 %copy-start.11 = (f32[9,640]{1,0:T(8,128)S(1)}, f32[9,640]{1,0:T(8,128)}, u32[]{:S(2)}) copy-start(f32[9,640]{1,0:T(8,128)} %chan.1) | copy-start | bytes 69124
  21.9 10.5 %copy-start.12 = (s32[512,9]{0,1:T(8,128)S(1)}, s32[512,9]{0,1:T(8,128)}, u32[]{:S(2)}) copy-start(s32[512,9]{0,1:T(8,128)} %param.19) | copy-start | bytes 55300
  21.9 10.5 %copy-start.13 = (f32[9,384]{1,0:T(8,128)S(1)}, f32[9,384]{1,0:T(8,128)}, u32[]{:S(2)}) copy-start(f32[9,384]{1,0:T(8,128)} %basis.1) | copy-start | bytes 41476
  21.9 10.5 %copy-start.14 = (s32[512]{0:T(512)S(1)}, s32[512]{0:T(512)}, u32[]{:S(2)}) copy-start(s32[512]{0:T(512)} %param.20) | copy-start | bytes 6148
  21.9 27.9 %all-to-all-start = ((bf16[32,64,128]{2,1,0:T(8,128)(2,1)}), bf16[32,64,128]{2,1,0:T(8,128)(2,1)S(1)}, u32[]{:S(2)}, u32[]{:S(2)}) async-start(bf16[32,64,128]{2,1,0:T(8,128)(2,1)} %shard_map.140), calls=%async_computation | async-start | bytes 1048576 | tf_op jit(solution)/shard_map/all_to_all | solution.py:331
  32.4 1.0 copy-start.10
  33.4 20.4 %copy-start.4 = (bf16[384,384]{1,0:T(8,128)(2,1)S(1)}, bf16[384,384]{1,0:T(8,128)(2,1)}, u32[]{:S(2)}) copy-start(bf16[384,384]{1,0:T(8,128)(2,1)} %constant.31.clone.forward) | copy-start | bytes 884740
  36.7 1.6 %copy-start = (bf16[2304,640]{1,0:T(8,128)(2,1)}, bf16[2304,640]{1,0:T(8,128)(2,1)S(1)}, u32[]{:S(2)}) copy-start(bf16[2304,640]{1,0:T(8,128)(2,1)S(1)} %get-tuple-element.24.rim_mix) | copy-start | bytes 8847364
  38.3 1.1 %copy-start.2 = (bf16[5,1152,128]{2,1,0:T(8,128)(2,1)}, bf16[5,1152,128]{2,1,0:T(8,128)(2,1)S(1)}, u32[]{:S(2)}) copy-start(bf16[5,1152,128]{2,1,0:T(8,128)(2,1)S(1)} %get-tuple-element.21.own_mix) | copy-start | bytes 4423684
  49.8 1.0 copy-start.6
  51.2 7.9 %collective-permute-start = (bf16[384,128]{1,0:T(8,128)(2,1)S(1)}, bf16[384,128]{1,0:T(8,128)(2,1)S(1)}, u32[]{:S(2)}, u32[]{:S(2)}) collective-permute-start(bf16[384,128]{1,0:T(8,128)(2,1)S(1)} %get-tuple-element.22), channel_id=1, source_target_pairs={{0,32},{32,64},{64,96},{96,128},{128,160},{160,192},{192,224},{224... | collective-permute-start | bytes 294920 | tf_op jit(solution)/shard_map/ppermute | solution.py:362
  52.5 6.6 %collective-permute-start.1 = (bf16[384,128]{1,0:T(8,128)(2,1)S(1)}, bf16[384,128]{1,0:T(8,128)(2,1)S(1)}, u32[]{:S(2)}, u32[]{:S(2)}) collective-permute-start(bf16[384,128]{1,0:T(8,128)(2,1)S(1)} %get-tuple-element.23), channel_id=1, source_target_pairs={{32,0},{64,32},{96,64},{128,96},{160,128},{192,160},{224,192},{256... | collective-permute-start | bytes 294920 | tf_op jit(solution)/shard_map/ppermute | solution.py:363
  53.8 1.4 %copy-start.3 = (bf16[5,1152,128]{2,1,0:T(8,128)(2,1)S(1)}, bf16[5,1152,128]{2,1,0:T(8,128)(2,1)}, u32[]{:S(2)}) copy-start(bf16[5,1152,128]{2,1,0:T(8,128)(2,1)} %copy-done.2) | copy-start | bytes 4423684
  55.2 3.9 %copy-start.1 = (bf16[2304,640]{1,0:T(8,128)(2,1)S(1)}, bf16[2304,640]{1,0:T(8,128)(2,1)}, u32[]{:S(2)}) copy-start(bf16[2304,640]{1,0:T(8,128)(2,1)} %copy-done) | copy-start | bytes 8847364
  55.2 3.9 %copy-start.7 = (bf16[384,384]{1,0:T(8,128)(2,1)S(1)}, bf16[384,384]{1,0:T(8,128)(2,1)}, u32[]{:S(2)}) copy-start(bf16[384,384]{1,0:T(8,128)(2,1)} %constant.32.clone.inverse) | copy-start | bytes 884740
  71.0 0.9 copy-start.8
Sparse Core Ops, SparseCore 0:
  22.0 48.9 reduce-scatter.1

commit v7 on v6

--- a/solution.py
+++ b/solution.py
@@ -149,11 +149,17 @@
         spread[k] = jnp.broadcast_to(basis[k : k + 1, :], (128, NLON)).T
 
 
-def open_kernel(slabs, pick, _ready, moved, first, last, tall):
+def open_kernel(slabs, _ready, moved, first, last, tall):
     from_slabs(slabs, tall)
     for j in range(GROUPS):
         moved[:, 128 * j : 128 * (j + 1)] = tall[pl.ds(j, NLON, stride=GROUPS), :].astype(bf16)
-    edges = nn(moved[...], pick[...]).astype(bf16)
+    row = lax.broadcasted_iota(jnp.int32, (640, 256), 0)
+    lane = lax.broadcasted_iota(jnp.int32, (640, 256), 1)
+    edge = row % 32 - (ROWS - REACH) * (1 - lane // 128)
+    pick = jnp.where(
+        (lane % 128 - row // 32 * REACH == edge) & (edge >= 0) & (edge < REACH), 1.0, 0.0
+    )
+    edges = nn(moved[...], pick.astype(bf16)).astype(bf16)
     last[...] = edges[:, :128]
     first[...] = edges[:, 128:]
 
@@ -246,15 +252,6 @@
     return jnp.asarray(forward.T, bf16), jnp.asarray(inverse.T, bf16)
 
 
-def rim_picks():
-    pick = np.zeros((640, 256), np.float32)
-    for c in range(LOCAL):
-        for r in range(REACH):
-            pick[c * 32 + ROWS - REACH + r, c * 4 + r] = 1.0
-            pick[c * 32 + r, 128 + c * 4 + r] = 1.0
-    return jnp.asarray(pick, bf16)
-
-
 def shape(*dims, dtype=bf16):
     return jax.ShapeDtypeStruct(dims, dtype)
 
@@ -336,7 +333,7 @@
 
     own_mix, rim_mix, spread, ready = call(
         prep_kernel,
-        (shape(GROUPS, NB * 128, 128), shape(NB * 256, 640), shape(NB, NLON, 128, dtype=f32), TOKEN),
+        (pltpu.HBM((GROUPS, NB * 128, 128), bf16), shape(NB * 256, 640), shape(NB, NLON, 128, dtype=f32), TOKEN),
         [SMEM] + [VMEM] * 5,
         1e9,
         6e6,
@@ -353,11 +350,11 @@
     moved, first, last = call(
         open_kernel,
         (shape(NLON, 640), shape(NLON, 128), shape(NLON, 128)),
-        [VMEM] * 3,
+        [VMEM] * 2,
         1e8,
         2e6,
         [pltpu.VMEM((TALL, 128), f32)],
-    )(received, rim_picks(), ready)
+    )(received, ready)
     up = [(i, i + 1) for i in range(n_lat - 1)]
     before = lax.ppermute(last, LAT, up)
     after = lax.ppermute(first, LAT, [(b, a) for a, b in up])
@@ -377,7 +374,7 @@
             pl.BlockSpec((1, NB * 128, 128), lambda j: (j, 0, 0)),
         ],
         out_specs=pl.BlockSpec((NLON, 128), lambda j: (0, j)),
-    )(moved, forward, spread, own_mix)
+    )(moved, forward, spread, pltpu.with_memory_space_constraint(own_mix, pltpu.HBM))
 
     extra = 32 if part == 40 else 40 * -(-2 * part // 128)
     answer = call(
@@ -400,7 +397,7 @@
         [pltpu.VMEM((PEERS, extra, 128), bf16), pltpu.SemaphoreType.DMA],
         out_specs=ANY,
         input_output_aliases={0: 0},
-    )(answer, column)
+    )(answer, pltpu.with_memory_space_constraint(column, pltpu.HBM))
     returned = lax.all_to_all(merged, LON, split_axis=0, concat_axis=0, tiled=True)
     grid_grad, grad_in, grad_out = call(
         final_kernel,

time: 109 us -> 109 us (level)
  local copies, waits for them, and re-layouts: 6.98 us -> 2.58 us
  Pallas kernels: 23 us -> 26.6 us
    unnamed x30 -> x22, local copies, waits for them, and re-layouts: 6.98 us -> 2.58 us
    pallas_call x1, Pallas kernels: 3.9 us -> 5.39 us  [body(): call(own_kernel, shape(NLON, 640, dtype=f32), None, 800000000.0, 5000000....]
  transfers between devices with their start and end apart: 5 -> 5, of which waited for: 2 -> 2; matrix products, arithmetic and copies ran while one was open for 0% -> 0% of each run, Pallas kernels for 13% -> 16%
where the time goes in v7:
time: 109 us; the launch traced here: 108 us
  blocking collectives  27.6 us (25%)
  Pallas kernels  26.6 us (24%)
  waiting for transfers between devices  20.8 us (19%)
  starting transfers between devices  14.9 us (14%)
  between operations  14.2 us (13%)
  local copies, waits for them, and re-layouts  2.58 us (2%)
  other arithmetic  1.62 us (1%)
    all_to_all x1, blocking collectives, body(): lax.all_to_all(merged, LON, split_axis=0, concat_axis=0, tiled=True)  27.6 us
    all_to_all x1, waiting for transfers between devices, body(): lax.all_to_all(send, LON, split_axis=0, concat_axis=0, tiled=True)  10.5 us
    all_to_all x1, starting transfers between devices, body(): lax.all_to_all(send, LON, split_axis=0, concat_axis=0, tiled=True)  10.4 us
    reduce_scatter x1, waiting for transfers between devices, body(): column = lax.psum_scatter(chip, 'z', scatter_dimension=0, tiled=True)  10.3 us
    pallas_call x1, Pallas kernels, body(): call(head_kernel, (pltpu.VMEM((tokens_n, 1280), bf16), pltpu.VMEM(half.sh...  7.12 us
    pallas_call x1, Pallas kernels, body(): call(own_kernel, shape(NLON, 640, dtype=f32), None, 800000000.0, 5000000....  5.39 us
    pallas_call x1, Pallas kernels, body(): call(prep_kernel, (pltpu.HBM((GROUPS, NB * 128, 128), bf16), shape(NB * 2...  4.38 us
    pallas_call x1, Pallas kernels, body(): call(lift_kernel, shape(PEERS, PAD, 128), None, 2000000000.0, 4000000.0,...  4 us
  transfers between devices with their start and end apart: 5, of which 2 were waited for; matrix products, arithmetic and copies ran while one was open for 0% of the time, Pallas kernels for 16%

profile of v7, /device:TPU:2, one launch (start us, length us, event | category | flops | bytes accessed | tf_op | source)
XLA Modules:
  0.0 108.3 jit_solution(11024825509239088211)
XLA Ops:
  7.2 0.0 reduce-scatter.2.cloned.1.call-start
  7.2 0.0 copy-start.3
  7.2 0.0 copy-start.5
  7.2 7.1 %shard_map.130 = (bf16[384,1280]{1,0:T(8,128)(2,1)S(1)}, bf16[8,2,40,1280]{3,2,1,0:T(8,128)(2,1)S(1)}, bf16[8,2,40,1280]{3,2,1,0:T(8,128)(2,1)S(1)}) custom-call(s32[1]{0:T(128)} %bitcast.core, bf16[384,640]{1,0:T(8,128)(2,1)} %bitcast.21, bf16[384,640]{1,0:T(8,128)(2,1)} %bitcast.15, bf16[640,1280]{1,0:T(8,128)(2,1)} %w_in.3, bf16[1280,640]{1,0:T(8,128)(2,1)} %w_out.1), custom_call_target="tpu_custom_call" | custom-call | flops 3000000000 | bytes 8000000 | tf_op jit(solution)/shard_map/pallas_call | solution.py:292
  14.4 1.9 %collective-permute-start.2 = (bf16[8,2,40,1280]{3,2,1,0:T(8,128)(2,1)S(1)}, bf16[8,2,40,1280]{3,2,1,0:T(8,128)(2,1)S(1)}, u32[]{:S(2)}, u32[]{:S(2)}) collective-permute-start(bf16[8,2,40,1280]{3,2,1,0:T(8,128)(2,1)S(1)} %get-tuple-element.27), channel_id=1, source_target_pairs={{0,32},{32,0},{1,33},{33,1},{2,34},{34,2},{3,35},{35,3},{4,36},{36... | collective-permute-start | bytes 4915208 | tf_op jit(solution)/shard_map/ppermute | solution.py:310
  16.3 0.0 copy-done.3
  16.3 0.0 copy-done.5
  16.3 4.0 %shard_map.131 = bf16[32,64,128]{2,1,0:T(8,128)(2,1)} custom-call(bf16[384,1280]{1,0:T(8,128)(2,1)S(1)} %get-tuple-element.17.pre_grad, bf16[384,640]{1,0:T(8,128)(2,1)S(1)} %bitcast.16, bf16[640,1280]{1,0:T(8,128)(2,1)S(1)} %copy-done.5), custom_call_target="tpu_custom_call" | custom-call | flops 2000000000 | bytes 4000000 | tf_op jit(solution)/shard_map/pallas_call | solution.py:312
  20.3 0.0 collective-permute-done.2
  20.3 1.5 %add_convert_fusion = bf16[8,2,40,1280]{3,2,1,0:T(8,128)(2,1)} fusion(bf16[8,2,40,1280]{3,2,1,0:T(8,128)(2,1)S(1)} %collective-permute-done.2, bf16[8,2,40,1280]{3,2,1,0:T(8,128)(2,1)S(1)} %get-tuple-element.26), kind=kLoop, calls=%fused_computation | loop fusion | flops 3276800 | bytes 4915200 | tf_op jit(solution)/shard_map/convert_element_type | solution.py:331
  21.9 0.0 copy-start.7
  21.9 0.0 copy-start.8
  21.9 0.0 copy-start.9
  21.9 0.0 copy-start.10
  21.9 0.0 reduce-scatter.2.cloned.1.call-update
  21.9 10.4 %all-to-all-start = ((bf16[32,64,128]{2,1,0:T(8,128)(2,1)}), bf16[32,64,128]{2,1,0:T(8,128)(2,1)S(1)}, u32[]{:S(2)}, u32[]{:S(2)}) async-start(bf16[32,64,128]{2,1,0:T(8,128)(2,1)} %shard_map.131), calls=%async_computation | async-start | bytes 1048576 | tf_op jit(solution)/shard_map/all_to_all | solution.py:328
  32.3 0.1 pad_add_fusion.place
  32.4 0.0 copy-done.7
  32.4 0.0 copy-done.8
  32.4 0.0 copy-done.9
  32.4 0.0 copy-done.10
  32.4 0.0 copy-start.6
  32.4 1.0 copy-done.6
  33.4 0.0 copy-start.2
  33.4 4.4 %shard_map.132 = (bf16[5,1152,128]{2,1,0:T(8,128)(2,1)}, bf16[2304,640]{1,0:T(8,128)(2,1)S(1)}, f32[9,384,128]{2,1,0:T(8,128)S(1)}, f32[8,128]{1,0:T(8,128)S(1)}) custom-call(s32[2]{0:T(128)S(1)} %pad_add_fusion.place, f32[9,9,512]{2,1,0:T(8,128)S(1)} %bitcast.18, s32[9,512]{1,0:T(8,128)S(1)} %bitcast.19, s32[1,512]{1,0:T(1,128)S(1)} %bitcast.20, ...), custom_call_target="tpu_custom_call" | custom-call | flops 1000000000 | bytes 6000000 | tf_op jit(solution)/shard_map/pallas_call | solution.py:334
  37.7 0.0 copy-start
  37.7 1.6 %copy-done = bf16[2304,640]{1,0:T(8,128)(2,1)} copy-done((bf16[2304,640]{1,0:T(8,128)(2,1)}, bf16[2304,640]{1,0:T(8,128)(2,1)S(1)}, u32[]{:S(2)}) %copy-start) | copy-done | bytes 2949144
  39.3 10.5 %all-to-all-done.slabs = bf16[32,64,128]{2,1,0:T(8,128)(2,1)S(1)} async-done(((bf16[32,64,128]{2,1,0:T(8,128)(2,1)}), bf16[32,64,128]{2,1,0:T(8,128)(2,1)S(1)}, u32[]{:S(2)}, u32[]{:S(2)}) %all-to-all-start) | async-done | bytes 524320 | tf_op jit(solution)/shard_map/all_to_all | solution.py:328
  49.8 0.6 shard_map.133
  50.4 1.3 %collective-permute-start = (bf16[384,128]{1,0:T(8,128)(2,1)S(1)}, bf16[384,128]{1,0:T(8,128)(2,1)S(1)}, u32[]{:S(2)}, u32[]{:S(2)}) collective-permute-start(bf16[384,128]{1,0:T(8,128)(2,1)S(1)} %get-tuple-element.22), channel_id=1, source_target_pairs={{0,32},{32,64},{64,96},{96,128},{128,160},{160,192},{192,224},{224... | collective-permute-start | bytes 294920 | tf_op jit(solution)/shard_map/ppermute | solution.py:359
  51.7 1.3 %collective-permute-start.1 = (bf16[384,128]{1,0:T(8,128)(2,1)S(1)}, bf16[384,128]{1,0:T(8,128)(2,1)S(1)}, u32[]{:S(2)}, u32[]{:S(2)}) collective-permute-start(bf16[384,128]{1,0:T(8,128)(2,1)S(1)} %get-tuple-element.23), channel_id=1, source_target_pairs={{32,0},{64,32},{96,64},{128,96},{160,128},{192,160},{224,192},{256... | collective-permute-start | bytes 294920 | tf_op jit(solution)/shard_map/ppermute | solution.py:360
  53.0 0.0 copy-done.2
  53.0 0.0 copy-start.1
  53.0 0.0 copy-start.4
  53.0 5.4 %shard_map.134.filtered = f32[384,640]{1,0:T(8,128)S(1)} custom-call(bf16[384,640]{1,0:T(8,128)(2,1)S(1)} %get-tuple-element.19.moved, bf16[384,384]{1,0:T(8,128)(2,1)S(1)} %copy-done.2, f32[9,384,128]{2,1,0:T(8,128)S(1)} %get-tuple-element.20.spread, bf16[5,1152,128]{2,1,0:T(8,128)(2,1)} %get-tuple-element.21.own_mix), custom_call_target="tpu_custom_call" | custom-call | flops 800000000 | bytes 5000000 | tf_op jit(solution)/shard_map/pallas_call | solution.py:362
  58.4 0.0 collective-permute-done.before
  58.4 0.0 collective-permute-done.1.after
  58.4 0.0 copy-done.1
  58.4 0.0 copy-done.4
  58.4 2.5 %shard_map.135.answer = bf16[32,96,128]{2,1,0:T(8,128)(2,1)S(1)} custom-call(f32[384,640]{1,0:T(8,128)S(1)} %shard_map.134.filtered, bf16[384,128]{1,0:T(8,128)(2,1)S(1)} %collective-permute-done.before, bf16[384,128]{1,0:T(8,128)(2,1)S(1)} %collective-permute-done.1.after, bf16[384,384]{1,0:T(8,128)(2,1)S(1)} %copy-done.2, bf16[384,384]{1,0:T(8,128)(2,1)S(1)} %copy-done.4, ...), custom_call_target="tpu_custom_call" | custom-call | flops 1500000000 | bytes 7000000 | tf_op jit(solution)/shard_map/pallas_call | solution.py:380
  60.9 10.3 %reduce-scatter.2.cloned.1.call-done.column = bf16[1,2,40,1280]{3,2,1,0:T(8,128)(2,1)} async-done(((bf16[8,2,40,1280]{3,2,1,0:T(8,128)(2,1)}), bf16[1,2,40,1280]{3,2,1,0:T(8,128)(2,1)}) %reduce-scatter.2.cloned.1.call-update) | async-done | bytes 204816 | tf_op jit(solution)/shard_map/reduce_scatter | solution.py:332
  71.2 1.2 %shard_map.136 = bf16[32,96,128]{2,1,0:T(8,128)(2,1)S(1)} custom-call(bf16[32,96,128]{2,1,0:T(8,128)(2,1)S(1)} %shard_map.135.answer, bf16[1,2,40,1280]{3,2,1,0:T(8,128)(2,1)} %reduce-scatter.2.cloned.1.call-done.column), custom_call_target="tpu_custom_call", output_to_operand_aliasing={{}: (0, {})} | custom-call | flops 1000000 | bytes 2000000 | tf_op jit(solution)/shard_map/pallas_call | solution.py:391
  72.4 27.6 %all_to_all.10.slabs = bf16[32,96,128]{2,1,0:T(8,128)(2,1)S(1)} all-to-all(bf16[32,96,128]{2,1,0:T(8,128)(2,1)S(1)} %shard_map.136), channel_id=1, replica_groups=mesh['z'=8,'core'=2,'y'=8,'x'=4] {'y','x'}, dimensions={0} | all-to-all | bytes 1572864 | tf_op jit(solution)/shard_map/all_to_all | solution.py:401
  100.0 1.5 %shard_map.137 = (bf16[384,640]{1,0:T(8,128)(2,1)}, f32[40,40]{1,0:T(8,128)}, f32[40,40]{1,0:T(8,128)}) custom-call(bf16[32,96,128]{2,1,0:T(8,128)(2,1)S(1)} %all_to_all.10.slabs, bf16[384,640]{1,0:T(8,128)(2,1)S(1)} %bitcast.17), custom_call_target="tpu_custom_call" | custom-call | flops 100000000 | bytes 2000000 | tf_op jit(solution)/shard_map/pallas_call | solution.py:402
Async XLA Ops:
  7.2 64.0 %reduce-scatter.2.cloned.1.call-start = ((), (), s32[]{:S(2)}) async-start(), calls=%async_computation.3 | async-start | bytes 1843200 | tf_op jit(solution)/shard_map/reduce_scatter | solution.py:332
  7.2 9.1 %copy-start.3 = (bf16[32,12,640]{2,0,1:T(8,128)(2,1)S(1)}, bf16[32,12,640]{2,0,1:T(8,128)(2,1)}, u32[]{:S(2)}) copy-start(bf16[32,12,640]{2,0,1:T(8,128)(2,1)} %param.12) | copy-start | bytes 1474564
  7.2 9.1 %copy-start.5 = (bf16[640,1280]{1,0:T(8,128)(2,1)S(1)}, bf16[640,1280]{1,0:T(8,128)(2,1)}, u32[]{:S(2)}) copy-start(bf16[640,1280]{1,0:T(8,128)(2,1)} %w_in.3) | copy-start | bytes 4915204
  14.4 5.9 %collective-permute-start.2 = (bf16[8,2,40,1280]{3,2,1,0:T(8,128)(2,1)S(1)}, bf16[8,2,40,1280]{3,2,1,0:T(8,128)(2,1)S(1)}, u32[]{:S(2)}, u32[]{:S(2)}) collective-permute-start(bf16[8,2,40,1280]{3,2,1,0:T(8,128)(2,1)S(1)} %get-tuple-element.27), channel_id=1, source_target_pairs={{0,32},{32,0},{1,33},{33,1},{2,34},{34,2},{3,35},{35,3},{4,36},{36... | collective-permute-start | bytes 4915208 | tf_op jit(solution)/shard_map/ppermute | solution.py:310
  21.9 10.5 %copy-start.7 = (f32[9,640]{1,0:T(8,128)S(1)}, f32[9,640]{1,0:T(8,128)}, u32[]{:S(2)}) copy-start(f32[9,640]{1,0:T(8,128)} %chan.1) | copy-start | bytes 69124
  21.9 10.5 %copy-start.8 = (s32[512,9]{0,1:T(8,128)S(1)}, s32[512,9]{0,1:T(8,128)}, u32[]{:S(2)}) copy-start(s32[512,9]{0,1:T(8,128)} %param.18) | copy-start | bytes 55300
  21.9 10.5 %copy-start.9 = (f32[9,384]{1,0:T(8,128)S(1)}, f32[9,384]{1,0:T(8,128)}, u32[]{:S(2)}) copy-start(f32[9,384]{1,0:T(8,128)} %basis.1) | copy-start | bytes 41476
  21.9 10.5 %copy-start.10 = (s32[512]{0:T(512)S(1)}, s32[512]{0:T(512)}, u32[]{:S(2)}) copy-start(s32[512]{0:T(512)} %param.19) | copy-start | bytes 6148
  21.9 27.9 %all-to-all-start = ((bf16[32,64,128]{2,1,0:T(8,128)(2,1)}), bf16[32,64,128]{2,1,0:T(8,128)(2,1)S(1)}, u32[]{:S(2)}, u32[]{:S(2)}) async-start(bf16[32,64,128]{2,1,0:T(8,128)(2,1)} %shard_map.131), calls=%async_computation | async-start | bytes 1048576 | tf_op jit(solution)/shard_map/all_to_all | solution.py:328
  32.4 1.0 copy-start.6
  33.4 19.6 %copy-start.2 = (bf16[384,384]{1,0:T(8,128)(2,1)S(1)}, bf16[384,384]{1,0:T(8,128)(2,1)}, u32[]{:S(2)}) copy-start(bf16[384,384]{1,0:T(8,128)(2,1)} %constant.29.clone.forward) | copy-start | bytes 884740
  37.7 1.6 %copy-start = (bf16[2304,640]{1,0:T(8,128)(2,1)}, bf16[2304,640]{1,0:T(8,128)(2,1)S(1)}, u32[]{:S(2)}) copy-start(bf16[2304,640]{1,0:T(8,128)(2,1)S(1)} %get-tuple-element.24.rim_mix) | copy-start | bytes 8847364
  50.4 8.0 %collective-permute-start = (bf16[384,128]{1,0:T(8,128)(2,1)S(1)}, bf16[384,128]{1,0:T(8,128)(2,1)S(1)}, u32[]{:S(2)}, u32[]{:S(2)}) collective-permute-start(bf16[384,128]{1,0:T(8,128)(2,1)S(1)} %get-tuple-element.22), channel_id=1, source_target_pairs={{0,32},{32,64},{64,96},{96,128},{128,160},{160,192},{192,224},{224... | collective-permute-start | bytes 294920 | tf_op jit(solution)/shard_map/ppermute | solution.py:359
  51.7 6.7 %collective-permute-start.1 = (bf16[384,128]{1,0:T(8,128)(2,1)S(1)}, bf16[384,128]{1,0:T(8,128)(2,1)S(1)}, u32[]{:S(2)}, u32[]{:S(2)}) collective-permute-start(bf16[384,128]{1,0:T(8,128)(2,1)S(1)} %get-tuple-element.23), channel_id=1, source_target_pairs={{32,0},{64,32},{96,64},{128,96},{160,128},{192,160},{224,192},{256... | collective-permute-start | bytes 294920 | tf_op jit(solution)/shard_map/ppermute | solution.py:360
  53.0 5.4 %copy-start.1 = (bf16[2304,640]{1,0:T(8,128)(2,1)S(1)}, bf16[2304,640]{1,0:T(8,128)(2,1)}, u32[]{:S(2)}) copy-start(bf16[2304,640]{1,0:T(8,128)(2,1)} %copy-done) | copy-start | bytes 8847364
  53.0 5.4 %copy-start.4 = (bf16[384,384]{1,0:T(8,128)(2,1)S(1)}, bf16[384,384]{1,0:T(8,128)(2,1)}, u32[]{:S(2)}) copy-start(bf16[384,384]{1,0:T(8,128)(2,1)} %constant.30.clone.inverse) | copy-start | bytes 884740
Sparse Core Ops, SparseCore 0:
  22.0 49.1 reduce-scatter.1

commit v8 on v7

--- a/solution.py
+++ b/solution.py
@@ -91,17 +91,15 @@
 
 
 def lift_kernel(pre_grad, cot, w_in, send, tall):
-    j = pl.program_id(0)
-    whole = cot[...].astype(f32).T + nt(w_in[...], pre_grad[...])
-    for a in range(LONS // 4):
-        tiles = [whole[q * 32 : (q + 1) * 32, a * 128 : (a + 1) * 128] for q in range(4)]
-        for b, tile in enumerate(swap_quarters(tiles)):
-            tall[pl.ds((4 * a + b) * GROUPS + j, PEERS, stride=SLAB), :] = tile
-
-    @pl.when(j == pl.num_programs(0) - 1)
-    def _():
-        tall[TALL - 8 :, :] = jnp.zeros((8, 128), f32)
-        to_slabs(tall, send)
+    tall[TALL - 8 :, :] = jnp.zeros((8, 128), f32)
+    for j in range(GROUPS):
+        part = slice(128 * j, 128 * (j + 1))
+        whole = cot[:, part].astype(f32).T + nt(w_in[part, :], pre_grad[...])
+        for a in range(LONS // 4):
+            tiles = [whole[q * 32 : (q + 1) * 32, a * 128 : (a + 1) * 128] for q in range(4)]
+            for b, tile in enumerate(swap_quarters(tiles)):
+                tall[pl.ds((4 * a + b) * GROUPS + j, PEERS, stride=SLAB), :] = tile
+    to_slabs(tall, send)
 
 
 def prep_kernel(place, row_w, cols, widths, chan, basis, own_mix, rim_mix, spread, token):
@@ -311,18 +309,14 @@
 
     send = call(
         lift_kernel,
-        shape(PEERS, PAD, 128),
+        pltpu.HBM((PEERS, PAD, 128), bf16),
         None,
         2e9,
         4e6,
         [pltpu.VMEM((TALL, 128), f32)],
         limit=48,
-        grid=(GROUPS,),
-        in_specs=[
-            whole(tokens_n, 1280),
-            pl.BlockSpec((tokens_n, 128), lambda j: (0, j)),
-            pl.BlockSpec((128, 1280), lambda j: (j, 0)),
-        ],
+        grid=(1,),
+        in_specs=[VMEM] * 3,
         out_specs=whole(PEERS, PAD, 128),
     )(pre_grad, cotangent, w_in)
     received = lax.all_to_all(send, LON, split_axis=0, concat_axis=0, tiled=True)

time: 109 us -> 108 us (level)
  Pallas kernels: 26.6 us -> 25.2 us
    pallas_call x1, Pallas kernels: 4 us -> 2.6 us  [body(): call(lift_kernel, pltpu.HBM((PEERS, PAD, 128), bf16), None, 2000000000.0,...]
  transfers between devices with their start and end apart: 5 -> 5, of which waited for: 2 -> 3; matrix products, arithmetic and copies ran while one was open for 0% -> 0% of each run, Pallas kernels for 16% -> 14%
where the time goes in v8:
time: 108 us
  blocking collectives  27.9 us (26%)
  Pallas kernels  25.2 us (23%)
  waiting for transfers between devices  21 us (19%)
  starting transfers between devices  15.1 us (14%)
  between operations  14.2 us (13%)
  local copies, waits for them, and re-layouts  2.58 us (2%)
  other arithmetic  1.62 us (2%)
    all_to_all x1, blocking collectives, body(): lax.all_to_all(merged, LON, split_axis=0, concat_axis=0, tiled=True)  27.9 us
    all_to_all x1, starting transfers between devices, body(): lax.all_to_all(send, LON, split_axis=0, concat_axis=0, tiled=True)  10.4 us
    all_to_all x1, waiting for transfers between devices, body(): lax.all_to_all(send, LON, split_axis=0, concat_axis=0, tiled=True)  10.1 us
    reduce_scatter x1, waiting for transfers between devices, body(): column = lax.psum_scatter(chip, 'z', scatter_dimension=0, tiled=True)  10.1 us
    pallas_call x1, Pallas kernels, body(): call(head_kernel, (pltpu.VMEM((tokens_n, 1280), bf16), pltpu.VMEM(half.sh...  7.12 us
    pallas_call x1, Pallas kernels, body(): call(own_kernel, shape(NLON, 640, dtype=f32), None, 800000000.0, 5000000....  5.39 us
    pallas_call x1, Pallas kernels, body(): call(prep_kernel, (pltpu.HBM((GROUPS, NB * 128, 128), bf16), shape(NB * 2...  4.38 us
    pallas_call x1, Pallas kernels, body(): call(lift_kernel, pltpu.HBM((PEERS, PAD, 128), bf16), None, 2000000000.0,...  2.6 us
  transfers between devices with their start and end apart: 5, of which 3 were waited for; matrix products, arithmetic and copies ran while one was open for 0% of the time, Pallas kernels for 14%

profile of v8, /device:TPU:2, one launch (start us, length us, event | category | flops | bytes accessed | tf_op | source)
XLA Modules:
  0.0 107.7 jit_solution(15214649024294380906)
XLA Ops:
  7.2 0.0 reduce-scatter.2.cloned.1.call-start
  7.2 0.0 copy-start.3
  7.2 0.0 copy-start.5
  7.2 7.1 %shard_map.130 = (bf16[384,1280]{1,0:T(8,128)(2,1)S(1)}, bf16[8,2,40,1280]{3,2,1,0:T(8,128)(2,1)S(1)}, bf16[8,2,40,1280]{3,2,1,0:T(8,128)(2,1)S(1)}) custom-call(s32[1]{0:T(128)} %bitcast.core, bf16[384,640]{1,0:T(8,128)(2,1)} %bitcast.21, bf16[384,640]{1,0:T(8,128)(2,1)} %bitcast.15, bf16[640,1280]{1,0:T(8,128)(2,1)} %w_in.3, bf16[1280,640]{1,0:T(8,128)(2,1)} %w_out.1), custom_call_target="tpu_custom_call" | custom-call | flops 3000000000 | bytes 8000000 | tf_op jit(solution)/shard_map/pallas_call | solution.py:290
  14.4 1.9 %collective-permute-start.2 = (bf16[8,2,40,1280]{3,2,1,0:T(8,128)(2,1)S(1)}, bf16[8,2,40,1280]{3,2,1,0:T(8,128)(2,1)S(1)}, u32[]{:S(2)}, u32[]{:S(2)}) collective-permute-start(bf16[8,2,40,1280]{3,2,1,0:T(8,128)(2,1)S(1)} %get-tuple-element.27), channel_id=1, source_target_pairs={{0,32},{32,0},{1,33},{33,1},{2,34},{34,2},{3,35},{35,3},{4,36},{36... | collective-permute-start | bytes 4915208 | tf_op jit(solution)/shard_map/ppermute | solution.py:308
  16.3 0.0 copy-done.3
  16.3 0.0 copy-done.5
  16.3 2.6 %shard_map.131 = bf16[32,64,128]{2,1,0:T(8,128)(2,1)} custom-call(bf16[384,1280]{1,0:T(8,128)(2,1)S(1)} %get-tuple-element.17.pre_grad, bf16[384,640]{1,0:T(8,128)(2,1)S(1)} %bitcast.16, bf16[640,1280]{1,0:T(8,128)(2,1)S(1)} %copy-done.5), custom_call_target="tpu_custom_call" | custom-call | flops 2000000000 | bytes 4000000 | tf_op jit(solution)/shard_map/pallas_call | solution.py:310
  18.9 0.9 collective-permute-done.2
  19.8 1.5 %add_convert_fusion = bf16[8,2,40,1280]{3,2,1,0:T(8,128)(2,1)} fusion(bf16[8,2,40,1280]{3,2,1,0:T(8,128)(2,1)S(1)} %collective-permute-done.2, bf16[8,2,40,1280]{3,2,1,0:T(8,128)(2,1)S(1)} %get-tuple-element.26), kind=kLoop, calls=%fused_computation | loop fusion | flops 3276800 | bytes 4915200 | tf_op jit(solution)/shard_map/convert_element_type | solution.py:325
  21.3 0.0 copy-start.7
  21.3 0.0 copy-start.8
  21.3 0.0 copy-start.9
  21.3 0.0 copy-start.10
  21.3 0.0 reduce-scatter.2.cloned.1.call-update
  21.3 10.4 %all-to-all-start = ((bf16[32,64,128]{2,1,0:T(8,128)(2,1)}), bf16[32,64,128]{2,1,0:T(8,128)(2,1)S(1)}, u32[]{:S(2)}, u32[]{:S(2)}) async-start(bf16[32,64,128]{2,1,0:T(8,128)(2,1)} %shard_map.131), calls=%async_computation | async-start | bytes 1048576 | tf_op jit(solution)/shard_map/all_to_all | solution.py:322
  31.8 0.1 pad_add_fusion.place
  31.8 0.0 copy-done.7
  31.8 0.0 copy-done.8
  31.8 0.0 copy-done.9
  31.8 0.0 copy-done.10
  31.9 0.0 copy-start.6
  31.9 1.0 copy-done.6
  32.8 0.0 copy-start.2
  32.8 4.4 %shard_map.132 = (bf16[5,1152,128]{2,1,0:T(8,128)(2,1)}, bf16[2304,640]{1,0:T(8,128)(2,1)S(1)}, f32[9,384,128]{2,1,0:T(8,128)S(1)}, f32[8,128]{1,0:T(8,128)S(1)}) custom-call(s32[2]{0:T(128)S(1)} %pad_add_fusion.place, f32[9,9,512]{2,1,0:T(8,128)S(1)} %bitcast.18, s32[9,512]{1,0:T(8,128)S(1)} %bitcast.19, s32[1,512]{1,0:T(1,128)S(1)} %bitcast.20, ...), custom_call_target="tpu_custom_call" | custom-call | flops 1000000000 | bytes 6000000 | tf_op jit(solution)/shard_map/pallas_call | solution.py:328
  37.2 0.0 copy-start
  37.2 1.6 %copy-done = bf16[2304,640]{1,0:T(8,128)(2,1)} copy-done((bf16[2304,640]{1,0:T(8,128)(2,1)}, bf16[2304,640]{1,0:T(8,128)(2,1)S(1)}, u32[]{:S(2)}) %copy-start) | copy-done | bytes 2949144
  38.8 10.1 %all-to-all-done.slabs = bf16[32,64,128]{2,1,0:T(8,128)(2,1)S(1)} async-done(((bf16[32,64,128]{2,1,0:T(8,128)(2,1)}), bf16[32,64,128]{2,1,0:T(8,128)(2,1)S(1)}, u32[]{:S(2)}, u32[]{:S(2)}) %all-to-all-start) | async-done | bytes 524320 | tf_op jit(solution)/shard_map/all_to_all | solution.py:322
  48.9 0.6 shard_map.133
  49.5 1.3 %collective-permute-start = (bf16[384,128]{1,0:T(8,128)(2,1)S(1)}, bf16[384,128]{1,0:T(8,128)(2,1)S(1)}, u32[]{:S(2)}, u32[]{:S(2)}) collective-permute-start(bf16[384,128]{1,0:T(8,128)(2,1)S(1)} %get-tuple-element.22), channel_id=1, source_target_pairs={{0,32},{32,64},{64,96},{96,128},{128,160},{160,192},{192,224},{224... | collective-permute-start | bytes 294920 | tf_op jit(solution)/shard_map/ppermute | solution.py:353
  50.8 1.5 %collective-permute-start.1 = (bf16[384,128]{1,0:T(8,128)(2,1)S(1)}, bf16[384,128]{1,0:T(8,128)(2,1)S(1)}, u32[]{:S(2)}, u32[]{:S(2)}) collective-permute-start(bf16[384,128]{1,0:T(8,128)(2,1)S(1)} %get-tuple-element.23), channel_id=1, source_target_pairs={{32,0},{64,32},{96,64},{128,96},{160,128},{192,160},{224,192},{256... | collective-permute-start | bytes 294920 | tf_op jit(solution)/shard_map/ppermute | solution.py:354
  52.2 0.0 copy-done.2
  52.3 0.0 copy-start.1
  52.3 0.0 copy-start.4
  52.3 5.4 %shard_map.134.filtered = f32[384,640]{1,0:T(8,128)S(1)} custom-call(bf16[384,640]{1,0:T(8,128)(2,1)S(1)} %get-tuple-element.19.moved, bf16[384,384]{1,0:T(8,128)(2,1)S(1)} %copy-done.2, f32[9,384,128]{2,1,0:T(8,128)S(1)} %get-tuple-element.20.spread, bf16[5,1152,128]{2,1,0:T(8,128)(2,1)} %get-tuple-element.21.own_mix), custom_call_target="tpu_custom_call" | custom-call | flops 800000000 | bytes 5000000 | tf_op jit(solution)/shard_map/pallas_call | solution.py:356
  57.7 0.0 collective-permute-done.before
  57.7 0.0 collective-permute-done.1.after
  57.7 0.0 copy-done.1
  57.7 0.0 copy-done.4
  57.7 2.5 %shard_map.135.answer = bf16[32,96,128]{2,1,0:T(8,128)(2,1)S(1)} custom-call(f32[384,640]{1,0:T(8,128)S(1)} %shard_map.134.filtered, bf16[384,128]{1,0:T(8,128)(2,1)S(1)} %collective-permute-done.before, bf16[384,128]{1,0:T(8,128)(2,1)S(1)} %collective-permute-done.1.after, bf16[384,384]{1,0:T(8,128)(2,1)S(1)} %copy-done.2, bf16[384,384]{1,0:T(8,128)(2,1)S(1)} %copy-done.4, ...), custom_call_target="tpu_custom_call" | custom-call | flops 1500000000 | bytes 7000000 | tf_op jit(solution)/shard_map/pallas_call | solution.py:374
  60.2 10.1 %reduce-scatter.2.cloned.1.call-done.column = bf16[1,2,40,1280]{3,2,1,0:T(8,128)(2,1)} async-done(((bf16[8,2,40,1280]{3,2,1,0:T(8,128)(2,1)}), bf16[1,2,40,1280]{3,2,1,0:T(8,128)(2,1)}) %reduce-scatter.2.cloned.1.call-update) | async-done | bytes 204816 | tf_op jit(solution)/shard_map/reduce_scatter | solution.py:326
  70.3 1.2 %shard_map.136 = bf16[32,96,128]{2,1,0:T(8,128)(2,1)S(1)} custom-call(bf16[32,96,128]{2,1,0:T(8,128)(2,1)S(1)} %shard_map.135.answer, bf16[1,2,40,1280]{3,2,1,0:T(8,128)(2,1)} %reduce-scatter.2.cloned.1.call-done.column), custom_call_target="tpu_custom_call", output_to_operand_aliasing={{}: (0, {})} | custom-call | flops 1000000 | bytes 2000000 | tf_op jit(solution)/shard_map/pallas_call | solution.py:385
  71.5 27.9 %all_to_all.10.slabs = bf16[32,96,128]{2,1,0:T(8,128)(2,1)S(1)} all-to-all(bf16[32,96,128]{2,1,0:T(8,128)(2,1)S(1)} %shard_map.136), channel_id=1, replica_groups=mesh['z'=8,'core'=2,'y'=8,'x'=4] {'y','x'}, dimensions={0} | all-to-all | bytes 1572864 | tf_op jit(solution)/shard_map/all_to_all | solution.py:395
  99.4 1.5 %shard_map.137 = (bf16[384,640]{1,0:T(8,128)(2,1)}, f32[40,40]{1,0:T(8,128)}, f32[40,40]{1,0:T(8,128)}) custom-call(bf16[32,96,128]{2,1,0:T(8,128)(2,1)S(1)} %all_to_all.10.slabs, bf16[384,640]{1,0:T(8,128)(2,1)S(1)} %bitcast.17), custom_call_target="tpu_custom_call" | custom-call | flops 100000000 | bytes 2000000 | tf_op jit(solution)/shard_map/pallas_call | solution.py:396
Async XLA Ops:
  7.2 63.1 %reduce-scatter.2.cloned.1.call-start = ((), (), s32[]{:S(2)}) async-start(), calls=%async_computation.3 | async-start | bytes 1843200 | tf_op jit(solution)/shard_map/reduce_scatter | solution.py:326
  7.2 9.1 %copy-start.3 = (bf16[32,12,640]{2,0,1:T(8,128)(2,1)S(1)}, bf16[32,12,640]{2,0,1:T(8,128)(2,1)}, u32[]{:S(2)}) copy-start(bf16[32,12,640]{2,0,1:T(8,128)(2,1)} %param.12) | copy-start | bytes 1474564
  7.2 9.1 %copy-start.5 = (bf16[640,1280]{1,0:T(8,128)(2,1)S(1)}, bf16[640,1280]{1,0:T(8,128)(2,1)}, u32[]{:S(2)}) copy-start(bf16[640,1280]{1,0:T(8,128)(2,1)} %w_in.3) | copy-start | bytes 4915204
  14.4 5.4 %collective-permute-start.2 = (bf16[8,2,40,1280]{3,2,1,0:T(8,128)(2,1)S(1)}, bf16[8,2,40,1280]{3,2,1,0:T(8,128)(2,1)S(1)}, u32[]{:S(2)}, u32[]{:S(2)}) collective-permute-start(bf16[8,2,40,1280]{3,2,1,0:T(8,128)(2,1)S(1)} %get-tuple-element.27), channel_id=1, source_target_pairs={{0,32},{32,0},{1,33},{33,1},{2,34},{34,2},{3,35},{35,3},{4,36},{36... | collective-permute-start | bytes 4915208 | tf_op jit(solution)/shard_map/ppermute | solution.py:308
  21.3 10.5 %copy-start.7 = (f32[9,640]{1,0:T(8,128)S(1)}, f32[9,640]{1,0:T(8,128)}, u32[]{:S(2)}) copy-start(f32[9,640]{1,0:T(8,128)} %chan.1) | copy-start | bytes 69124
  21.3 10.5 %copy-start.8 = (s32[512,9]{0,1:T(8,128)S(1)}, s32[512,9]{0,1:T(8,128)}, u32[]{:S(2)}) copy-start(s32[512,9]{0,1:T(8,128)} %param.18) | copy-start | bytes 55300
  21.3 10.5 %copy-start.9 = (f32[9,384]{1,0:T(8,128)S(1)}, f32[9,384]{1,0:T(8,128)}, u32[]{:S(2)}) copy-start(f32[9,384]{1,0:T(8,128)} %basis.1) | copy-start | bytes 41476
  21.3 10.5 %copy-start.10 = (s32[512]{0:T(512)S(1)}, s32[512]{0:T(512)}, u32[]{:S(2)}) copy-start(s32[512]{0:T(512)} %param.19) | copy-start | bytes 6148
  21.3 27.5 %all-to-all-start = ((bf16[32,64,128]{2,1,0:T(8,128)(2,1)}), bf16[32,64,128]{2,1,0:T(8,128)(2,1)S(1)}, u32[]{:S(2)}, u32[]{:S(2)}) async-start(bf16[32,64,128]{2,1,0:T(8,128)(2,1)} %shard_map.131), calls=%async_computation | async-start | bytes 1048576 | tf_op jit(solution)/shard_map/all_to_all | solution.py:322
  31.9 1.0 copy-start.6
  32.8 19.4 %copy-start.2 = (bf16[384,384]{1,0:T(8,128)(2,1)S(1)}, bf16[384,384]{1,0:T(8,128)(2,1)}, u32[]{:S(2)}) copy-start(bf16[384,384]{1,0:T(8,128)(2,1)} %constant.29.clone.forward) | copy-start | bytes 884740
  37.2 1.6 %copy-start = (bf16[2304,640]{1,0:T(8,128)(2,1)}, bf16[2304,640]{1,0:T(8,128)(2,1)S(1)}, u32[]{:S(2)}) copy-start(bf16[2304,640]{1,0:T(8,128)(2,1)S(1)} %get-tuple-element.24.rim_mix) | copy-start | bytes 8847364
  49.5 8.2 %collective-permute-start = (bf16[384,128]{1,0:T(8,128)(2,1)S(1)}, bf16[384,128]{1,0:T(8,128)(2,1)S(1)}, u32[]{:S(2)}, u32[]{:S(2)}) collective-permute-start(bf16[384,128]{1,0:T(8,128)(2,1)S(1)} %get-tuple-element.22), channel_id=1, source_target_pairs={{0,32},{32,64},{64,96},{96,128},{128,160},{160,192},{192,224},{224... | collective-permute-start | bytes 294920 | tf_op jit(solution)/shard_map/ppermute | solution.py:353
  50.8 6.9 %collective-permute-start.1 = (bf16[384,128]{1,0:T(8,128)(2,1)S(1)}, bf16[384,128]{1,0:T(8,128)(2,1)S(1)}, u32[]{:S(2)}, u32[]{:S(2)}) collective-permute-start(bf16[384,128]{1,0:T(8,128)(2,1)S(1)} %get-tuple-element.23), channel_id=1, source_target_pairs={{32,0},{64,32},{96,64},{128,96},{160,128},{192,160},{224,192},{256... | collective-permute-start | bytes 294920 | tf_op jit(solution)/shard_map/ppermute | solution.py:354
  52.3 5.4 %copy-start.1 = (bf16[2304,640]{1,0:T(8,128)(2,1)S(1)}, bf16[2304,640]{1,0:T(8,128)(2,1)}, u32[]{:S(2)}) copy-start(bf16[2304,640]{1,0:T(8,128)(2,1)} %copy-done) | copy-start | bytes 8847364
  52.3 5.4 %copy-start.4 = (bf16[384,384]{1,0:T(8,128)(2,1)S(1)}, bf16[384,384]{1,0:T(8,128)(2,1)}, u32[]{:S(2)}) copy-start(bf16[384,384]{1,0:T(8,128)(2,1)} %constant.30.clone.inverse) | copy-start | bytes 884740
Sparse Core Ops, SparseCore 0:
  21.5 48.7 reduce-scatter.1

commit v9 on v8

--- a/solution.py
+++ b/solution.py
@@ -162,14 +162,20 @@
     first[...] = edges[:, 128:]
 
 
-def own_kernel(moved, forward, spread, own_mix, filtered, mixed):
-    spectra = nn(forward[...], moved[...])
-    first, second = spectra[:NF], spectra[NF:]
-    for k in range(NB):
-        cosine, sine = spread[k, :NF], spread[k, NF:]
-        mixed[:NF, k * 128 : (k + 1) * 128] = (cosine * first + sine * second).astype(bf16)
-        mixed[NF:, k * 128 : (k + 1) * 128] = (cosine * second - sine * first).astype(bf16)
-    filtered[...] = nn(mixed[...], own_mix[0])
+def own_kernel(moved, forward, spread, own_mix, filtered, mixed, held, sems):
+    copies = [pltpu.make_async_copy(own_mix.at[j], held.at[j], sems.at[j]) for j in range(GROUPS)]
+    for copy in copies:
+        copy.start()
+    for j in range(GROUPS):
+        lanes = slice(128 * j, 128 * (j + 1))
+        spectra = nn(forward[...], moved[:, lanes])
+        first, second = spectra[:NF], spectra[NF:]
+        for k in range(NB):
+            cosine, sine = spread[k, :NF], spread[k, NF:]
+            mixed[j % 2, :NF, k * 128 : (k + 1) * 128] = (cosine * first + sine * second).astype(bf16)
+            mixed[j % 2, NF:, k * 128 : (k + 1) * 128] = (cosine * second - sine * first).astype(bf16)
+        copies[j].wait()
+        filtered[:, lanes] = nn(mixed[j % 2], held[j])
 
 
 def close_kernel(filtered, before, after, forward, inverse, spread, rim_mix, send, mixed, tall):
@@ -356,18 +362,14 @@
     filtered = call(
         own_kernel,
         shape(NLON, 640, dtype=f32),
-        None,
+        [VMEM] * 3 + [ANY],
         8e8,
         5e6,
-        [pltpu.VMEM((NLON, NB * 128), bf16)],
-        grid=(GROUPS,),
-        in_specs=[
-            pl.BlockSpec((NLON, 128), lambda j: (0, j)),
-            whole(NLON, NLON),
-            whole(NB, NLON, 128),
-            pl.BlockSpec((1, NB * 128, 128), lambda j: (j, 0, 0)),
+        [
+            pltpu.VMEM((2, NLON, NB * 128), bf16),
+            pltpu.VMEM((GROUPS, NB * 128, 128), bf16),
+            pltpu.SemaphoreType.DMA((GROUPS,)),
         ],
-        out_specs=pl.BlockSpec((NLON, 128), lambda j: (0, j)),
     )(moved, forward, spread, pltpu.with_memory_space_constraint(own_mix, pltpu.HBM))
 
     extra = 32 if part == 40 else 40 * -(-2 * part // 128)

time: 108 us -> 108 us (level)
  no operation moved by 1% of the time
where the time goes in v9:
time: 108 us
  blocking collectives  27.9 us (26%)
  Pallas kernels  24.5 us (23%)
  waiting for transfers between devices  21.8 us (20%)
  starting transfers between devices  15.1 us (14%)
  between operations  14.2 us (13%)
  local copies, waits for them, and re-layouts  2.58 us (2%)
  other arithmetic  1.62 us (2%)
    all_to_all x1, blocking collectives, body(): lax.all_to_all(merged, LON, split_axis=0, concat_axis=0, tiled=True)  27.9 us
    reduce_scatter x1, waiting for transfers between devices, body(): column = lax.psum_scatter(chip, 'z', scatter_dimension=0, tiled=True)  10.8 us
    all_to_all x1, starting transfers between devices, body(): lax.all_to_all(send, LON, split_axis=0, concat_axis=0, tiled=True)  10.4 us
    all_to_all x1, waiting for transfers between devices, body(): lax.all_to_all(send, LON, split_axis=0, concat_axis=0, tiled=True)  10.1 us
    pallas_call x1, Pallas kernels, body(): call(head_kernel, (pltpu.VMEM((tokens_n, 1280), bf16), pltpu.VMEM(half.sh...  7.12 us
    pallas_call x1, Pallas kernels, body(): call(own_kernel, shape(NLON, 640, dtype=f32), [VMEM] * 3 + [ANY], 8000000...  4.65 us
    pallas_call x1, Pallas kernels, body(): call(prep_kernel, (pltpu.HBM((GROUPS, NB * 128, 128), bf16), shape(NB * 2...  4.38 us
    pallas_call x1, Pallas kernels, body(): call(lift_kernel, pltpu.HBM((PEERS, PAD, 128), bf16), None, 2000000000.0,...  2.6 us
  transfers between devices with their start and end apart: 5, of which 3 were waited for; matrix products, arithmetic and copies ran while one was open for 0% of the time, Pallas kernels for 14%

profile of v9, /device:TPU:2, one launch (start us, length us, event | category | flops | bytes accessed | tf_op | source)
XLA Modules:
  0.0 107.7 jit_solution(11668944348137978089)
XLA Ops:
  7.2 0.0 reduce-scatter.2.cloned.1.call-start
  7.2 0.0 copy-start.3
  7.2 0.0 copy-start.5
  7.2 7.1 %shard_map.130 = (bf16[384,1280]{1,0:T(8,128)(2,1)S(1)}, bf16[8,2,40,1280]{3,2,1,0:T(8,128)(2,1)S(1)}, bf16[8,2,40,1280]{3,2,1,0:T(8,128)(2,1)S(1)}) custom-call(s32[1]{0:T(128)} %bitcast.core, bf16[384,640]{1,0:T(8,128)(2,1)} %bitcast.21, bf16[384,640]{1,0:T(8,128)(2,1)} %bitcast.15, bf16[640,1280]{1,0:T(8,128)(2,1)} %w_in.3, bf16[1280,640]{1,0:T(8,128)(2,1)} %w_out.1), custom_call_target="tpu_custom_call" | custom-call | flops 3000000000 | bytes 8000000 | tf_op jit(solution)/shard_map/pallas_call | solution.py:296
  14.4 1.9 %collective-permute-start.2 = (bf16[8,2,40,1280]{3,2,1,0:T(8,128)(2,1)S(1)}, bf16[8,2,40,1280]{3,2,1,0:T(8,128)(2,1)S(1)}, u32[]{:S(2)}, u32[]{:S(2)}) collective-permute-start(bf16[8,2,40,1280]{3,2,1,0:T(8,128)(2,1)S(1)} %get-tuple-element.27), channel_id=1, source_target_pairs={{0,32},{32,0},{1,33},{33,1},{2,34},{34,2},{3,35},{35,3},{4,36},{36... | collective-permute-start | bytes 4915208 | tf_op jit(solution)/shard_map/ppermute | solution.py:314
  16.3 0.0 copy-done.3
  16.3 0.0 copy-done.5
  16.3 2.6 %shard_map.131 = bf16[32,64,128]{2,1,0:T(8,128)(2,1)} custom-call(bf16[384,1280]{1,0:T(8,128)(2,1)S(1)} %get-tuple-element.17.pre_grad, bf16[384,640]{1,0:T(8,128)(2,1)S(1)} %bitcast.16, bf16[640,1280]{1,0:T(8,128)(2,1)S(1)} %copy-done.5), custom_call_target="tpu_custom_call" | custom-call | flops 2000000000 | bytes 4000000 | tf_op jit(solution)/shard_map/pallas_call | solution.py:316
  18.9 0.9 collective-permute-done.2
  19.8 1.5 %add_convert_fusion = bf16[8,2,40,1280]{3,2,1,0:T(8,128)(2,1)} fusion(bf16[8,2,40,1280]{3,2,1,0:T(8,128)(2,1)S(1)} %collective-permute-done.2, bf16[8,2,40,1280]{3,2,1,0:T(8,128)(2,1)S(1)} %get-tuple-element.26), kind=kLoop, calls=%fused_computation | loop fusion | flops 3276800 | bytes 4915200 | tf_op jit(solution)/shard_map/convert_element_type | solution.py:331
  21.3 0.0 copy-start.7
  21.3 0.0 copy-start.8
  21.3 0.0 copy-start.9
  21.3 0.0 copy-start.10
  21.3 0.0 reduce-scatter.2.cloned.1.call-update
  21.3 10.4 %all-to-all-start = ((bf16[32,64,128]{2,1,0:T(8,128)(2,1)}), bf16[32,64,128]{2,1,0:T(8,128)(2,1)S(1)}, u32[]{:S(2)}, u32[]{:S(2)}) async-start(bf16[32,64,128]{2,1,0:T(8,128)(2,1)} %shard_map.131), calls=%async_computation | async-start | bytes 1048576 | tf_op jit(solution)/shard_map/all_to_all | solution.py:328
  31.8 0.1 pad_add_fusion.place
  31.8 0.0 copy-done.7
  31.8 0.0 copy-done.8
  31.8 0.0 copy-done.9
  31.8 0.0 copy-done.10
  31.9 0.0 copy-start.6
  31.9 1.0 copy-done.6
  32.8 0.0 copy-start.2
  32.8 4.4 %shard_map.132 = (bf16[5,1152,128]{2,1,0:T(8,128)(2,1)}, bf16[2304,640]{1,0:T(8,128)(2,1)S(1)}, f32[9,384,128]{2,1,0:T(8,128)S(1)}, f32[8,128]{1,0:T(8,128)S(1)}) custom-call(s32[2]{0:T(128)S(1)} %pad_add_fusion.place, f32[9,9,512]{2,1,0:T(8,128)S(1)} %bitcast.18, s32[9,512]{1,0:T(8,128)S(1)} %bitcast.19, s32[1,512]{1,0:T(1,128)S(1)} %bitcast.20, ...), custom_call_target="tpu_custom_call" | custom-call | flops 1000000000 | bytes 6000000 | tf_op jit(solution)/shard_map/pallas_call | solution.py:334
  37.2 0.0 copy-start
  37.2 1.6 %copy-done = bf16[2304,640]{1,0:T(8,128)(2,1)} copy-done((bf16[2304,640]{1,0:T(8,128)(2,1)}, bf16[2304,640]{1,0:T(8,128)(2,1)S(1)}, u32[]{:S(2)}) %copy-start) | copy-done | bytes 2949144
  38.8 10.1 %all-to-all-done.slabs = bf16[32,64,128]{2,1,0:T(8,128)(2,1)S(1)} async-done(((bf16[32,64,128]{2,1,0:T(8,128)(2,1)}), bf16[32,64,128]{2,1,0:T(8,128)(2,1)S(1)}, u32[]{:S(2)}, u32[]{:S(2)}) %all-to-all-start) | async-done | bytes 524320 | tf_op jit(solution)/shard_map/all_to_all | solution.py:328
  48.9 0.6 shard_map.133
  49.5 1.3 %collective-permute-start = (bf16[384,128]{1,0:T(8,128)(2,1)S(1)}, bf16[384,128]{1,0:T(8,128)(2,1)S(1)}, u32[]{:S(2)}, u32[]{:S(2)}) collective-permute-start(bf16[384,128]{1,0:T(8,128)(2,1)S(1)} %get-tuple-element.22), channel_id=1, source_target_pairs={{0,32},{32,64},{64,96},{96,128},{128,160},{160,192},{192,224},{224... | collective-permute-start | bytes 294920 | tf_op jit(solution)/shard_map/ppermute | solution.py:359
  50.8 1.5 %collective-permute-start.1 = (bf16[384,128]{1,0:T(8,128)(2,1)S(1)}, bf16[384,128]{1,0:T(8,128)(2,1)S(1)}, u32[]{:S(2)}, u32[]{:S(2)}) collective-permute-start(bf16[384,128]{1,0:T(8,128)(2,1)S(1)} %get-tuple-element.23), channel_id=1, source_target_pairs={{32,0},{64,32},{96,64},{128,96},{160,128},{192,160},{224,192},{256... | collective-permute-start | bytes 294920 | tf_op jit(solution)/shard_map/ppermute | solution.py:360
  52.2 0.0 copy-done.2
  52.3 0.0 copy-start.1
  52.3 0.0 copy-start.4
  52.3 4.6 %shard_map.134.filtered = f32[384,640]{1,0:T(8,128)S(1)} custom-call(bf16[384,640]{1,0:T(8,128)(2,1)S(1)} %get-tuple-element.19.moved, bf16[384,384]{1,0:T(8,128)(2,1)S(1)} %copy-done.2, f32[9,384,128]{2,1,0:T(8,128)S(1)} %get-tuple-element.20.spread, bf16[5,1152,128]{2,1,0:T(8,128)(2,1)} %get-tuple-element.21.own_mix), custom_call_target="tpu_custom_call" | custom-call | flops 800000000 | bytes 5000000 | tf_op jit(solution)/shard_map/pallas_call | solution.py:362
  56.9 0.0 collective-permute-done.before
  56.9 0.0 collective-permute-done.1.after
  57.0 0.0 copy-done.1
  57.0 0.0 copy-done.4
  57.0 2.5 %shard_map.135.answer = bf16[32,96,128]{2,1,0:T(8,128)(2,1)S(1)} custom-call(f32[384,640]{1,0:T(8,128)S(1)} %shard_map.134.filtered, bf16[384,128]{1,0:T(8,128)(2,1)S(1)} %collective-permute-done.before, bf16[384,128]{1,0:T(8,128)(2,1)S(1)} %collective-permute-done.1.after, bf16[384,384]{1,0:T(8,128)(2,1)S(1)} %copy-done.2, bf16[384,384]{1,0:T(8,128)(2,1)S(1)} %copy-done.4, ...), custom_call_target="tpu_custom_call" | custom-call | flops 1500000000 | bytes 7000000 | tf_op jit(solution)/shard_map/pallas_call | solution.py:376
  59.4 10.8 %reduce-scatter.2.cloned.1.call-done.column = bf16[1,2,40,1280]{3,2,1,0:T(8,128)(2,1)} async-done(((bf16[8,2,40,1280]{3,2,1,0:T(8,128)(2,1)}), bf16[1,2,40,1280]{3,2,1,0:T(8,128)(2,1)}) %reduce-scatter.2.cloned.1.call-update) | async-done | bytes 204816 | tf_op jit(solution)/shard_map/reduce_scatter | solution.py:332
  70.3 1.2 %shard_map.136 = bf16[32,96,128]{2,1,0:T(8,128)(2,1)S(1)} custom-call(bf16[32,96,128]{2,1,0:T(8,128)(2,1)S(1)} %shard_map.135.answer, bf16[1,2,40,1280]{3,2,1,0:T(8,128)(2,1)} %reduce-scatter.2.cloned.1.call-done.column), custom_call_target="tpu_custom_call", output_to_operand_aliasing={{}: (0, {})} | custom-call | flops 1000000 | bytes 2000000 | tf_op jit(solution)/shard_map/pallas_call | solution.py:387
  71.5 27.9 %all_to_all.10.slabs = bf16[32,96,128]{2,1,0:T(8,128)(2,1)S(1)} all-to-all(bf16[32,96,128]{2,1,0:T(8,128)(2,1)S(1)} %shard_map.136), channel_id=1, replica_groups=mesh['z'=8,'core'=2,'y'=8,'x'=4] {'y','x'}, dimensions={0} | all-to-all | bytes 1572864 | tf_op jit(solution)/shard_map/all_to_all | solution.py:397
  99.4 1.5 %shard_map.137 = (bf16[384,640]{1,0:T(8,128)(2,1)}, f32[40,40]{1,0:T(8,128)}, f32[40,40]{1,0:T(8,128)}) custom-call(bf16[32,96,128]{2,1,0:T(8,128)(2,1)S(1)} %all_to_all.10.slabs, bf16[384,640]{1,0:T(8,128)(2,1)S(1)} %bitcast.17), custom_call_target="tpu_custom_call" | custom-call | flops 100000000 | bytes 2000000 | tf_op jit(solution)/shard_map/pallas_call | solution.py:398
Async XLA Ops:
  7.2 63.1 %reduce-scatter.2.cloned.1.call-start = ((), (), s32[]{:S(2)}) async-start(), calls=%async_computation.3 | async-start | bytes 1843200 | tf_op jit(solution)/shard_map/reduce_scatter | solution.py:332
  7.2 9.1 %copy-start.3 = (bf16[32,12,640]{2,0,1:T(8,128)(2,1)S(1)}, bf16[32,12,640]{2,0,1:T(8,128)(2,1)}, u32[]{:S(2)}) copy-start(bf16[32,12,640]{2,0,1:T(8,128)(2,1)} %param.12) | copy-start | bytes 1474564
  7.2 9.1 %copy-start.5 = (bf16[640,1280]{1,0:T(8,128)(2,1)S(1)}, bf16[640,1280]{1,0:T(8,128)(2,1)}, u32[]{:S(2)}) copy-start(bf16[640,1280]{1,0:T(8,128)(2,1)} %w_in.3) | copy-start | bytes 4915204
  14.4 5.4 %collective-permute-start.2 = (bf16[8,2,40,1280]{3,2,1,0:T(8,128)(2,1)S(1)}, bf16[8,2,40,1280]{3,2,1,0:T(8,128)(2,1)S(1)}, u32[]{:S(2)}, u32[]{:S(2)}) collective-permute-start(bf16[8,2,40,1280]{3,2,1,0:T(8,128)(2,1)S(1)} %get-tuple-element.27), channel_id=1, source_target_pairs={{0,32},{32,0},{1,33},{33,1},{2,34},{34,2},{3,35},{35,3},{4,36},{36... | collective-permute-start | bytes 4915208 | tf_op jit(solution)/shard_map/ppermute | solution.py:314
  21.3 10.5 %copy-start.7 = (f32[9,640]{1,0:T(8,128)S(1)}, f32[9,640]{1,0:T(8,128)}, u32[]{:S(2)}) copy-start(f32[9,640]{1,0:T(8,128)} %chan.1) | copy-start | bytes 69124
  21.3 10.5 %copy-start.8 = (s32[512,9]{0,1:T(8,128)S(1)}, s32[512,9]{0,1:T(8,128)}, u32[]{:S(2)}) copy-start(s32[512,9]{0,1:T(8,128)} %param.18) | copy-start | bytes 55300
  21.3 10.5 %copy-start.9 = (f32[9,384]{1,0:T(8,128)S(1)}, f32[9,384]{1,0:T(8,128)}, u32[]{:S(2)}) copy-start(f32[9,384]{1,0:T(8,128)} %basis.1) | copy-start | bytes 41476
  21.3 10.5 %copy-start.10 = (s32[512]{0:T(512)S(1)}, s32[512]{0:T(512)}, u32[]{:S(2)}) copy-start(s32[512]{0:T(512)} %param.19) | copy-start | bytes 6148
  21.3 27.5 %all-to-all-start = ((bf16[32,64,128]{2,1,0:T(8,128)(2,1)}), bf16[32,64,128]{2,1,0:T(8,128)(2,1)S(1)}, u32[]{:S(2)}, u32[]{:S(2)}) async-start(bf16[32,64,128]{2,1,0:T(8,128)(2,1)} %shard_map.131), calls=%async_computation | async-start | bytes 1048576 | tf_op jit(solution)/shard_map/all_to_all | solution.py:328
  31.9 1.0 copy-start.6
  32.8 19.4 %copy-start.2 = (bf16[384,384]{1,0:T(8,128)(2,1)S(1)}, bf16[384,384]{1,0:T(8,128)(2,1)}, u32[]{:S(2)}) copy-start(bf16[384,384]{1,0:T(8,128)(2,1)} %constant.29.clone.forward) | copy-start | bytes 884740
  37.2 1.6 %copy-start = (bf16[2304,640]{1,0:T(8,128)(2,1)}, bf16[2304,640]{1,0:T(8,128)(2,1)S(1)}, u32[]{:S(2)}) copy-start(bf16[2304,640]{1,0:T(8,128)(2,1)S(1)} %get-tuple-element.24.rim_mix) | copy-start | bytes 8847364
  49.5 7.5 %collective-permute-start = (bf16[384,128]{1,0:T(8,128)(2,1)S(1)}, bf16[384,128]{1,0:T(8,128)(2,1)S(1)}, u32[]{:S(2)}, u32[]{:S(2)}) collective-permute-start(bf16[384,128]{1,0:T(8,128)(2,1)S(1)} %get-tuple-element.22), channel_id=1, source_target_pairs={{0,32},{32,64},{64,96},{96,128},{128,160},{160,192},{192,224},{224... | collective-permute-start | bytes 294920 | tf_op jit(solution)/shard_map/ppermute | solution.py:359
  50.8 6.2 %collective-permute-start.1 = (bf16[384,128]{1,0:T(8,128)(2,1)S(1)}, bf16[384,128]{1,0:T(8,128)(2,1)S(1)}, u32[]{:S(2)}, u32[]{:S(2)}) collective-permute-start(bf16[384,128]{1,0:T(8,128)(2,1)S(1)} %get-tuple-element.23), channel_id=1, source_target_pairs={{32,0},{64,32},{96,64},{128,96},{160,128},{192,160},{224,192},{256... | collective-permute-start | bytes 294920 | tf_op jit(solution)/shard_map/ppermute | solution.py:360
  52.3 4.7 %copy-start.1 = (bf16[2304,640]{1,0:T(8,128)(2,1)S(1)}, bf16[2304,640]{1,0:T(8,128)(2,1)}, u32[]{:S(2)}) copy-start(bf16[2304,640]{1,0:T(8,128)(2,1)} %copy-done) | copy-start | bytes 8847364
  52.3 4.7 %copy-start.4 = (bf16[384,384]{1,0:T(8,128)(2,1)S(1)}, bf16[384,384]{1,0:T(8,128)(2,1)}, u32[]{:S(2)}) copy-start(bf16[384,384]{1,0:T(8,128)(2,1)} %constant.30.clone.inverse) | copy-start | bytes 884740
Sparse Core Ops, SparseCore 0:
  21.5 48.7 reduce-scatter.1
